TPU v7x, 32 devices: a whole 2x2x4 slice. The times are simulated.
32 devices in a mesh: dp: 8 (over y, x, core), mp: 4 (over z).
Axes of the slice: x: 2, y: 2, z: 4, core: 2. Of those that a mesh axis runs over, the one named last changes fastest.
Arguments:
- patches: bfloat16 [16928, 768], P(('dp', 'mp')), may hold values from -6 to 6
- lengths: int32 [32], P('dp'), may hold values from 40 to 529, as said below
- encoder_attention_gain: float32 [768], replicated, may hold values from 0.1 to 1.9
- encoder_attention_shift: float32 [768], replicated, may hold values from -2 to 2
- encoder_projections: bfloat16 [3, 768, 768], P(None, None, 'mp'), may hold values from -0.21875 to 0.21875
- encoder_head_bias: float32 [2, 768], P(None, 'mp'), may hold values from -2 to 2
- encoder_output_weight: bfloat16 [768, 768], P('mp'), may hold values from -0.875 to 0.875
- encoder_output_bias: float32 [768], replicated, may hold values from -2 to 2
- encoder_feed_gain: float32 [768], replicated, may hold values from 0.1 to 1.9
- encoder_feed_shift: float32 [768], replicated, may hold values from -2 to 2
- encoder_up_weight: bfloat16 [768, 3072], P(None, 'mp'), may hold values from -0.21875 to 0.21875
- encoder_up_bias: float32 [3072], P('mp'), may hold values from -2 to 2
- encoder_down_weight: bfloat16 [3072, 768], P('mp'), may hold values from -0.109375 to 0.109375
- encoder_down_bias: float32 [768], replicated, may hold values from -2 to 2
- bridge_weight: bfloat16 [768, 512], replicated, may hold values from -0.21875 to 0.21875
- bridge_bias: float32 [512], replicated, may hold values from -2 to 2
- decoder_attention_gain: float32 [512], replicated, may hold values from 0.1 to 1.9
- decoder_attention_shift: float32 [512], replicated, may hold values from -2 to 2
- decoder_projections: bfloat16 [3, 512, 512], P(None, None, 'mp'), may hold values from -0.25 to 0.25
- decoder_head_bias: float32 [2, 512], P(None, 'mp'), may hold values from -2 to 2
- decoder_output_weight: bfloat16 [512, 512], P('mp'), may hold values from -1 to 1
- decoder_output_bias: float32 [512], replicated, may hold values from -2 to 2
- decoder_feed_gain: float32 [512], replicated, may hold values from 0.1 to 1.9
- decoder_feed_shift: float32 [512], replicated, may hold values from -2 to 2
- decoder_up_weight: bfloat16 [512, 2048], P(None, 'mp'), may hold values from -0.25 to 0.25
- decoder_up_bias: float32 [2048], P('mp'), may hold values from -2 to 2
- decoder_down_weight: bfloat16 [2048, 512], P('mp'), may hold values from -0.125 to 0.125
- decoder_down_bias: float32 [512], replicated, may hold values from -2 to 2
- cotangent: bfloat16 [16928, 512], P(('dp', 'mp')), may hold values from -6 to 6
Outputs:
- decoded: bfloat16 [16928, 512], P(('dp', 'mp'))
- patches_gradient: bfloat16 [16928, 768], P(('dp', 'mp'))
- encoder_attention_gain_gradient: float32 [768], P(('dp', 'mp'))
- encoder_attention_shift_gradient: float32 [768], P(('dp', 'mp'))
- encoder_projections_gradient: float32 [3, 768, 768], P(None, 'dp', 'mp')
- encoder_head_bias_gradient: float32 [2, 768], P(None, ('mp', 'dp'))
- encoder_output_weight_gradient: float32 [768, 768], P('mp', 'dp')
- encoder_output_bias_gradient: float32 [768], P(('dp', 'mp'))
- encoder_feed_gain_gradient: float32 [768], P(('dp', 'mp'))
- encoder_feed_shift_gradient: float32 [768], P(('dp', 'mp'))
- encoder_up_weight_gradient: float32 [768, 3072], P('dp', 'mp')
- encoder_up_bias_gradient: float32 [3072], P(('mp', 'dp'))
- encoder_down_weight_gradient: float32 [3072, 768], P('mp', 'dp')
- encoder_down_bias_gradient: float32 [768], P(('dp', 'mp'))
- bridge_weight_gradient: float32 [768, 512], P(('dp', 'mp'))
- bridge_bias_gradient: float32 [512], P(('dp', 'mp'))
- decoder_attention_gain_gradient: float32 [512], P(('dp', 'mp'))
- decoder_attention_shift_gradient: float32 [512], P(('dp', 'mp'))
- decoder_projections_gradient: float32 [3, 512, 512], P(None, 'dp', 'mp')
- decoder_head_bias_gradient: float32 [2, 512], P(None, ('mp', 'dp'))
- decoder_output_weight_gradient: float32 [512, 512], P('mp', 'dp')
- decoder_output_bias_gradient: float32 [512], P(('dp', 'mp'))
- decoder_feed_gain_gradient: float32 [512], P(('dp', 'mp'))
- decoder_feed_shift_gradient: float32 [512], P(('dp', 'mp'))
- decoder_up_weight_gradient: float32 [512, 2048], P('dp', 'mp')
- decoder_up_bias_gradient: float32 [2048], P(('mp', 'dp'))
- decoder_down_weight_gradient: float32 [2048, 512], P('mp', 'dp')
- decoder_down_bias_gradient: float32 [512], P(('dp', 'mp'))
Inputs may be any that keep to these rules, and one draw needn't show every extreme that they name: `lengths`: slots at or past a strip's length are blanks that no query attends to; some strip has length 529 and some has 40.
All inputs are finite; a program needn't handle non-finite values.
Results may differ from a plain program's by a relative error of at most 0.035.
Values may be sent and summed in bfloat16 or wider, within the bound.
A program may use at most 192 MiB of HBM per device.

v0:
```python
from functools import partial

import jax
import jax.numpy as jnp
from jax import lax
from jax.sharding import PartitionSpec as P

HEAD = 64
DHEAD = 32


EPSILON = 1e-06


def normalize(stream, gain_vector, shift_vector):
    centered = stream - jnp.mean(stream, -1, keepdims=True)
    variance = jnp.mean(centered * centered, -1, keepdims=True)
    return centered * lax.rsqrt(variance + EPSILON) * gain_vector + shift_vector


def layer_back(stream, gain_vector, shift_vector, upstream):
    unused, pullback = jax.vjp(normalize, stream, gain_vector, shift_vector)
    return pullback(upstream)


def gelu_exact(inputs):
    return jax.nn.gelu(inputs, approximate=False)


def contract_rows(left, right):
    return lax.dot_general(
        left, right, (((0,), (0,)), ((), ())), preferred_element_type=jnp.float32
    )


def contract_cols(left, right):
    return lax.dot_general(
        left, right, (((1,), (1,)), ((), ())), preferred_element_type=jnp.float32
    )


def norm_spread(normed):
    return lax.all_gather(normed, "mp", axis=0, tiled=True)


def branch_collect(partial_out):
    return lax.psum_scatter(
        partial_out.astype(jnp.bfloat16), "mp", scatter_dimension=0, tiled=True
    ).astype(jnp.float32)


def grad_spread(rounded):
    return lax.all_gather(rounded, "mp", axis=0, tiled=True)


def input_collect(partial_in):
    return lax.psum_scatter(
        partial_in.astype(jnp.bfloat16), "mp", scatter_dimension=0, tiled=True
    ).astype(jnp.float32)


def strip_scores(query_block, key_block, length, head_dim):
    positions = query_block.shape[0]
    head_count = query_block.shape[1] // head_dim
    query_heads = query_block.reshape(positions, head_count, head_dim)
    key_heads = key_block.reshape(positions, head_count, head_dim)
    scores = jnp.einsum(
        "qhd,khd->hqk", query_heads, key_heads, preferred_element_type=jnp.float32
    ) * head_dim ** (-0.5)
    visible = lax.iota(jnp.int32, positions) < length
    return jnp.where(visible[None, None, :], scores, -1e30)


def strip_forward(member, head_dim):
    query_block, key_block, value_block, length = member
    positions = query_block.shape[0]
    head_count = query_block.shape[1] // head_dim
    scores = strip_scores(query_block, key_block, length, head_dim)
    ceiling = jnp.max(scores, -1, keepdims=True)
    exponent = jnp.exp(scores - ceiling)
    denominator = jnp.sum(exponent, -1, keepdims=True)
    chances = (exponent / denominator).astype(jnp.bfloat16)
    value_heads = value_block.reshape(positions, head_count, head_dim)
    attended = jnp.einsum("hqk,khd->qhd", chances, value_heads, preferred_element_type=jnp.float32)
    logsum = (ceiling + jnp.log(denominator))[..., 0]
    return (attended.reshape(positions, head_count * head_dim).astype(jnp.bfloat16), logsum)


def strip_backward(member, head_dim):
    query_block, key_block, value_block, length, logsum, mixed_grad = member
    positions = query_block.shape[0]
    head_count = query_block.shape[1] // head_dim
    factor = head_dim ** (-0.5)
    scores = strip_scores(query_block, key_block, length, head_dim)
    chances = jnp.exp(scores - logsum[..., None])
    query_heads = query_block.reshape(positions, head_count, head_dim)
    key_heads = key_block.reshape(positions, head_count, head_dim)
    value_heads = value_block.reshape(positions, head_count, head_dim)
    grad_heads = mixed_grad.reshape(positions, head_count, head_dim)
    value_grad = jnp.einsum(
        "hqk,qhd->khd", chances.astype(jnp.bfloat16), grad_heads, preferred_element_type=jnp.float32
    )
    chance_grad = jnp.einsum(
        "qhd,khd->hqk", grad_heads, value_heads, preferred_element_type=jnp.float32
    )
    score_grad = chances * (chance_grad - jnp.sum(chance_grad * chances, -1, keepdims=True))
    score_grad = score_grad.astype(jnp.bfloat16)
    query_grad = (
        jnp.einsum("hqk,khd->qhd", score_grad, key_heads, preferred_element_type=jnp.float32)
        * factor
    )
    key_grad = (
        jnp.einsum("hqk,qhd->khd", score_grad, query_heads, preferred_element_type=jnp.float32)
        * factor
    )
    full_width = head_count * head_dim
    return (
        query_grad.reshape(positions, full_width),
        key_grad.reshape(positions, full_width),
        value_grad.reshape(positions, full_width),
    )


def block_forward(stream, params, lengths, head_dim):
    (
        attention_gain,
        attention_shift,
        projections,
        head_bias,
        output_weight,
        output_bias,
        feed_gain,
        feed_shift,
        up_weight,
        up_bias,
        down_weight,
        down_bias,
    ) = params
    strips = lengths.shape[0]
    local_width = projections.shape[2]
    attn_input = norm_spread(
        normalize(stream, attention_gain, attention_shift).astype(jnp.bfloat16)
    )
    triple = jnp.einsum("td,jde->jte", attn_input, projections, preferred_element_type=jnp.float32)
    queries = (triple[0] + head_bias[0]).astype(jnp.bfloat16)
    key_rows = triple[1].astype(jnp.bfloat16)
    values = (triple[2] + head_bias[1]).astype(jnp.bfloat16)
    attended, logsum = lax.map(
        partial(strip_forward, head_dim=head_dim),
        (
            queries.reshape(strips, -1, local_width),
            key_rows.reshape(strips, -1, local_width),
            values.reshape(strips, -1, local_width),
            lengths,
        ),
    )
    attended = attended.reshape(-1, local_width)
    middle = stream + (
        branch_collect(jnp.dot(attended, output_weight, preferred_element_type=jnp.float32))
        + output_bias
    )
    feed_input = norm_spread(normalize(middle, feed_gain, feed_shift).astype(jnp.bfloat16))
    before = jnp.dot(feed_input, up_weight, preferred_element_type=jnp.float32) + up_bias
    hidden = gelu_exact(before).astype(jnp.bfloat16)
    result = middle + (
        branch_collect(jnp.dot(hidden, down_weight, preferred_element_type=jnp.float32)) + down_bias
    )
    stored = (
        stream,
        attn_input,
        queries,
        key_rows,
        values,
        logsum,
        attended,
        middle,
        feed_input,
        before,
        hidden,
    )
    return (result, stored)


def block_backward(upstream, params, stored, lengths, head_dim):
    (
        attention_gain,
        attention_shift,
        projections,
        head_bias,
        output_weight,
        output_bias,
        feed_gain,
        feed_shift,
        up_weight,
        up_bias,
        down_weight,
        down_bias,
    ) = params
    (
        stream,
        attn_input,
        queries,
        key_rows,
        values,
        logsum,
        attended,
        middle,
        feed_input,
        before,
        hidden,
    ) = stored
    strips = lengths.shape[0]
    local_width = projections.shape[2]
    branch_rows = upstream.astype(jnp.bfloat16)
    down_bias_grad = jnp.sum(branch_rows.astype(jnp.float32), 0)
    branch_grad = grad_spread(branch_rows)
    down_grad = contract_rows(hidden, branch_grad)
    hidden_grad = contract_cols(branch_grad, down_weight)
    unused, gelu_pull = jax.vjp(gelu_exact, before)
    before_grad = gelu_pull(hidden_grad)[0].astype(jnp.bfloat16)
    up_bias_grad = jnp.sum(before_grad.astype(jnp.float32), 0)
    up_grad = contract_rows(feed_input, before_grad)
    feed_rows = input_collect(contract_cols(before_grad, up_weight))
    middle_part, feed_gain_grad, feed_shift_grad = layer_back(
        middle, feed_gain, feed_shift, feed_rows
    )
    middle_grad = upstream + middle_part
    attn_rows = middle_grad.astype(jnp.bfloat16)
    output_bias_grad = jnp.sum(attn_rows.astype(jnp.float32), 0)
    attn_grad = grad_spread(attn_rows)
    output_grad = contract_rows(attended, attn_grad)
    mixed_grad = contract_cols(attn_grad, output_weight).astype(jnp.bfloat16)
    query_grad, key_grad, value_grad = lax.map(
        partial(strip_backward, head_dim=head_dim),
        (
            queries.reshape(strips, -1, local_width),
            key_rows.reshape(strips, -1, local_width),
            values.reshape(strips, -1, local_width),
            lengths,
            logsum,
            mixed_grad.reshape(strips, -1, local_width),
        ),
    )
    triple_grad = jnp.stack(
        [
            query_grad.reshape(-1, local_width),
            key_grad.reshape(-1, local_width),
            value_grad.reshape(-1, local_width),
        ]
    ).astype(jnp.bfloat16)
    triple_sums = jnp.sum(triple_grad.astype(jnp.float32), 1)
    head_bias_grad = jnp.stack([triple_sums[0], triple_sums[2]])
    projections_grad = jnp.einsum(
        "td,jte->jde", attn_input, triple_grad, preferred_element_type=jnp.float32
    )
    input_rows = input_collect(
        jnp.einsum("jte,jde->td", triple_grad, projections, preferred_element_type=jnp.float32)
    )
    stream_part, attention_gain_grad, attention_shift_grad = layer_back(
        stream, attention_gain, attention_shift, input_rows
    )
    gradients = (
        attention_gain_grad,
        attention_shift_grad,
        projections_grad,
        head_bias_grad,
        output_grad,
        output_bias_grad,
        feed_gain_grad,
        feed_shift_grad,
        up_grad,
        up_bias_grad,
        down_grad,
        down_bias_grad,
    )
    return (middle_grad + stream_part, gradients)


def shards(
    patches,
    lengths,
    encoder_attention_gain,
    encoder_attention_shift,
    encoder_projections,
    encoder_head_bias,
    encoder_output_weight,
    encoder_output_bias,
    encoder_feed_gain,
    encoder_feed_shift,
    encoder_up_weight,
    encoder_up_bias,
    encoder_down_weight,
    encoder_down_bias,
    bridge_weight,
    bridge_bias,
    decoder_attention_gain,
    decoder_attention_shift,
    decoder_projections,
    decoder_head_bias,
    decoder_output_weight,
    decoder_output_bias,
    decoder_feed_gain,
    decoder_feed_shift,
    decoder_up_weight,
    decoder_up_bias,
    decoder_down_weight,
    decoder_down_bias,
    cotangent,
):
    stream = patches.astype(jnp.float32)
    encoder = (
        encoder_attention_gain,
        encoder_attention_shift,
        encoder_projections,
        encoder_head_bias,
        encoder_output_weight,
        encoder_output_bias,
        encoder_feed_gain,
        encoder_feed_shift,
        encoder_up_weight,
        encoder_up_bias,
        encoder_down_weight,
        encoder_down_bias,
    )
    decoder = (
        decoder_attention_gain,
        decoder_attention_shift,
        decoder_projections,
        decoder_head_bias,
        decoder_output_weight,
        decoder_output_bias,
        decoder_feed_gain,
        decoder_feed_shift,
        decoder_up_weight,
        decoder_up_bias,
        decoder_down_weight,
        decoder_down_bias,
    )
    encoded = block_forward(stream, encoder, lengths, HEAD)[0]
    bridge_input = encoded.astype(jnp.bfloat16)
    bridged = jnp.dot(bridge_input, bridge_weight, preferred_element_type=jnp.float32) + bridge_bias
    decoded, dec_stored = block_forward(bridged, decoder, lengths, DHEAD)
    bridged_grad, dec_grads = block_backward(
        cotangent.astype(jnp.float32), decoder, dec_stored, lengths, DHEAD
    )
    bridge_rows = bridged_grad.astype(jnp.bfloat16)
    bridge_weight_grad = contract_rows(bridge_input, bridge_rows)
    bridge_bias_grad = jnp.sum(bridge_rows.astype(jnp.float32), 0)
    encoded_grad = contract_cols(bridge_rows, bridge_weight)
    enc_stored = block_forward(stream, encoder, lengths, HEAD)[1]
    patches_grad, enc_grads = block_backward(encoded_grad, encoder, enc_stored, lengths, HEAD)
    all_sharded = (
        lax.psum_scatter(enc_grads[2], "dp", scatter_dimension=1, tiled=True),
        lax.psum_scatter(enc_grads[3], "dp", scatter_dimension=1, tiled=True),
        lax.psum_scatter(enc_grads[4], "dp", scatter_dimension=1, tiled=True),
        lax.psum_scatter(enc_grads[8], "dp", scatter_dimension=0, tiled=True),
        lax.psum_scatter(enc_grads[9], "dp", scatter_dimension=0, tiled=True),
        lax.psum_scatter(enc_grads[10], "dp", scatter_dimension=1, tiled=True),
        lax.psum_scatter(dec_grads[2], "dp", scatter_dimension=1, tiled=True),
        lax.psum_scatter(dec_grads[3], "dp", scatter_dimension=1, tiled=True),
        lax.psum_scatter(dec_grads[4], "dp", scatter_dimension=1, tiled=True),
        lax.psum_scatter(dec_grads[8], "dp", scatter_dimension=0, tiled=True),
        lax.psum_scatter(dec_grads[9], "dp", scatter_dimension=0, tiled=True),
        lax.psum_scatter(dec_grads[10], "dp", scatter_dimension=1, tiled=True),
    )
    all_shared = (
        lax.psum_scatter(enc_grads[0], ("dp", "mp"), scatter_dimension=0, tiled=True),
        lax.psum_scatter(enc_grads[1], ("dp", "mp"), scatter_dimension=0, tiled=True),
        lax.psum_scatter(enc_grads[5], ("dp", "mp"), scatter_dimension=0, tiled=True),
        lax.psum_scatter(enc_grads[6], ("dp", "mp"), scatter_dimension=0, tiled=True),
        lax.psum_scatter(enc_grads[7], ("dp", "mp"), scatter_dimension=0, tiled=True),
        lax.psum_scatter(enc_grads[11], ("dp", "mp"), scatter_dimension=0, tiled=True),
        lax.psum_scatter(dec_grads[0], ("dp", "mp"), scatter_dimension=0, tiled=True),
        lax.psum_scatter(dec_grads[1], ("dp", "mp"), scatter_dimension=0, tiled=True),
        lax.psum_scatter(dec_grads[5], ("dp", "mp"), scatter_dimension=0, tiled=True),
        lax.psum_scatter(dec_grads[6], ("dp", "mp"), scatter_dimension=0, tiled=True),
        lax.psum_scatter(dec_grads[7], ("dp", "mp"), scatter_dimension=0, tiled=True),
        lax.psum_scatter(dec_grads[11], ("dp", "mp"), scatter_dimension=0, tiled=True),
        lax.psum_scatter(bridge_weight_grad, ("dp", "mp"), scatter_dimension=0, tiled=True),
        lax.psum_scatter(bridge_bias_grad, ("dp", "mp"), scatter_dimension=0, tiled=True),
    )
    enc_sharded = all_sharded[0:6]
    dec_sharded = all_sharded[6:12]
    enc_shared = all_shared[0:6]
    dec_shared = all_shared[6:14]
    enc_out = (
        enc_shared[0],
        enc_shared[1],
        enc_sharded[0],
        enc_sharded[1],
        enc_sharded[2],
        enc_shared[2],
        enc_shared[3],
        enc_shared[4],
        enc_sharded[3],
        enc_sharded[4],
        enc_sharded[5],
        enc_shared[5],
    )
    dec_out = (
        dec_shared[0],
        dec_shared[1],
        dec_sharded[0],
        dec_sharded[1],
        dec_sharded[2],
        dec_shared[2],
        dec_shared[3],
        dec_shared[4],
        dec_sharded[3],
        dec_sharded[4],
        dec_sharded[5],
        dec_shared[5],
    )
    bridge_out = (dec_shared[6], dec_shared[7])
    return (
        decoded.astype(jnp.bfloat16),
        patches_grad.astype(jnp.bfloat16),
        enc_out[0],
        enc_out[1],
        enc_out[2],
        enc_out[3],
        enc_out[4],
        enc_out[5],
        enc_out[6],
        enc_out[7],
        enc_out[8],
        enc_out[9],
        enc_out[10],
        enc_out[11],
        bridge_out[0],
        bridge_out[1],
        dec_out[0],
        dec_out[1],
        dec_out[2],
        dec_out[3],
        dec_out[4],
        dec_out[5],
        dec_out[6],
        dec_out[7],
        dec_out[8],
        dec_out[9],
        dec_out[10],
        dec_out[11],
    )


def solution(mesh):
    return jax.shard_map(
        shards,
        mesh=mesh,
        in_specs=(
            P(("dp", "mp"), None),
            P("dp"),
            P(),
            P(),
            P(None, None, "mp"),
            P(None, "mp"),
            P("mp", None),
            P(),
            P(),
            P(),
            P(None, "mp"),
            P("mp"),
            P("mp", None),
            P(),
            P(),
            P(),
            P(),
            P(),
            P(None, None, "mp"),
            P(None, "mp"),
            P("mp", None),
            P(),
            P(),
            P(),
            P(None, "mp"),
            P("mp"),
            P("mp", None),
            P(),
            P(("dp", "mp"), None),
        ),
        out_specs=(
            P(("dp", "mp"), None),
            P(("dp", "mp"), None),
            P(("dp", "mp")),
            P(("dp", "mp")),
            P(None, "dp", "mp"),
            P(None, ("mp", "dp")),
            P("mp", "dp"),
            P(("dp", "mp")),
            P(("dp", "mp")),
            P(("dp", "mp")),
            P("dp", "mp"),
            P(("mp", "dp")),
            P("mp", "dp"),
            P(("dp", "mp")),
            P(("dp", "mp"), None),
            P(("dp", "mp")),
            P(("dp", "mp")),
            P(("dp", "mp")),
            P(None, "dp", "mp"),
            P(None, ("mp", "dp")),
            P("mp", "dp"),
            P(("dp", "mp")),
            P(("dp", "mp")),
            P(("dp", "mp")),
            P("dp", "mp"),
            P(("mp", "dp")),
            P("mp", "dp"),
            P(("dp", "mp")),
        ),
        check_vma=False,
    )
```

profile of v0, /device:TPU:28, one launch (start us, length us, event | category | flops | bytes accessed | tf_op | source)
XLA Modules:
  0.0 1723.3 jit_solution(17137778862966622798)
XLA Ops:
  14.0 64.5 %all-gather.19.cloned.1.call-done = bf16[4,529,768]{2,1,0:T(8,128)(2,1)} async-done(((bf16[1,529,768]{2,1,0:T(8,128)(2,1)}), bf16[4,529,768]{2,1,0:T(8,128)(2,1)}) %all-gather.19.cloned.1.call-update) | async-done | bytes 3250192 | tf_op jit(solution)/shard_map/all_gather | solution.py:43
  102.0 27.0 %while.65 = (s32[]{:T(128)}, bf16[4,529,192]{1,2,0:T(8,128)(2,1)}, f32[4,3,529]{2,1,0:T(4,128)}, bf16[4,529,192]{1,2,0:T(8,128)(2,1)S(1)}, s32[4]{0:T(128)S(1)},...) while((s32[]{:T(128)}, bf16[4,529,192]{1,2,0:T(8,128)(2,1)}, ...), condition=%wide.region_32.33_spmd, body=%wide.region_29.32_spmd.sunk | while | flops 225092656 | bytes 12611449 | solution.py:148
  130.0 43.8 %while.62 = (s32[]{:T(128)}, bf16[4,529,192]{1,2,0:T(8,128)(2,1)}, bf16[4,529,192]{1,2,0:T(8,128)(2,1)S(1)}, s32[4]{0:T(128)S(1)}, bf16[4,529,192]{1,2,0:T(8,128...) while((s32[]{:T(128)}, bf16[4,529,192]{1,2,0:T(8,128)(2,1)}, bf16[4,529,192]{1,2,0:T(8,128)(2,1)S(1)}, ...), condition=%wide.region_5.6_spmd, body=%wide.region_2.5_spmd.sunk | while | flops 220057632 | bytes 9210307 | solution.py:148
  133.1 4.5 fusion.295
  144.1 4.5 fusion.295
  166.0 4.5 fusion.295
  192.9 114.0 %fusion.143 = (bf16[536,768]{1,0:T(8,128)(2,1)S(1)}, bf16[536,768]{1,0:T(8,128)(2,1)}) fusion(bf16[2116,768]{1,0:T(8,128)(2,1)} %convolution_convert_fusion.1, bf16[2116,768]{1,0:T(8,128)(2,1)} %convolution_convert_fusion.3), kind=kCustom, calls=%all-reduce-scatter.10 | all-reduce-scatter fusion | flops 3293185 | bytes 8147456
  314.0 6.0 concatenate
  332.7 64.6 %all-gather.21.cloned.1.call-done = bf16[4,529,768]{2,1,0:T(8,128)(2,1)} async-done(((bf16[1,529,768]{2,1,0:T(8,128)(2,1)}), bf16[4,529,768]{2,1,0:T(8,128)(2,1)}) %all-gather.21.cloned.1.call-update) | async-done | bytes 3250192 | tf_op jit(solution)/shard_map/all_gather | solution.py:43
  397.3 4.5 reshape.463
  401.8 21.7 %convolution_convert_fusion.2 = bf16[2116,768]{1,0:T(8,128)(2,1)} fusion(bf16[768,768]{1,0:T(8,128)(2,1)S(1)} %copy-done, bf16[2116,768]{1,0:T(8,128)(2,1)} %reshape.463, bf16[768,768]{1,0:T(8,128)(2,1)} %param.49, f32[768]{0:T(1024)S(1)} %copy-done.89), kind=kOutput, calls=%fused_computation.128 | convolution fusion | flops 5101151232 | bytes 8862720 | tf_op jit(solution)/shard_map/dot_general | solution.py:166
  423.5 60.8 %fusion.1 = bf16[536,768]{1,0:T(8,128)(2,1)} fusion(bf16[2116,768]{1,0:T(8,128)(2,1)} %convolution_convert_fusion.2), kind=kCustom, calls=%all-reduce-scatter.1 | all-reduce-scatter fusion | flops 1646593 | bytes 4073984
  486.4 4.6 collective-permute-done.1
  490.9 6.0 concatenate.1
  503.9 46.2 %all-gather.23.cloned.1.call-done = bf16[4,529,512]{2,1,0:T(8,128)(2,1)} async-done(((bf16[1,529,512]{2,1,0:T(8,128)(2,1)}), bf16[4,529,512]{2,1,0:T(8,128)(2,1)}) %all-gather.23.cloned.1.call-update) | async-done | bytes 2166800 | tf_op jit(solution)/shard_map/all_gather | solution.py:43
  571.5 32.6 %while.63 = (s32[]{:T(128)}, bf16[4,529,128]{2,1,0:T(8,128)(2,1)}, f32[4,4,529]{2,1,0:T(4,128)S(1)}, bf16[4,529,128]{1,2,0:T(8,128)(2,1)}, s32[4]{0:T(128)S(1)},...) while((s32[]{:T(128)}, bf16[4,529,128]{2,1,0:T(8,128)(2,1)}, ...), condition=%wide.region_15.16_spmd, body=%wide.region_12.15_spmd.sunk | while | flops 156777072 | bytes 15405377 | solution.py:148
  609.7 42.7 %fusion.2 = bf16[536,512]{1,0:T(8,128)(2,1)} fusion(bf16[2116,512]{1,0:T(8,128)(2,1)} %convolution_convert_fusion.6), kind=kCustom, calls=%all-reduce-scatter.2 | all-reduce-scatter fusion | flops 1097729 | bytes 2716160
  671.3 43.0 %all-gather.25.cloned.1.call-done = bf16[4,529,512]{2,1,0:T(8,128)(2,1)} async-done(((bf16[1,529,512]{2,1,0:T(8,128)(2,1)}), bf16[4,529,512]{2,1,0:T(8,128)(2,1)}) %all-gather.25.cloned.1.call-update) | async-done | bytes 2166800 | tf_op jit(solution)/shard_map/all_gather | solution.py:43
  721.1 12.9 convert_reduce_fusion.2
  738.0 42.7 %fusion.4 = bf16[536,512]{1,0:T(8,128)(2,1)} fusion(bf16[2116,512]{1,0:T(8,128)(2,1)} %convolution_convert_fusion.4), kind=kCustom, calls=%all-reduce-scatter.4 | all-reduce-scatter fusion | flops 1097729 | bytes 2716160
  782.8 4.5 collective-permute-done.4
  787.3 5.1 concatenate.4
  800.6 46.0 %all-gather.29.cloned.1.call-done = bf16[4,529,512]{2,1,0:T(8,128)(2,1)} async-done(((bf16[1,529,512]{2,1,0:T(8,128)(2,1)}), bf16[4,529,512]{2,1,0:T(8,128)(2,1)}) %all-gather.29.cloned.1.call-update) | async-done | bytes 2166800 | tf_op jit(solution)/shard_map/all_gather | solution.py:53
  852.7 53.6 %while.64 = (s32[]{:T(128)}, bf16[4,529,128]{1,2,0:T(8,128)(2,1)}, bf16[4,529,128]{1,2,0:T(8,128)(2,1)}, bf16[4,529,128]{1,2,0:T(8,128)(2,1)}, bf16[4,529,128]{1...) while((s32[]{:T(128)}, bf16[4,529,128]{1,2,0:T(8,128)(2,1)}, ...), condition=%wide.region_25.26_spmd, body=%wide.region_23.25_spmd.sunk | while | flops 375256192 | bytes 37248716 | solution.py:233
  919.8 42.9 %fusion.5 = bf16[536,512]{1,0:T(8,128)(2,1)} fusion(bf16[2116,512]{1,0:T(8,128)(2,1)} %fusion.60), kind=kCustom, calls=%all-reduce-scatter.5 | all-reduce-scatter fusion | flops 1097729 | bytes 2716160
  982.5 4.6 reshape.473
  987.2 7.3 fusion.160
  994.5 52.8 %all-gather.33.cloned.1.call-done = bf16[4,529,768]{2,1,0:T(8,128)(2,1)} async-done(((bf16[1,529,768]{2,1,0:T(8,128)(2,1)}), bf16[4,529,768]{2,1,0:T(8,128)(2,1)}) %all-gather.33.cloned.1.call-update) | async-done | bytes 3250192 | tf_op jit(solution)/shard_map/all_gather | solution.py:53
  1047.3 4.5 reshape.475
  1051.8 19.8 %convert_reduce_fusion = (f32[768]{0:T(1024)S(1)}, bf16[2116,768]{1,0:T(8,128)(2,1)S(1)}, f32[2116,768]{1,0:T(8,128)}) fusion(f32[2116,768]{1,0:T(8,128)} %fusion.160, f32[768]{0:T(1024)S(1)} %copy-done.90, bf16[2116,768]{1,0:T(8,128)(2,1)} %reshape.475, bf16[768,768]{1,0:T(8,128)(2,1)S(1)} %copy-done), kind=kOutput, calls=%fused_computation.95 | convolution fusion | flops 2618016000 | bytes 20686848 | tf_op jit(solution)/shard_map/dot_general | solution.py:37
  1077.4 61.2 %fusion.7 = bf16[536,768]{1,0:T(8,128)(2,1)} fusion(bf16[2116,768]{1,0:T(8,128)(2,1)} %convolution_convert_fusion), kind=kCustom, calls=%all-reduce-scatter.7 | all-reduce-scatter fusion | flops 1646593 | bytes 4073984
  1140.7 4.6 collective-permute-done.7
  1145.3 6.0 concatenate.7
  1171.8 53.0 %all-gather.35.cloned.1.call-done = bf16[4,529,768]{2,1,0:T(8,128)(2,1)} async-done(((bf16[1,529,768]{2,1,0:T(8,128)(2,1)}), bf16[4,529,768]{2,1,0:T(8,128)(2,1)}) %all-gather.35.cloned.1.call-update) | async-done | bytes 3250192 | tf_op jit(solution)/shard_map/all_gather | solution.py:53
  1235.8 50.8 %while.66 = (s32[]{:T(128)}, bf16[4,529,192]{1,2,0:T(8,128)(2,1)}, bf16[4,529,192]{1,2,0:T(8,128)(2,1)}, bf16[4,529,192]{1,2,0:T(8,128)(2,1)}, bf16[4,529,192]{1...) while((s32[]{:T(128)}, bf16[4,529,192]{1,2,0:T(8,128)(2,1)}, ...), condition=%wide.region_41.42_spmd, body=%wide.region_39.41_spmd.sunk | while | flops 550292736 | bytes 30235540 | solution.py:233
  1312.4 5.2 convolution_bitcast_fusion.2
  1321.8 4.7 reshape.486
  1326.6 4.8 multiply_convert_fusion.3
  1335.2 4.8 fusion.164
  1346.8 10.2 fusion.67
  1367.0 7.5 fusion.161
  1374.5 6.3 bitcast_convert_fusion
  1380.7 95.5 %fusion.142 = (bf16[536,512]{1,0:T(8,128)(2,1)}, bf16[536,768]{1,0:T(8,128)(2,1)}) fusion(bf16[2116,512]{1,0:T(8,128)(2,1)} %convolution_convert_fusion.5, bf16[2116,768]{1,0:T(8,128)(2,1)} %bitcast_convert_fusion), kind=kCustom, calls=%all-reduce-scatter.9 | all-reduce-scatter fusion | flops 2744321 | bytes 6789632
  1482.6 12.3 all-reduce.36
  1509.3 44.0 %all-reduce.35 = (f32[768]{0:T(1024)S(1)}, f32[768]{0:T(1024)S(1)}, f32[768]{0:T(1024)S(1)}, f32[768]{0:T(1024)S(1)}, f32[768]{0:T(1024)S(1)}, /*index=5*/f32[76...) all-reduce(f32[768]{0:T(1024)S(1)} %get-tuple-element.461, ...), channel_id=11, replica_groups=mesh['dp'=8,'mp'=4] {'dp','mp'}, use_global_device_ids=true, to_apply=%region_46.47.clone | all-reduce | flops 8192 | bytes 65536
  1567.5 55.7 %reduce-scatter.39.cloned.1.call-done = f32[24,512]{1,0:T(8,128)} async-done(((f32[768,512]{1,0:T(8,128)}), f32[24,512]{1,0:T(8,128)}) %reduce-scatter.39.cloned.1.call-update) | async-done | bytes 49168 | tf_op jit(solution)/shard_map/reduce_scatter | solution.py:379
  1623.2 46.6 %reduce-scatter.37.cloned.1.call-done = f32[768,96]{0,1:T(8,128)} async-done(((f32[768,768]{0,1:T(8,128)}), f32[768,96]{0,1:T(8,128)}) %reduce-scatter.37.cloned.1.call-update) | async-done | bytes 294928 | tf_op jit(solution)/shard_map/reduce_scatter | solution.py:358
  1669.8 46.4 %reduce-scatter.35.cloned.1.call-done = f32[96,768]{1,0:T(8,128)} async-done(((f32[768,768]{1,0:T(8,128)}), f32[96,768]{1,0:T(8,128)}) %reduce-scatter.35.cloned.1.call-update) | async-done | bytes 294928 | tf_op jit(solution)/shard_map/reduce_scatter | solution.py:356
  (655 shorter events, 500.0 us)
Async XLA Ops:
  7.2 394.6 %copy-start = (bf16[768,768]{1,0:T(8,128)(2,1)S(1)}, bf16[768,768]{1,0:T(8,128)(2,1)}, u32[]{:S(2)}) copy-start(bf16[768,768]{1,0:T(8,128)(2,1)} %param.51) | copy-start | bytes 3538948
  7.2 71.3 %all-gather.19.cloned.1.call-start = ((), (), s32[]{:S(2)}) async-start(), calls=%async_computation.15 | async-start | bytes 4116480 | tf_op jit(solution)/shard_map/all_gather | solution.py:43
  13.9 383.4 %all-gather.21.cloned.1.call-start = ((), (), s32[]{:S(2)}) async-start(), calls=%async_computation.16 | async-start | bytes 4116480 | tf_op jit(solution)/shard_map/all_gather | solution.py:43
  14.0 69.0 %copy-start.84 = (bf16[3,768,192]{1,2,0:T(8,128)(2,1)S(1)}, bf16[3,768,192]{1,2,0:T(8,128)(2,1)}, u32[]{:S(2)}) copy-start(bf16[3,768,192]{1,2,0:T(8,128)(2,1)} %param.43) | copy-start | bytes 2654212
  192.9 117.6 %copy-start.82 = (u32[32]{0:T(128)S(1)}, u32[32]{0:T(128)}, u32[]{:S(2)}) copy-start(u32[32]{0:T(128)} %constant.237) | copy-start | bytes 388
  307.9 6.1 collective-permute-start
  309.2 10.8 collective-permute-start.6
  332.6 69.2 %copy-start.89 = (f32[768]{0:T(1024)S(1)}, f32[768]{0:T(1024)}, u32[]{:S(2)}) copy-start(f32[768]{0:T(1024)} %param.50) | copy-start | bytes 9220
  332.6 217.4 %all-gather.23.cloned.1.call-start = ((), (), s32[]{:S(2)}) async-start(), calls=%async_computation.17 | async-start | bytes 2744320 | tf_op jit(solution)/shard_map/all_gather | solution.py:43
  423.5 73.4 %copy-start.10 = (bf16[557,768]{1,0:T(8,128)(2,1)S(1)}, bf16[557,768]{1,0:T(8,128)(2,1)}, u32[]{:S(2)}) copy-start(bf16[557,768]{1,0:T(8,128)(2,1)} %concatenate) | copy-start | bytes 2566660
  423.5 73.4 %copy-start.75 = (f32[768]{0:T(1024)S(1)}, f32[768]{0:T(1024)}, u32[]{:S(2)}) copy-start(f32[768]{0:T(1024)} %param.52) | copy-start | bytes 9220
  485.1 5.9 collective-permute-start.1
  503.0 164.8 %all-gather.27.cloned.1.call-start = ((), (), s32[]{:S(2)}) async-start(), calls=%async_computation.19 | async-start | bytes 2744320 | tf_op jit(solution)/shard_map/all_gather | solution.py:53
  503.6 210.7 %all-gather.25.cloned.1.call-start = ((), (), s32[]{:S(2)}) async-start(), calls=%async_computation.18 | async-start | bytes 2744320 | tf_op jit(solution)/shard_map/all_gather | solution.py:43
  606.6 56.6 %copy-start.77 = (f32[512]{0:T(512)S(1)}, f32[512]{0:T(512)}, u32[]{:S(2)}) copy-start(f32[512]{0:T(512)} %param.60) | copy-start | bytes 6148
  653.2 5.7 collective-permute-start.2
  664.6 130.8 %copy-start.3 = (f32[529,512]{1,0:T(8,128)}, f32[529,512]{1,0:T(8,128)S(1)}, u32[]{:S(2)}) copy-start(f32[529,512]{1,0:T(8,128)S(1)} %get-tuple-element.594) | copy-start | bytes 3250180
  667.3 179.4 %all-gather.29.cloned.1.call-start = ((), (), s32[]{:S(2)}) async-start(), calls=%async_computation.20 | async-start | bytes 2744320 | tf_op jit(solution)/shard_map/all_gather | solution.py:53
  781.5 5.8 collective-permute-start.4
  799.7 182.8 %all-gather.31.cloned.1.call-start = ((), (), s32[]{:S(2)}) async-start(), calls=%async_computation.21 | async-start | bytes 4116480 | tf_op jit(solution)/shard_map/all_gather | solution.py:43
  800.4 246.9 %all-gather.33.cloned.1.call-start = ((), (), s32[]{:S(2)}) async-start(), calls=%async_computation.22 | async-start | bytes 4116480 | tf_op jit(solution)/shard_map/all_gather | solution.py:53
  919.8 55.3 %copy-start.57 = (f32[529]{0:T(1024)S(1)}, f32[529]{0:T(1024)}, u32[]{:S(2)}) copy-start(f32[529]{0:T(1024)} %copy-done.56) | copy-start | bytes 6352
  919.8 57.7 %copy-start.17 = (f32[529,512]{1,0:T(8,128)S(1)}, f32[529,512]{1,0:T(8,128)}, u32[]{:S(2)}) copy-start(f32[529,512]{1,0:T(8,128)} %copy-done.16) | copy-start | bytes 3250180
  963.4 5.7 collective-permute-start.5
  982.4 242.4 %all-gather.35.cloned.1.call-start = ((), (), s32[]{:S(2)}) async-start(), calls=%async_computation.23 | async-start | bytes 4116480 | tf_op jit(solution)/shard_map/all_gather | solution.py:53
  994.5 57.3 %copy-start.90 = (f32[768]{0:T(1024)S(1)}, f32[768]{0:T(1024)}, u32[]{:S(2)}) copy-start(f32[768]{0:T(1024)} %param.50) | copy-start | bytes 9220
  1077.4 73.9 %copy-start.2 = (bf16[529,768]{1,0:T(8,128)(2,1)S(1)}, bf16[529,768]{1,0:T(8,128)(2,1)}, u32[]{:S(2)}) copy-start(bf16[529,768]{1,0:T(8,128)(2,1)} %param.39) | copy-start | bytes 2437636
  1077.4 73.9 %copy-start.6 = (bf16[557,768]{1,0:T(8,128)(2,1)S(1)}, bf16[557,768]{1,0:T(8,128)(2,1)}, u32[]{:S(2)}) copy-start(bf16[557,768]{1,0:T(8,128)(2,1)} %copy-done.5) | copy-start | bytes 2566660
  1077.4 73.9 %copy-start.42 = (f32[768]{0:T(1024)S(1)}, f32[768]{0:T(1024)}, u32[]{:S(2)}) copy-start(f32[768]{0:T(1024)} %param.46) | copy-start | bytes 9220
  1077.4 73.9 %copy-start.46 = (f32[529]{0:T(1024)S(1)}, f32[529]{0:T(1024)}, u32[]{:S(2)}) copy-start(f32[529]{0:T(1024)} %copy-done.45) | copy-start | bytes 6352
  1077.4 73.9 %copy-start.53 = (f32[768]{0:T(1024)S(1)}, f32[768]{0:T(1024)}, u32[]{:S(2)}) copy-start(f32[768]{0:T(1024)} %param.47) | copy-start | bytes 9220
  1077.4 76.3 %copy-start.61 = (f32[529]{0:T(1024)S(1)}, f32[529]{0:T(1024)}, u32[]{:S(2)}) copy-start(f32[529]{0:T(1024)} %copy-done.60) | copy-start | bytes 6352
  1077.4 76.3 %copy-start.55 = (f32[529]{0:T(1024)S(1)}, f32[529]{0:T(1024)}, u32[]{:S(2)}) copy-start(f32[529]{0:T(1024)} %copy-done.54) | copy-start | bytes 6352
  1139.4 5.9 collective-permute-start.7
  1159.9 204.2 %reduce-scatter.51.cloned.1.call-start = ((), (), s32[]{:S(2)}) async-start(), calls=%async_computation.26 | async-start | bytes 73728
  1166.9 198.5 %all-reduce.41.cloned.1.call-start = ((), (), s32[]{:S(2)}) async-start(), calls=%async_computation.27 | async-start | bytes 2097152
  1171.8 57.5 %copy-start.35 = (bf16[192,768]{1,0:T(8,128)(2,1)S(1)}, bf16[192,768]{1,0:T(8,128)(2,1)}, u32[]{:S(2)}) copy-start(bf16[192,768]{1,0:T(8,128)(2,1)} %param.45) | copy-start | bytes 884740
  1171.8 392.1 %reduce-scatter.49.cloned.1.call-start = ((), (), s32[]{:S(2)}) async-start(), calls=%async_computation.25 | async-start | bytes 884736
  1307.7 257.9 %reduce-scatter.47.cloned.1.call-start = ((), (), s32[]{:S(2)}) async-start(), calls=%async_computation.24 | async-start | bytes 2211840
  1326.5 240.9 %reduce-scatter.45.cloned.1.call-start = ((), (), s32[]{:S(2)}) async-start(), calls=%async_computation.14 | async-start | bytes 1179648 | tf_op jit(solution)/shard_map/reduce_scatter | solution.py:364
  1335.2 232.3 %reduce-scatter.43.cloned.1.call-start = ((), (), s32[]{:S(2)}) async-start(), calls=%async_computation.13 | async-start | bytes 1179648 | tf_op jit(solution)/shard_map/reduce_scatter | solution.py:362
  1340.0 227.4 %reduce-scatter.41.cloned.1.call-start = ((), (), s32[]{:S(2)}) async-start(), calls=%async_computation.12 | async-start | bytes 294912 | tf_op jit(solution)/shard_map/reduce_scatter | solution.py:361
  1343.5 279.7 %reduce-scatter.39.cloned.1.call-start = ((), (), s32[]{:S(2)}) async-start(), calls=%async_computation.11 | async-start | bytes 1622016 | tf_op jit(solution)/shard_map/reduce_scatter | solution.py:379
  1346.7 323.1 %reduce-scatter.37.cloned.1.call-start = ((), (), s32[]{:S(2)}) async-start(), calls=%async_computation.10 | async-start | bytes 2654208 | tf_op jit(solution)/shard_map/reduce_scatter | solution.py:358
  1357.0 359.3 %reduce-scatter.35.cloned.1.call-start = ((), (), s32[]{:S(2)}) async-start(), calls=%async_computation.9 | async-start | bytes 2654208 | tf_op jit(solution)/shard_map/reduce_scatter | solution.py:356
  1380.7 101.9 %copy-start.80 = (f32[512]{0:T(512)S(1)}, f32[512]{0:T(512)}, u32[]{:S(2)}) copy-start(f32[512]{0:T(512)} %get-tuple-element.579) | copy-start | bytes 6148
  1477.1 19.7 %collective-permute-start.3 = (bf16[21,512]{1,0:T(8,128)(2,1)S(1)}, bf16[21,512]{1,0:T(8,128)(2,1)S(1)}, u32[]{:S(2)}, u32[]{:S(2)}) collective-permute-start(bf16[21,512]{1,0:T(8,128)(2,1)S(1)} %slice.74), channel_id=1, source_target_pairs={{0,1},{1,2},{2,3},{4,5},{5,6},{6,7},{8,9},{9,10},{10,11},{12,13},{... | collective-permute-start | bytes 64520
  1479.2 24.1 %collective-permute-start.8 = (bf16[21,768]{1,0:T(8,128)(2,1)S(1)}, bf16[21,768]{1,0:T(8,128)(2,1)S(1)}, u32[]{:S(2)}, u32[]{:S(2)}) collective-permute-start(bf16[21,768]{1,0:T(8,128)(2,1)S(1)} %slice.79), channel_id=1, source_target_pairs={{0,1},{1,2},{2,3},{4,5},{5,6},{6,7},{8,9},{9,10},{10,11},{12,13},{... | collective-permute-start | bytes 96776
  (77 other events, 801.2 us)
Sparse Core Ops, SparseCore 0:
  14.0 64.4 all-gather.18
  332.7 64.4 all-gather.20
  503.1 46.9 all-gather.22
  551.5 46.6 all-gather.26
  667.4 46.8 all-gather.24
  799.8 46.8 all-gather.28
  848.8 64.5 all-gather.30
  982.5 64.7 all-gather.32
  1160.0 64.8 all-gather.34
  1228.3 34.2 reduce-scatter.50
  1266.0 55.6 all-reduce.40
  1325.1 34.9 reduce-scatter.48
  1363.9 40.2 reduce-scatter.46
  1407.8 36.0 reduce-scatter.44
  1447.4 35.9 reduce-scatter.42
  1486.9 33.6 reduce-scatter.40
  1527.1 96.0 reduce-scatter.38
  1627.3 42.4 reduce-scatter.36
  1673.7 42.4 reduce-scatter.34
where the time goes:
time: 1740 us; the launch traced here: 1720 us
  waiting for transfers between devices  545 us (31%)
  blocking collectives  516 us (30%)
  local copies, waits for them, and re-layouts  285 us (16%)
  matrix products  246 us (14%)
  other arithmetic  98.1 us (6%)
  between operations  18.4 us (1%)
    unnamed x9, blocking collectives  516 us
    all_gather x5, waiting for transfers between devices, norm_spread(): return lax.all_gather(normed, 'mp', axis=0, tiled=True)  218 us
    all_gather x4, waiting for transfers between devices, grad_spread(): return lax.all_gather(rounded, 'mp', axis=0, tiled=True)  152 us
    unnamed x253, local copies, waits for them, and re-layouts  140 us
    reduce_scatter x1, waiting for transfers between devices, shards(): lax.psum_scatter(bridge_weight_grad, ('dp', 'mp'), scatter_dimension=0, t...  55.7 us
    dynamic_slice x80, local copies, waits for them, and re-layouts, block_forward(): lax.map(partial(strip_forward, head_dim=head_dim), (queries.reshape(strip...  54.3 us
    reduce_scatter x1, waiting for transfers between devices, shards(): lax.psum_scatter(enc_grads[10], 'dp', scatter_dimension=1, tiled=True)  46.6 us
    reduce_scatter x1, waiting for transfers between devices, shards(): lax.psum_scatter(enc_grads[8], 'dp', scatter_dimension=0, tiled=True)  46.4 us
  transfers between devices with their start and end apart: 28, of which 16 were waited for; matrix products, arithmetic and copies ran while one was open for 32% of the time, Pallas kernels for 0%

commit v1 on v0

v1 whole, which is shorter than its diff:
```python
from functools import partial

import jax
import jax.numpy as jnp
from jax import lax
from jax.experimental import pallas as pl
from jax.experimental.pallas import tpu as pltpu
from jax.sharding import PartitionSpec as P

HEAD = 64
DHEAD = 32
EPSILON = 1e-06
MESH = pl.DeviceIdType.MESH
F32 = jnp.float32
BF16 = jnp.bfloat16
VMEM_BYTES = 60 * 1024 * 1024


def neighbours():
    dp, mp = lax.axis_index("dp"), lax.axis_index("mp")
    core, x, y = dp % 2, (dp // 2) % 2, dp // 4
    across_core = dp + 1 - 2 * core
    across_x = dp + 2 - 4 * x
    across_y = dp + 4 - 8 * y
    return dp, mp, core, x, y, across_core, across_x, across_y


def entry_barrier(parts):
    mp, across_core, across_x, across_y = parts
    dp = lax.axis_index("dp")
    barrier = pltpu.get_barrier_semaphore()
    planes = lax.axis_size("mp")
    for other in (across_core, across_x, across_y):
        pl.semaphore_signal(barrier, inc=1, device_id=(other, mp), device_id_type=MESH)
    for step in range(1, planes):
        pl.semaphore_signal(
            barrier, inc=1, device_id=(dp, (mp + step) % planes), device_id_type=MESH
        )
    pl.semaphore_wait(barrier, 3 + planes - 1)


def gather_kernel(count, planes, *refs):
    shards, wholes = refs[:count], refs[count : 2 * count]
    local_sem, send_sem, recv_sem = refs[2 * count :]
    dp, mp, core, x, y, across_core, across_x, across_y = neighbours()
    entry_barrier((mp, across_core, across_x, across_y))
    sends = []

    def send(src, dst, m, plane, kind, target, slot=None):
        copy = pltpu.make_async_remote_copy(
            src_ref=src,
            dst_ref=dst,
            send_sem=send_sem.at[m, plane if slot is None else slot, kind],
            recv_sem=recv_sem.at[m, plane, kind],
            device_id=target,
            device_id_type=MESH,
        )
        copy.start()
        sends.append(copy)

    def arrived(m, plane, kind, ref):
        pltpu.make_async_remote_copy(
            src_ref=ref,
            dst_ref=ref,
            send_sem=send_sem.at[m, plane, kind],
            recv_sem=recv_sem.at[m, plane, kind],
            device_id=(across_core, mp),
            device_id_type=MESH,
        ).wait_recv()

    def rows_of(m, owner, half=None):
        piece = shards[m].shape[0] // 8
        if half is None:
            return pl.ds(owner * piece, piece)
        return pl.ds(owner * piece + half * (piece // 2), piece // 2)

    A, X, Y, S, DY, DX, SX, SY, SDY, SDX = range(10)
    others = [(mp + step) % planes for step in range(1, planes)]
    copies = []
    for m in range(count):
        own = rows_of(m, dp)
        for plane in others:
            send(shards[m].at[own], wholes[m].at[mp, own], m, mp, A, (dp, plane), plane)
    for m in range(count):
        copy = pltpu.make_async_copy(shards[m], wholes[m].at[mp], local_sem.at[m])
        copy.start()
        copies.append(copy)

    diag = across_x + across_y - dp

    def stage_b(m):
        own = rows_of(m, dp)
        for plane in others:
            piece = wholes[m].at[plane, own]
            arrived(m, plane, A, piece)
            send(piece, piece, m, plane, X, (across_x, mp))
            send(piece, piece, m, plane, Y, (across_y, mp))
            send(piece, piece, m, plane, S, (across_core, mp))

    def stage_c(m):
        for plane in others:
            piece = wholes[m].at[plane, rows_of(m, across_x)]
            half = wholes[m].at[plane, rows_of(m, across_x, 0)]
            arrived(m, plane, X, piece)
            send(half, half, m, plane, DY, (across_y, mp))
            send(piece, piece, m, plane, SX, (across_core, mp))
            piece = wholes[m].at[plane, rows_of(m, across_y)]
            half = wholes[m].at[plane, rows_of(m, across_y, 1)]
            arrived(m, plane, Y, piece)
            send(half, half, m, plane, DX, (across_x, mp))
            send(piece, piece, m, plane, SY, (across_core, mp))

    def stage_d(m):
        for plane in others:
            half = wholes[m].at[plane, rows_of(m, diag, 0)]
            arrived(m, plane, DY, half)
            send(half, half, m, plane, SDY, (across_core, mp))
            half = wholes[m].at[plane, rows_of(m, diag, 1)]
            arrived(m, plane, DX, half)
            send(half, half, m, plane, SDX, (across_core, mp))

    shift = across_core - dp

    def stage_e(m):
        for plane in others:
            arrived(m, plane, S, wholes[m].at[plane, rows_of(m, across_core)])
            arrived(m, plane, SX, wholes[m].at[plane, rows_of(m, across_x + shift)])
            arrived(m, plane, SY, wholes[m].at[plane, rows_of(m, across_y + shift)])
            arrived(m, plane, SDY, wholes[m].at[plane, rows_of(m, diag + shift, 0)])
            arrived(m, plane, SDX, wholes[m].at[plane, rows_of(m, diag + shift, 1)])

    stages = (stage_b, stage_c, stage_d, stage_e)
    for tick in range(count + len(stages) - 1):
        for late, stage in enumerate(stages):
            if 0 <= tick - late < count:
                stage(tick - late)
    for copy in copies:
        copy.wait()
    for copy in sends:
        copy.wait_send()


def gather_weights(shards, planes):
    count = len(shards)
    kinds = 10
    return pl.pallas_call(
        partial(gather_kernel, count, planes),
        out_shape=[jax.ShapeDtypeStruct((planes,) + s.shape, s.dtype) for s in shards],
        in_specs=[pl.BlockSpec(memory_space=pl.ANY)] * count,
        out_specs=[pl.BlockSpec(memory_space=pl.ANY)] * count,
        scratch_shapes=[
            pltpu.SemaphoreType.DMA((count,)),
            pltpu.SemaphoreType.DMA((count, planes, kinds)),
            pltpu.SemaphoreType.DMA((count, planes, kinds)),
        ],
        compiler_params=pltpu.CompilerParams(
            collective_id=0, has_side_effects=True, vmem_limit_bytes=VMEM_BYTES
        ),
        name="gather_weights",
    )(*shards)


def reduce_kernel(count, planes, *refs):
    parts, sums = refs[:count], refs[count : 2 * count]
    rest = refs[2 * count :]
    mine, from_core, from_x, from_y, then_y, then_x, from_z = (
        rest[k * count : (k + 1) * count] for k in range(7)
    )
    local_sem, send_sem, recv_sem = rest[7 * count :]
    dp, mp, core, x, y, across_core, across_x, across_y = neighbours()
    entry_barrier((mp, across_core, across_x, across_y))
    sends = []
    C, X, Y, XY, YX, Z = range(6)

    def send(src, dst, m, kind, target, send_slot=None, recv_slot=None):
        copy = pltpu.make_async_remote_copy(
            src_ref=src,
            dst_ref=dst,
            send_sem=send_sem.at[m, kind if send_slot is None else send_slot],
            recv_sem=recv_sem.at[m, kind if recv_slot is None else recv_slot],
            device_id=target,
            device_id_type=MESH,
        )
        copy.start()
        sends.append(copy)

    def arrived(m, kind, ref):
        pltpu.make_async_remote_copy(
            src_ref=ref,
            dst_ref=ref,
            send_sem=send_sem.at[m, kind],
            recv_sem=recv_sem.at[m, kind],
            device_id=(across_core, mp),
            device_id_type=MESH,
        ).wait_recv()

    local = []
    for m in range(count):
        copy = pltpu.make_async_copy(parts[m].at[:, :, :, core], mine[m], local_sem.at[m])
        copy.start()
        local.append(copy)
        send(parts[m].at[:, :, :, 1 - core], from_core[m], m, C, (across_core, mp))

    def stage_core(m):
        local[m].wait()
        arrived(m, C, from_core[m])
        half = mine[m].shape[3] // 2

        @pl.loop(0, planes)
        def _(p):
            for b in range(2):
                for a in range(2):
                    mine[m][p, b, a] = mine[m][p, b, a] + from_core[m][p, b, a]

        send(mine[m].at[:, :, 1 - x, pl.ds(0, half)], from_x[m], m, X, (across_x, mp))
        send(mine[m].at[:, 1 - y, :, pl.ds(half, half)], from_y[m], m, Y, (across_y, mp))

    def stage_plane(m):
        half = mine[m].shape[3] // 2
        first, second = pl.ds(0, half), pl.ds(half, half)
        arrived(m, X, from_x[m])

        @pl.loop(0, planes)
        def _(p):
            for b in range(2):
                mine[m][p, b, x, first] = mine[m][p, b, x, first] + from_x[m][p, b]

        send(mine[m].at[:, 1 - y, x, first], then_y[m], m, XY, (across_y, mp))
        arrived(m, Y, from_y[m])

        @pl.loop(0, planes)
        def _(p):
            for a in range(2):
                mine[m][p, y, a, second] = mine[m][p, y, a, second] + from_y[m][p, a]

        send(mine[m].at[:, y, 1 - x, second], then_x[m], m, YX, (across_x, mp))

    def stage_corner(m):
        half = mine[m].shape[3] // 2
        first, second = pl.ds(0, half), pl.ds(half, half)
        arrived(m, XY, then_y[m])
        arrived(m, YX, then_x[m])

        @pl.loop(0, planes)
        def _(p):
            mine[m][p, y, x, first] = mine[m][p, y, x, first] + then_y[m][p]
            mine[m][p, y, x, second] = mine[m][p, y, x, second] + then_x[m][p]

        for step in range(1, planes):
            plane = (mp + step) % planes
            send(
                mine[m].at[plane, y, x],
                from_z[m].at[mp],
                m,
                Z,
                (dp, plane),
                Z + plane,
                Z + mp,
            )

    def stage_line(m):
        total = mine[m][mp, y, x].astype(F32)
        for step in range(1, planes):
            plane = (mp + step) % planes
            arrived(m, Z + plane, from_z[m].at[plane])
            total = total + from_z[m][plane].astype(F32)
        sums[m][...] = total

    stages = (stage_core, stage_plane, stage_corner, stage_line)
    for tick in range(count + len(stages) - 1):
        for late, stage in enumerate(stages):
            if 0 <= tick - late < count:
                stage(tick - late)
    for copy in sends:
        copy.wait_send()


def reduce_gradients(parts, planes):
    count = len(parts)
    shapes = [part.shape[4:] for part in parts]

    def buffers(*lead, halves=False):
        return [
            pltpu.VMEM(lead + (r // 2 if halves else r, c), BF16) for r, c in shapes
        ]

    return pl.pallas_call(
        partial(reduce_kernel, count, planes),
        out_shape=[jax.ShapeDtypeStruct(s, F32) for s in shapes],
        in_specs=[pl.BlockSpec(memory_space=pl.ANY)] * count,
        out_specs=[pl.BlockSpec(memory_space=pltpu.VMEM)] * count,
        scratch_shapes=buffers(planes, 2, 2)
        + buffers(planes, 2, 2)
        + buffers(planes, 2, halves=True)
        + buffers(planes, 2, halves=True)
        + buffers(planes, halves=True)
        + buffers(planes, halves=True)
        + buffers(planes)
        + [
            pltpu.SemaphoreType.DMA((count,)),
            pltpu.SemaphoreType.DMA((count, 5 + planes)),
            pltpu.SemaphoreType.DMA((count, 5 + planes)),
        ],
        compiler_params=pltpu.CompilerParams(
            collective_id=1, has_side_effects=True, vmem_limit_bytes=VMEM_BYTES
        ),
        name="reduce_gradients",
    )(*parts)


def spread(shards, sizes):
    planes = sizes["mp"]
    if sizes["dp"] == 8:
        return gather_weights(shards, planes)
    return [lax.all_gather(s, "mp", axis=0) for s in shards]


def collect(parts, sizes):
    planes = sizes["mp"]
    if sizes["dp"] == 8:
        return reduce_gradients(
            [p.reshape((planes, 2, 2, 2) + p.shape[2:]) for p in parts], planes
        )
    sums = []
    for part in parts:
        part = lax.psum_scatter(part, "mp", scatter_dimension=0, tiled=False)
        sums.append(lax.psum_scatter(part.astype(F32), "dp", scatter_dimension=0, tiled=False))
    return sums


def attention_forward_kernel(head_dim, length_ref, triple_ref, out_ref, logsum_ref):
    rows, width = triple_ref.shape[0], triple_ref.shape[1] // 3
    visible = lax.broadcasted_iota(jnp.int32, (1, rows), 1) < length_ref[0]
    for head in range(width // head_dim):
        low = head * head_dim
        query = triple_ref[:, low : low + head_dim]
        key = triple_ref[:, width + low : width + low + head_dim]
        value = triple_ref[:, 2 * width + low : 2 * width + low + head_dim]
        scores = lax.dot_general(
            query, key, (((1,), (1,)), ((), ())), preferred_element_type=F32
        ) * head_dim ** (-0.5)
        scores = jnp.where(visible, scores, -1e30)
        ceiling = jnp.max(scores, -1, keepdims=True)
        exponent = jnp.exp(scores - ceiling)
        denominator = jnp.sum(exponent, -1, keepdims=True)
        chances = (exponent / denominator).astype(BF16)
        attended = jnp.dot(chances, value, preferred_element_type=F32)
        out_ref[:, low : low + head_dim] = attended.astype(BF16)
        logsum_ref[:, head : head + 1] = ceiling + jnp.log(denominator)


def attention_backward_kernel(
    head_dim, length_ref, triple_ref, attended_ref, mixed_ref, logsum_ref, out_ref
):
    rows, width = triple_ref.shape[0], triple_ref.shape[1] // 3
    factor = head_dim ** (-0.5)
    visible = lax.broadcasted_iota(jnp.int32, (1, rows), 1) < length_ref[0]
    for head in range(width // head_dim):
        low = head * head_dim
        query = triple_ref[:, low : low + head_dim]
        key = triple_ref[:, width + low : width + low + head_dim]
        value = triple_ref[:, 2 * width + low : 2 * width + low + head_dim]
        mixed = mixed_ref[:, low : low + head_dim]
        attended = attended_ref[:, low : low + head_dim]
        scores = (
            lax.dot_general(query, key, (((1,), (1,)), ((), ())), preferred_element_type=F32)
            * factor
        )
        scores = jnp.where(visible, scores, -1e30)
        chances = jnp.exp(scores - logsum_ref[:, head : head + 1])
        chance_grad = lax.dot_general(
            mixed, value, (((1,), (1,)), ((), ())), preferred_element_type=F32
        )
        row_sums = jnp.sum(mixed.astype(F32) * attended.astype(F32), -1, keepdims=True)
        score_grad = (chances * (chance_grad - row_sums)).astype(BF16)
        query_grad = jnp.dot(score_grad, key, preferred_element_type=F32) * factor
        key_grad = (
            lax.dot_general(
                score_grad, query, (((0,), (0,)), ((), ())), preferred_element_type=F32
            )
            * factor
        )
        value_grad = lax.dot_general(
            chances.astype(BF16), mixed, (((0,), (0,)), ((), ())), preferred_element_type=F32
        )
        out_ref[:, low : low + head_dim] = query_grad.astype(BF16)
        out_ref[:, width + low : width + low + head_dim] = key_grad.astype(BF16)
        out_ref[:, 2 * width + low : 2 * width + low + head_dim] = value_grad.astype(BF16)


def plane_spec(*shape):
    return pl.BlockSpec((None,) + shape, lambda p: (p, 0, 0))


LENGTH_SPEC = pl.BlockSpec(memory_space=pltpu.SMEM)


def attention_forward(triple, length, head_dim):
    planes, rows, width = triple.shape
    width //= 3
    heads = width // head_dim
    return pl.pallas_call(
        partial(attention_forward_kernel, head_dim),
        grid=(planes,),
        out_shape=[
            jax.ShapeDtypeStruct((planes, rows, width), BF16),
            jax.ShapeDtypeStruct((planes, rows, heads), F32),
        ],
        in_specs=[LENGTH_SPEC, plane_spec(rows, 3 * width)],
        out_specs=[plane_spec(rows, width), plane_spec(rows, heads)],
        compiler_params=pltpu.CompilerParams(vmem_limit_bytes=VMEM_BYTES),
        name="attention_forward",
    )(length, triple)


def attention_backward(triple, attended, mixed, logsum, length, head_dim):
    planes, rows, width = attended.shape
    heads = width // head_dim
    return pl.pallas_call(
        partial(attention_backward_kernel, head_dim),
        grid=(planes,),
        out_shape=jax.ShapeDtypeStruct((planes, rows, 3 * width), BF16),
        in_specs=[
            LENGTH_SPEC,
            plane_spec(rows, 3 * width),
            plane_spec(rows, width),
            plane_spec(rows, width),
            plane_spec(rows, heads),
        ],
        out_specs=plane_spec(rows, 3 * width),
        compiler_params=pltpu.CompilerParams(vmem_limit_bytes=VMEM_BYTES),
        name="attention_backward",
    )(length, triple, attended, mixed, logsum)


def normalize(stream, gain_vector, shift_vector):
    centered = stream - jnp.mean(stream, -1, keepdims=True)
    variance = jnp.mean(centered * centered, -1, keepdims=True)
    return centered * lax.rsqrt(variance + EPSILON) * gain_vector + shift_vector


def layer_back(stream, gain_vector, shift_vector, upstream):
    unused, pullback = jax.vjp(normalize, stream, gain_vector, shift_vector)
    return pullback(upstream)


def gelu_exact(inputs):
    return jax.nn.gelu(inputs, approximate=False)


def mm(spec, left, right):
    return jnp.einsum(spec, left, right, preferred_element_type=F32)


def block_forward(stream, params, weights, length, head_dim):
    (gain, shift, head_bias, output_bias, feed_gain, feed_shift, up_bias, down_bias) = params
    attn, up, down = weights
    planes, width = attn.shape[0], attn.shape[2] // 4
    normed = normalize(stream, gain, shift).astype(BF16)
    bias = jnp.concatenate([head_bias[0], jnp.zeros_like(head_bias[0]), head_bias[1]], -1)
    triple = mm("td,zde->zte", normed, attn[:, :, : 3 * width])
    triple = (triple + bias[:, None]).astype(BF16)
    attended, logsum = attention_forward(triple, length, head_dim)
    middle = stream + (mm("zte,zde->td", attended, attn[:, :, 3 * width :]) + output_bias)
    feed_input = normalize(middle, feed_gain, feed_shift).astype(BF16)
    before = mm("td,zdf->ztf", feed_input, up) + up_bias[:, None]
    hidden = gelu_exact(before).astype(BF16)
    result = middle + (mm("ztf,zfd->td", hidden, down) + down_bias)
    return result, (stream, normed, triple, logsum, attended, middle, feed_input, before, hidden)


def column_sums(values):
    return jnp.sum(values.astype(F32), -2)


def block_backward(upstream, params, weights, stored, length, head_dim):
    (gain, shift, head_bias, output_bias, feed_gain, feed_shift, up_bias, down_bias) = params
    attn, up, down = weights
    stream, normed, triple, logsum, attended, middle, feed_input, before, hidden = stored
    planes, width = attn.shape[0], attn.shape[2] // 4
    branch_grad = upstream.astype(BF16)
    down_bias_grad = column_sums(branch_grad)
    down_grad = mm("td,ztf->zdf", branch_grad, hidden).astype(BF16)
    hidden_grad = mm("td,zfd->ztf", branch_grad, down)
    unused, gelu_pull = jax.vjp(gelu_exact, before)
    before_grad = gelu_pull(hidden_grad)[0].astype(BF16)
    up_bias_grad = column_sums(before_grad)
    up_grad = mm("td,ztf->zdf", feed_input, before_grad).astype(BF16)
    feed_rows = mm("ztf,zdf->td", before_grad, up)
    middle_part, feed_gain_grad, feed_shift_grad = layer_back(
        middle, feed_gain, feed_shift, feed_rows
    )
    middle_grad = upstream + middle_part
    attn_grad = middle_grad.astype(BF16)
    output_bias_grad = column_sums(attn_grad)
    output_grad = mm("td,zte->zde", attn_grad, attended)
    mixed_grad = mm("td,zde->zte", attn_grad, attn[:, :, 3 * width :]).astype(BF16)
    triple_grad = attention_backward(triple, attended, mixed_grad, logsum, length, head_dim)
    triple_sums = column_sums(triple_grad)
    head_bias_grad = jnp.stack([triple_sums[:, :width], triple_sums[:, 2 * width :]])
    triple_weight_grad = mm("td,zte->zde", normed, triple_grad)
    attn_weight_grad = jnp.concatenate([triple_weight_grad, output_grad], -1).astype(BF16)
    input_rows = mm("zte,zde->td", triple_grad, attn[:, :, : 3 * width])
    stream_part, gain_grad, shift_grad = layer_back(stream, gain, shift, input_rows)
    vectors = (
        gain_grad,
        shift_grad,
        output_bias_grad,
        feed_gain_grad,
        feed_shift_grad,
        down_bias_grad,
    )
    return middle_grad + stream_part, (attn_weight_grad, up_grad, down_grad), vectors, (
        head_bias_grad,
        up_bias_grad,
    )


def shards(sizes, *inputs):
    patches, lengths = inputs[:2]
    cotangent = inputs[28]
    planes, groups = sizes["mp"], sizes["dp"]
    mp = lax.axis_index("mp")
    length = lax.dynamic_slice_in_dim(lengths, mp, 1)

    def block_of(at):
        (gain, shift, proj, head_bias, out, out_bias, f_gain, f_shift, up, up_bias, down, d_bias) = (
            inputs[at : at + 12]
        )
        packed = jnp.concatenate([proj[0], proj[1], proj[2], out.T], -1)
        vectors = (gain, shift, out_bias, f_gain, f_shift, d_bias)
        return (packed, up, down), vectors, (head_bias, up_bias)

    enc_shards, enc_vectors, enc_split = block_of(2)
    bridge_weight, bridge_bias = inputs[14:16]
    dec_shards, dec_vectors, dec_split = block_of(16)
    wholes = spread(enc_shards + dec_shards, sizes)
    small = jnp.concatenate([v.reshape(-1) for v in enc_split + dec_split])
    small = lax.all_gather(small, "mp", axis=0)

    def params_of(vectors, split, at):
        gain, shift, out_bias, f_gain, f_shift, d_bias = vectors
        width, hidden = split[0].shape[1], split[1].shape[0]
        head_bias = small[:, at : at + 2 * width].reshape(planes, 2, width).transpose(1, 0, 2)
        up_bias = small[:, at + 2 * width : at + 2 * width + hidden]
        return (gain, shift, head_bias, out_bias, f_gain, f_shift, up_bias, d_bias)

    encoder = params_of(enc_vectors, enc_split, 0)
    decoder = params_of(dec_vectors, dec_split, 2 * enc_split[0].shape[1] + enc_split[1].shape[0])

    rows = patches.shape[0]
    padded = -(-rows // 32) * 32
    stream = jnp.pad(patches, ((0, padded - rows), (0, 0))).astype(F32)
    upstream = jnp.pad(cotangent, ((0, padded - rows), (0, 0))).astype(F32)

    encoded, enc_stored = block_forward(stream, encoder, wholes[:3], length, HEAD)
    bridge_input = encoded.astype(BF16)
    bridged = mm("td,de->te", bridge_input, bridge_weight) + bridge_bias
    decoded, dec_stored = block_forward(bridged, decoder, wholes[3:], length, DHEAD)
    bridged_grad, dec_mats, dec_vecs, dec_splits = block_backward(
        upstream, decoder, wholes[3:], dec_stored, length, DHEAD
    )
    bridge_rows = bridged_grad.astype(BF16)
    bridge_weight_grad = mm("td,te->de", bridge_input, bridge_rows)
    bridge_bias_grad = column_sums(bridge_rows)
    encoded_grad = mm("te,de->td", bridge_rows, bridge_weight)
    patches_grad, enc_mats, enc_vecs, enc_splits = block_backward(
        encoded_grad, encoder, wholes[:3], enc_stored, length, HEAD
    )

    def by_group(vector):
        return vector.reshape(groups, planes, -1).transpose(1, 0, 2)

    def by_plane(vector):
        return vector.reshape(planes, groups, -1)

    pieces = [by_group(v) for v in enc_vecs + dec_vecs + (bridge_bias_grad,)]
    for head_bias_grad, up_bias_grad in (enc_splits, dec_splits):
        pieces += [by_plane(head_bias_grad[0]), by_plane(head_bias_grad[1]), by_plane(up_bias_grad)]
    lengths_of = [p.shape[-1] for p in pieces]
    packed = jnp.concatenate(pieces, -1)
    wide = bridge_weight.shape[1]
    bridge_part = bridge_weight_grad.reshape(groups, planes, -1, wide).transpose(1, 0, 2, 3)
    deep = bridge_part.shape[2]
    lines = -(-packed.shape[-1] // wide)
    packed = jnp.pad(packed, ((0, 0), (0, 0), (0, lines * wide - packed.shape[-1])))
    packed = packed.reshape(planes, groups, lines, wide)
    spare = -(deep + lines) % 32
    misc = jnp.concatenate(
        [bridge_part, packed, jnp.zeros((planes, groups, spare, wide), F32)], 2
    ).astype(BF16)

    def in_groups(grad):
        return grad.reshape(planes, groups, -1, grad.shape[-1])

    sums = collect([in_groups(g) for g in enc_mats + dec_mats] + [misc], sizes)
    misc_sum = sums[6]
    bridge_out = misc_sum[:deep]
    flat = misc_sum[deep : deep + lines].reshape(-1)
    taken, at = [], 0
    for size in lengths_of:
        taken.append(flat[at : at + size])
        at += size

    def block_out(mats, vectors, splits):
        attn, up, down = mats
        width = attn.shape[1] // 4
        proj = attn[:, : 3 * width].reshape(-1, 3, width).transpose(1, 0, 2)
        gain, shift, out_bias, f_gain, f_shift, d_bias = vectors
        head_bias = jnp.stack([splits[0], splits[1]])
        return (
            gain,
            shift,
            proj,
            head_bias,
            attn[:, 3 * width :].T,
            out_bias,
            f_gain,
            f_shift,
            up,
            splits[2],
            down.T,
            d_bias,
        )

    enc_out = block_out(sums[0:3], taken[0:6], taken[13:16])
    dec_out = block_out(sums[3:6], taken[6:12], taken[16:19])
    return (
        (decoded[:rows].astype(BF16), patches_grad[:rows].astype(BF16))
        + enc_out
        + (bridge_out, taken[12])
        + dec_out
    )


def solution(mesh):
    block_in = (
        P(),
        P(),
        P(None, None, "mp"),
        P(None, "mp"),
        P("mp", None),
        P(),
        P(),
        P(),
        P(None, "mp"),
        P("mp"),
        P("mp", None),
        P(),
    )
    both = P(("dp", "mp"))
    block_out = (
        both,
        both,
        P(None, "dp", "mp"),
        P(None, ("mp", "dp")),
        P("mp", "dp"),
        both,
        both,
        both,
        P("dp", "mp"),
        P(("mp", "dp")),
        P("mp", "dp"),
        both,
    )
    rows = P(("dp", "mp"), None)
    return jax.shard_map(
        partial(shards, dict(mesh.shape)),
        mesh=mesh,
        in_specs=(rows, P("dp")) + block_in + (P(), P()) + block_in + (rows,),
        out_specs=(rows, rows) + block_out + (rows, both) + block_out,
        check_vma=False,
    )
```

time: 1740 us -> 552 us (0.32)
  waiting for transfers between devices: 545 us -> 0 us
  blocking collectives: 516 us -> 13.2 us
  Pallas kernels: 0 us -> 346 us
  local copies, waits for them, and re-layouts: 285 us -> 38.3 us
  matrix products: 246 us -> 118 us
  other arithmetic: 98.1 us -> 26.8 us
    unnamed x9 -> x0, blocking collectives: 516 us -> none
    all_gather x9 -> x0, waiting for transfers between devices: 370 us -> none  [the longest x5 218 us: norm_spread(): return lax.all_gather(normed, 'mp', axis=0, tiled=True)]
    pallas_call x0 -> x6, Pallas kernels: none -> 346 us  [the longest x1 162 us: gather_weights(): pl.pallas_call(partial(gather_kernel, count, planes), out_shape=[jax.Shap...]
    reduce_scatter x6 -> x0, waiting for transfers between devices: 149 us -> none  [the longest x1 55.7 us: shards(): lax.psum_scatter(bridge_weight_grad, ('dp', 'mp'), scatter_dimension=0, t...]
    unnamed x253 -> x155, local copies, waits for them, and re-layouts: 140 us -> 10.7 us
    dot_general x86 -> x27, matrix products: 220 us -> 118 us  [mm(): return jnp.einsum(spec, left, right, preferred_element_type=F32)]
    dynamic_slice x80 -> x1, local copies, waits for them, and re-layouts: 54.3 us -> 0.58 us  [shards(): length = lax.dynamic_slice_in_dim(lengths, mp, 1)]
    convert_element_type x15 -> x0, other arithmetic: 30.3 us -> none  [the longest x8 12 us: strip_backward(): score_grad = score_grad.astype(jnp.bfloat16)]
  transfers between devices with their start and end apart: 28 -> 0, of which waited for: 16 -> 0; matrix products, arithmetic and copies ran while one was open for 32% -> 0% of each run, Pallas kernels for 0% -> 0%
where the time goes in v1:
time: 552 us; the launch traced here: 544 us
  Pallas kernels  346 us (63%)
  matrix products  118 us (21%)
  local copies, waits for them, and re-layouts  38.3 us (7%)
  other arithmetic  26.8 us (5%)
  blocking collectives  13.2 us (2%)
    pallas_call x1, Pallas kernels, gather_weights(): pl.pallas_call(partial(gather_kernel, count, planes), out_shape=[jax.Shap...  162 us
    dot_general x27, matrix products, mm(): return jnp.einsum(spec, left, right, preferred_element_type=F32)  118 us
    pallas_call x1, Pallas kernels, reduce_gradients(): pl.pallas_call(partial(reduce_kernel, count, planes), out_shape=[jax.Shap...  107 us
    pallas_call x2, Pallas kernels, attention_backward(): pl.pallas_call(partial(attention_backward_kernel, head_dim), grid=(planes...  45.9 us
    pallas_call x2, Pallas kernels, attention_forward(): pl.pallas_call(partial(attention_forward_kernel, head_dim), grid=(planes,...  30.4 us
    all_gather x1, blocking collectives, shards(): small = lax.all_gather(small, 'mp', axis=0)  13.2 us
    transpose x4, local copies, waits for them, and re-layouts, mm(): return jnp.einsum(spec, left, right, preferred_element_type=F32)  12.5 us

profile of v1, /device:TPU:28, one launch (start us, length us, event | category | flops | bytes accessed | tf_op | source)
XLA Modules:
  0.0 543.8 jit_solution(11192599345497508012)
XLA Ops:
  0.7 1.3 fusion.130
  2.7 1.5 pad_maximum_fusion.2.refs_0_
  5.3 162.1 %gather_weights.1 = (bf16[4,768,768]{2,1,0:T(8,128)(2,1)}, bf16[4,768,768]{2,1,0:T(8,128)(2,1)}, bf16[4,768,768]{2,1,0:T(8,128)(2,1)}, bf16[4,512,512]{2,1,0:T(8...) custom-call(bf16[768,768]{1,0:T(8,128)(2,1)} %pad_maximum_fusion.2.refs_0_, ...), custom_call_target="tpu_custom_call" | custom-call | tf_op jit(solution)/shard_map/gather_weights/pallas_call | solution.py:146
  167.6 13.2 %all-gather.1 = f32[4,1,1920]{2,1,0:T(1,128)S(1)} all-gather(f32[1,1,1920]{2,1,0:T(1,128)S(1)} %reshape.346), channel_id=2, replica_groups=mesh['dp'=8,'mp'=4] {'mp'}, dimensions={0}, use_global_device_ids=true | all-gather | bytes 38400 | tf_op jit(solution)/shard_map/all_gather | solution.py:539
  181.6 6.0 %fusion.48.triple_ref = bf16[4,544,576]{2,1,0:T(8,128)(2,1)} fusion(f32[4,576]{1,0:T(4,128)S(1)} %pad_maximum_fusion.4, bf16[4,768,768]{2,1,0:T(8,128)(2,1)} %get-tuple-element.45, f32[768]{0:T(1024)S(1)} %copy-done.50, f32[768]{0:T(1024)S(1)} %copy-done.36, f32[544]{0:T(1024)S(1)} %fusion.101, f32[544]{0:T(1024)S(1)} %broadcast_multiply_fusion.3, ...), kind=kOutput, calls=%fused_computation.72 | convolution fusion | flops 1930199040 | bytes 7271168 | tf_op jit(solution)/shard_map/td,zde->zte/dot_general | solution.py:452
  188.3 13.8 %attention_forward.2 = (bf16[4,544,192]{2,1,0:T(8,128)(2,1)}, f32[4,544,3]{2,1,0:T(8,128)}) custom-call(s32[1]{0:T(128)} %dynamic_slice.3.length_ref, bf16[4,544,576]{2,1,0:T(8,128)(2,1)} %fusion.48.triple_ref), custom_call_target="tpu_custom_call" | custom-call | tf_op jit(solution)/shard_map/attention_forward/pallas_call | solution.py:402
  202.1 3.2 fusion.134
  205.8 18.1 %fusion.9 = (bf16[4,544,768]{2,1,0:T(8,128)(2,1)S(1)}, f32[4,544,768]{2,1,0:T(8,128)}, f32[4,768,544]{1,2,0:T(8,128)}) fusion(f32[4,768]{1,0:T(4,128)S(1)} %slice.289, bf16[4,768,768]{2,1,0:T(8,128)(2,1)S(1)} %bitcast.436, f32[544,768]{1,0:T(8,128)S(1)} %get-tuple-element.266, f32[768]{0:T(1024)S(1)} %copy-done.49, f32[768]{0:T(1024)S(1)} %copy-done.35, ...), kind=kOutput, calls=%fused_computation.17 | convolution fusion | flops 2679300096 | bytes 23124224 | tf_op jit(solution)/shard_map/td,zdf->ztf/dot_general | solution.py:452
  223.9 2.8 fusion.64
  229.0 2.3 fusion.66.triple_ref
  231.4 16.6 %attention_forward.3 = (bf16[4,544,128]{2,1,0:T(8,128)(2,1)}, f32[4,544,4]{2,1,0:T(8,128)}) custom-call(s32[1]{0:T(128)} %dynamic_slice.3.length_ref, bf16[4,544,384]{2,1,0:T(8,128)(2,1)} %fusion.66.triple_ref), custom_call_target="tpu_custom_call" | custom-call | tf_op jit(solution)/shard_map/attention_forward/pallas_call | solution.py:402
  248.0 1.9 fusion.136
  250.3 11.9 %fusion.31 = (bf16[4,544,512]{2,1,0:T(8,128)(2,1)}, f32[4,544,512]{2,1,0:T(8,128)S(1)}, f32[4,512,544]{1,2,0:T(8,128)S(1)}) fusion(f32[4,512]{1,0:T(4,128)S(1)} %slice.293, bf16[4,512,512]{2,1,0:T(8,128)(2,1)S(1)} %copy-done.46, f32[544,512]{1,0:T(8,128)S(1)} %get-tuple-element.271, f32[512]{0:T(512)S(1)} %copy-done.53, f32[512]{0:T(512)S(1)} %copy-done.41, ...), kind=kOutput, calls=%fused_computation.50 | convolution fusion | flops 1215774720 | bytes 14369024 | tf_op jit(solution)/shard_map/td,zdf->ztf/dot_general | solution.py:452
  262.2 3.0 fusion.138
  265.2 1.6 multiply_reduce_fusion.2
  268.4 2.3 fusion.79.mixed_ref
  270.8 27.3 %attention_backward.2 = bf16[4,544,384]{2,1,0:T(8,128)(2,1)} custom-call(s32[1]{0:T(128)} %dynamic_slice.3.length_ref, bf16[4,544,384]{2,1,0:T(8,128)(2,1)} %fusion.66.triple_ref, bf16[4,544,128]{2,1,0:T(8,128)(2,1)} %get-tuple-element.50.attended_ref, bf16[4,544,128]{2,1,0:T(8,128)(2,1)} %fusion.79.mixed_ref, f32[4,544,4]{2,1,0:T(8,128)} %get-tuple-element.53.logsum_ref), custom_call_target="tpu_custom_call" | custom-call | tf_op jit(solution)/shard_map/attention_backward/pallas_call | solution.py:419
  298.1 3.7 multiply_reduce_fusion.3
  303.5 10.0 %fusion.137 = (bf16[4,768]{1,0:T(4,128)(2,1)S(1)}, bf16[4,544,768]{2,1,0:T(8,128)(2,1)S(1)}) fusion(f32[4,544,768]{2,1,0:T(8,128)} %get-tuple-element.231, bf16[4,768,768]{2,1,0:T(8,128)(2,1)} %get-tuple-element.48, f32[544,768]{1,0:T(8,128)S(1)} %fusion.139, f32[4,768,544]{1,2,0:T(8,128)} %get-tuple-element.267, f32[4,768]{1,0:T(4,128)S(1)} %slice.289), kind=kOutput, calls=%fused_computation.244 | convolution fusion | flops 2594067456 | bytes 23119872 | tf_op jit(solution)/shard_map/td,zfd->ztf/dot_general | solution.py:452
  313.5 3.1 fusion.62
  318.9 3.3 convolution_convert_fusion.6
  322.2 1.5 copy.188
  323.7 18.6 %attention_backward.3 = bf16[4,544,576]{2,1,0:T(8,128)(2,1)} custom-call(s32[1]{0:T(128)} %dynamic_slice.3.length_ref, bf16[4,544,576]{2,1,0:T(8,128)(2,1)} %fusion.48.triple_ref, bf16[4,544,192]{2,1,0:T(8,128)(2,1)} %get-tuple-element.46.attended_ref, bf16[4,544,192]{2,1,0:T(8,128)(2,1)} %bitcast.399, f32[4,544,3]{2,1,0:T(8,128)} %get-tuple-element.54.logsum_ref), custom_call_target="tpu_custom_call" | custom-call | tf_op jit(solution)/shard_map/attention_backward/pallas_call | solution.py:419
  342.3 6.7 %fusion.59 = (bf16[768]{0:T(1024)(128)(2,1)S(1)}, f32[544]{0:T(1024)S(1)}, bf16[768]{0:T(1024)(128)(2,1)S(1)}, f32[544,768,1]{1,0,2:T(8,128)}) fusion(f32[544]{0:T(1024)S(1)} %fusion.101, f32[544]{0:T(1024)S(1)} %broadcast_multiply_fusion.3, bf16[529,768]{1,0:T(8,128)(2,1)S(1)} %copy-done.7, f32[768]{0:T(1024)S(1)} %copy-done.36, ...), kind=kOutput, calls=%fused_computation.90 | convolution fusion | flops 1928943616 | bytes 9213824 | tf_op jit(solution)/shard_map/zte,zde->td/dot_general | solution.py:452
  349.2 2.3 reduce.5
  352.6 1.7 reduce.7
  355.1 2.0 convolution_convert_fusion.7
  357.2 1.3 maximum_maximum_fusion.refs_6_
  359.0 3.4 convolution_convert_fusion.3
  362.3 2.7 fusion.67
  365.0 2.7 copy.193
  367.8 1.4 fusion.80
  369.2 1.3 copy.194
  370.5 3.1 pad_maximum_fusion.1.refs_3_
  373.6 7.7 %convolution_convert_fusion = bf16[4,768,768]{1,2,0:T(8,128)(2,1)} fusion(bf16[4,544,768]{2,1,0:T(8,128)(2,1)} %copy-done.61, f32[544,768]{1,0:T(8,128)S(1)} %copy-done.10), kind=kOutput, calls=%fused_computation.70 | convolution fusion | flops 2569691136 | bytes 9732096 | tf_op jit(solution)/shard_map/td,ztf->zdf/dot_general | solution.py:452
  381.3 6.2 %convolution_convert_fusion.1 = bf16[4,768,768]{1,2,0:T(8,128)(2,1)} fusion(bf16[4,544,768]{2,1,0:T(8,128)(2,1)S(1)} %copy-done.63, f32[544,768]{1,0:T(8,128)S(1)} %copy-done.13, f32[768]{0:T(1024)S(1)} %copy-done.49, f32[768]{0:T(1024)S(1)} %copy-done.35, f32[544]{0:T(1024)S(1)} %fusion.102, f32[544]{0:T(1024)S(1)} %broadcast_multiply_fusion.2), kind=kOutput, calls=%fused_computation.71 | convolution fusion | flops 2571362304 | bytes 9742592 | tf_op jit(solution)/shard_map/td,ztf->zdf/dot_general | solution.py:452
  387.5 4.9 convert_bitcast_fusion
  392.4 5.9 %copy.190 = bf16[4,768,576]{2,1,0:T(8,128)(2,1)} copy(bf16[4,768,576]{1,2,0:T(8,128)(2,1)} %convert_bitcast_fusion) | data formatting | bytes 7077888 | tf_op jit(solution)/shard_map/td,zte->zde/transpose | solution.py:452
  398.3 3.9 fusion.68
  402.3 2.5 copy.192
  404.8 6.1 %pad_maximum_fusion.refs_0_ = bf16[4,2,2,2,96,768]{5,4,3,2,1,0:T(8,128)(2,1)} fusion(bf16[4,2,2,2,96,192]{5,4,3,2,1,0:T(8,128)(2,1)} %bitcast.395, bf16[4,2,2,2,96,576]{5,4,3,2,1,0:T(8,128)(2,1)} %bitcast.394), kind=kLoop, calls=%fused_computation.33 | loop fusion | flops 9437184 | bytes 9437184 | tf_op jit(solution)/shard_map/concatenate | solution.py:502
  410.9 3.2 convolution_convert_fusion.2
  414.0 107.0 %reduce_gradients.1 = (f32[96,768]{1,0:T(8,128)}, f32[96,768]{1,0:T(8,128)}, f32[96,768]{1,0:T(8,128)}, f32[64,512]{1,0:T(8,128)}, f32[64,512]{1,0:T(8,128)}, /*index=5*/f32[64,512]{1,0:T(8,128)}, f32[32,512]{1,0:T(8,128)}) custom-call(bf16[4,2,2,2,96,768]{5,4,3,2,1,0:T(8,128)(2,1)} %pad_maximum_fusion.refs_0_, bf16[4,2,2,2,96,768]{5,4,3,2,1,0:T(8,128)(2,1)} %bitcast.398, ...), custom_call_target="tpu_custom_call" | custom-call | tf_op jit(solution)/shard_map/reduce_gradients/pallas_call | solution.py:287
  521.1 1.6 slice_bitcast_fusion.8
  523.2 1.5 slice_bitcast_fusion.16
  531.3 1.4 slice_bitcast_fusion.4
  533.8 2.3 fusion.124
  538.1 1.3 convolution_bitcast_fusion.1
  (258 shorter events, 28.4 us)
Async XLA Ops:
  0.7 226.0 %copy-start = (bf16[768,512]{1,0:T(8,128)(2,1)S(1)}, bf16[768,512]{1,0:T(8,128)(2,1)}, u32[]{:S(2)}) copy-start(bf16[768,512]{1,0:T(8,128)(2,1)} %param.43) | copy-start | bytes 2359300
  5.2 162.2 %copy-start.39 = (f32[2,192]{1,0:T(2,128)S(1)}, f32[2,192]{1,0:T(2,128)}, u32[]{:S(2)}) copy-start(f32[2,192]{1,0:T(2,128)} %param.34) | copy-start | bytes 4612
  5.2 162.3 %copy-start.34 = (f32[768]{0:T(1024)S(1)}, f32[768]{0:T(1024)}, u32[]{:S(2)}) copy-start(f32[768]{0:T(1024)} %param.40) | copy-start | bytes 9220
  5.3 162.3 %copy-start.38 = (f32[512]{0:T(512)S(1)}, f32[512]{0:T(512)}, u32[]{:S(2)}) copy-start(f32[512]{0:T(512)} %param.54) | copy-start | bytes 6148
  5.3 162.3 %copy-start.43 = (f32[2,128]{1,0:T(2,128)S(1)}, f32[2,128]{1,0:T(2,128)}, u32[]{:S(2)}) copy-start(f32[2,128]{1,0:T(2,128)} %param.48) | copy-start | bytes 3076
  5.3 175.7 %copy-start.6 = (bf16[529,768]{1,0:T(8,128)(2,1)S(1)}, bf16[529,768]{1,0:T(8,128)(2,1)}, u32[]{:S(2)}) copy-start(bf16[529,768]{1,0:T(8,128)(2,1)} %param.29) | copy-start | bytes 2437636
  5.3 176.3 %copy-start.36 = (f32[768]{0:T(1024)S(1)}, f32[768]{0:T(1024)}, u32[]{:S(2)}) copy-start(f32[768]{0:T(1024)} %param.31) | copy-start | bytes 9220
  5.3 176.3 %copy-start.50 = (f32[768]{0:T(1024)S(1)}, f32[768]{0:T(1024)}, u32[]{:S(2)}) copy-start(f32[768]{0:T(1024)} %param.32) | copy-start | bytes 9220
  181.6 6.1 %copy-start.32 = (f32[544]{0:T(1024)}, f32[544]{0:T(1024)S(1)}, u32[]{:S(2)}) copy-start(f32[544]{0:T(1024)S(1)} %fusion.60) | copy-start | bytes 6532
  181.6 6.1 %copy-start.55 = (s32[4]{0:T(128)S(1)}, s32[4]{0:T(128)}, u32[]{:S(2)}) copy-start(s32[4]{0:T(128)} %param.30) | copy-start | bytes 52
  187.7 14.4 %copy-start.47 = (f32[768]{0:T(1024)S(1)}, f32[768]{0:T(1024)}, u32[]{:S(2)}) copy-start(f32[768]{0:T(1024)} %param.36) | copy-start | bytes 9220
  188.3 17.4 %slice-start = ((s8[4718592]{0:T(1024)(128)(4,1)}), s8[524288]{0:T(1024)(128)(4,1)S(1)}, s32[]{:S(2)}) async-start(s8[4718592]{0:T(1024)(128)(4,1)} %bitcast.435), calls=%async_computation | async-start | bytes 1048576
  202.1 3.6 copy-start.35
  202.1 3.6 slice-start.1
  202.1 3.6 copy-start.49
  202.1 21.8 %slice-start.4 = ((s8[4718592]{0:T(1024)(128)(4,1)}), s8[4194304]{0:T(1024)(128)(4,1)S(1)}, s32[]{:S(2)}) async-start(s8[4718592]{0:T(1024)(128)(4,1)} %bitcast.439), calls=%async_computation.4 | async-start | bytes 8388608
  205.3 18.6 %copy-start.11 = (f32[544,768]{1,0:T(8,128)}, f32[544,768]{1,0:T(8,128)S(1)}, u32[]{:S(2)}) copy-start(f32[544,768]{1,0:T(8,128)S(1)} %get-tuple-element.266) | copy-start | bytes 5013508
  205.7 18.2 %slice-start.5 = ((s8[4718592]{0:T(1024)(128)(4,1)}), s8[524288]{0:T(1024)(128)(4,1)S(1)}, s32[]{:S(2)}) async-start(s8[4718592]{0:T(1024)(128)(4,1)} %bitcast.439), calls=%async_computation.5 | async-start | bytes 1048576
  205.7 18.2 %copy-start.48 = (f32[768]{0:T(1024)S(1)}, f32[768]{0:T(1024)}, u32[]{:S(2)}) copy-start(f32[768]{0:T(1024)} %param.42) | copy-start | bytes 9220
  223.9 2.8 copy-start.61
  223.9 2.8 copy-start.52
  227.5 20.5 %copy-start.3 = (f32[544,512]{1,0:T(8,128)}, f32[544,512]{1,0:T(8,128)S(1)}, u32[]{:S(2)}) copy-start(f32[544,512]{1,0:T(8,128)S(1)} %get-tuple-element.269) | copy-start | bytes 3342340
  229.0 18.9 %copy-start.40 = (f32[512]{0:T(512)S(1)}, f32[512]{0:T(512)}, u32[]{:S(2)}) copy-start(f32[512]{0:T(512)} %param.50) | copy-start | bytes 6148
  250.3 11.9 %copy-start.21 = (bf16[529,512]{1,0:T(8,128)(2,1)S(1)}, bf16[529,512]{1,0:T(8,128)(2,1)}, u32[]{:S(2)}) copy-start(bf16[529,512]{1,0:T(8,128)(2,1)} %param.57) | copy-start | bytes 1625092
  250.3 11.9 %copy-start.44 = (bf16[4,512,512]{2,1,0:T(8,128)(2,1)S(1)}, bf16[4,512,512]{2,1,0:T(8,128)(2,1)}, u32[]{:S(2)}) copy-start(bf16[4,512,512]{2,1,0:T(8,128)(2,1)} %get-tuple-element.52) | copy-start | bytes 6291460
  298.1 3.7 copy-start.4
  302.3 11.2 %slice-start.2 = ((s8[4718592]{0:T(1024)(128)(4,1)}), s8[4194304]{0:T(1024)(128)(4,1)S(1)}, s32[]{:S(2)}) async-start(s8[4718592]{0:T(1024)(128)(4,1)} %bitcast.437), calls=%async_computation.2 | async-start | bytes 8388608
  303.3 14.1 %copy-start.9 = (f32[544,768]{1,0:T(8,128)}, f32[544,768]{1,0:T(8,128)S(1)}, u32[]{:S(2)}) copy-start(f32[544,768]{1,0:T(8,128)S(1)} %fusion.139) | copy-start | bytes 5013508
  303.5 10.0 %copy-start.12 = (f32[544,768]{1,0:T(8,128)S(1)}, f32[544,768]{1,0:T(8,128)}, u32[]{:S(2)}) copy-start(f32[544,768]{1,0:T(8,128)} %copy-done.11) | copy-start | bytes 5013508
  303.5 10.0 %slice-start.3 = ((s8[4718592]{0:T(1024)(128)(4,1)}), s8[524288]{0:T(1024)(128)(4,1)S(1)}, s32[]{:S(2)}) async-start(s8[4718592]{0:T(1024)(128)(4,1)} %bitcast.437), calls=%async_computation.3 | async-start | bytes 1048576
  313.5 3.2 copy-start.62
  323.7 18.6 %copy-start.7 = (bf16[529,768]{1,0:T(8,128)(2,1)S(1)}, bf16[529,768]{1,0:T(8,128)(2,1)}, u32[]{:S(2)}) copy-start(bf16[529,768]{1,0:T(8,128)(2,1)} %param.29) | copy-start | bytes 2437636
  349.2 5.9 %copy-start.20 = (bf16[544,512]{1,0:T(8,128)(2,1)S(1)}, bf16[544,512]{1,0:T(8,128)(2,1)}, u32[]{:S(2)}) copy-start(bf16[544,512]{1,0:T(8,128)(2,1)} %copy-done.19) | copy-start | bytes 1671172
  359.0 3.4 copy-start.5
  359.0 3.4 copy-start.8
  365.0 2.8 copy-start.18
  370.5 3.1 copy-start.10
  373.6 7.7 %copy-start.13 = (f32[544,768]{1,0:T(8,128)S(1)}, f32[544,768]{1,0:T(8,128)}, u32[]{:S(2)}) copy-start(f32[544,768]{1,0:T(8,128)} %copy-done.11) | copy-start | bytes 5013508
  373.6 7.7 %copy-start.63 = (bf16[4,544,768]{2,1,0:T(8,128)(2,1)S(1)}, bf16[4,544,768]{2,1,0:T(8,128)(2,1)}, u32[]{:S(2)}) copy-start(bf16[4,544,768]{2,1,0:T(8,128)(2,1)} %copy-done.62) | copy-start | bytes 10027012
  381.3 6.2 %copy-start.2 = (bf16[4,544,576]{2,1,0:T(8,128)(2,1)S(1)}, bf16[4,544,576]{2,1,0:T(8,128)(2,1)}, u32[]{:S(2)}) copy-start(bf16[4,544,576]{2,1,0:T(8,128)(2,1)} %attention_backward.3) | copy-start | bytes 7520260
  381.3 6.2 %copy-start.51 = (f32[768]{0:T(1024)S(1)}, f32[768]{0:T(1024)}, u32[]{:S(2)}) copy-start(f32[768]{0:T(1024)} %param.32) | copy-start | bytes 9220
  404.8 6.1 %copy-start.22 = (bf16[529,512]{1,0:T(8,128)(2,1)S(1)}, bf16[529,512]{1,0:T(8,128)(2,1)}, u32[]{:S(2)}) copy-start(bf16[529,512]{1,0:T(8,128)(2,1)} %param.57) | copy-start | bytes 1625092
  404.8 6.1 %copy-start.57 = (bf16[4,544,512]{2,1,0:T(8,128)(2,1)S(1)}, bf16[4,544,512]{2,1,0:T(8,128)(2,1)}, u32[]{:S(2)}) copy-start(bf16[4,544,512]{2,1,0:T(8,128)(2,1)} %get-tuple-element.228) | copy-start | bytes 6684676
  521.1 9.5 %copy-start.31 = (f32[32,512]{1,0:T(8,128)S(1)}, f32[32,512]{1,0:T(8,128)}, u32[]{:S(2)}) copy-start(f32[32,512]{1,0:T(8,128)} %get-tuple-element.55) | copy-start | bytes 196612
  521.1 12.7 %copy-start.33 = (f32[544]{0:T(1024)S(1)}, f32[544]{0:T(1024)}, u32[]{:S(2)}) copy-start(f32[544]{0:T(1024)} %copy-done.32) | copy-start | bytes 6532
  533.8 3.5 copy-start.58
  538.1 5.2 copy-start.1
  539.5 3.2 copy-start.28
  (22 other events, 40.4 us)

commit v2 on v1

v2 whole, which is shorter than its diff:
```python
from functools import partial

import jax
import jax.numpy as jnp
from jax import lax
from jax.experimental import pallas as pl
from jax.experimental.pallas import tpu as pltpu
from jax.sharding import PartitionSpec as P

HEAD = 64
DHEAD = 32
EPSILON = 1e-06
MESH = pl.DeviceIdType.MESH
F32 = jnp.float32
BF16 = jnp.bfloat16
VMEM_BYTES = 60 * 1024 * 1024


def neighbours():
    dp, mp = lax.axis_index("dp"), lax.axis_index("mp")
    core, x, y = dp % 2, (dp // 2) % 2, dp // 4
    across_core = dp + 1 - 2 * core
    across_x = dp + 2 - 4 * x
    across_y = dp + 4 - 8 * y
    return dp, mp, core, x, y, across_core, across_x, across_y


def entry_barrier(parts):
    mp, across_core, across_x, across_y = parts
    dp = lax.axis_index("dp")
    barrier = pltpu.get_barrier_semaphore()
    planes = lax.axis_size("mp")
    for other in (across_core, across_x, across_y):
        pl.semaphore_signal(barrier, inc=1, device_id=(other, mp), device_id_type=MESH)
    for step in range(1, planes):
        pl.semaphore_signal(
            barrier, inc=1, device_id=(dp, (mp + step) % planes), device_id_type=MESH
        )
    pl.semaphore_wait(barrier, 3 + planes - 1)


def plane_order(mp, planes):
    if planes != 4:
        return [(mp + step) % planes for step in range(1, planes)]
    upper = mp // 2
    place = mp + upper * (3 - 2 * mp)
    return [o + upper * (3 - 2 * o) for o in (place + 1, 2 - 2 * place, 3)]


def gather_kernel(count, planes, *refs):
    shards, small = refs[:count], refs[count]
    wholes, smalls = refs[count + 1 : 2 * count + 1], refs[2 * count + 1]
    holds = refs[2 * count + 2 : 3 * count + 2]
    local_sem, send_sem, recv_sem = refs[3 * count + 2 :]
    dp, mp, core, x, y, across_core, across_x, across_y = neighbours()
    entry_barrier((mp, across_core, across_x, across_y))
    diag = across_x + across_y - dp
    shift = across_core - dp
    others = plane_order(mp, planes)
    A, X, Y, S, DY, DX, SX, SY, SDY, SDX = range(10)
    sends = []

    def send(src, dst, m, plane, kind, target, slot=None):
        copy = pltpu.make_async_remote_copy(
            src_ref=src,
            dst_ref=dst,
            send_sem=send_sem.at[m, plane if slot is None else slot, kind],
            recv_sem=recv_sem.at[m, plane, kind],
            device_id=target,
            device_id_type=MESH,
        )
        copy.start()
        sends.append(copy)

    def arrived(m, plane, kind, ref):
        pltpu.make_async_remote_copy(
            src_ref=ref,
            dst_ref=ref,
            send_sem=send_sem.at[m, plane, kind],
            recv_sem=recv_sem.at[m, plane, kind],
            device_id=(across_core, mp),
            device_id_type=MESH,
        ).wait_recv()

    def rows_of(m, owner, half=None):
        piece = shards[m].shape[0] // 8
        if half is None:
            return pl.ds(owner * piece, piece)
        return pl.ds(owner * piece + half * (piece // 2), piece // 2)

    def along_z(m, i):
        own, plane = rows_of(m, dp), others[i]
        send(shards[m].at[own], wholes[m].at[mp, own], m, mp, A, (dp, plane), plane)

    def to_plane(m, i):
        plane = others[i]
        piece = wholes[m].at[plane, rows_of(m, dp)]
        arrived(m, plane, A, piece)
        send(piece, piece, m, plane, X, (across_x, mp))
        send(piece, piece, m, plane, Y, (across_y, mp))
        send(piece, piece, m, plane, S, (across_core, mp))

    def to_corner(m, i):
        plane = others[i]
        piece = wholes[m].at[plane, rows_of(m, across_x)]
        half = wholes[m].at[plane, rows_of(m, across_x, 0)]
        arrived(m, plane, X, piece)
        send(half, half, m, plane, DY, (across_y, mp))
        send(piece, piece, m, plane, SX, (across_core, mp))
        piece = wholes[m].at[plane, rows_of(m, across_y)]
        half = wholes[m].at[plane, rows_of(m, across_y, 1)]
        arrived(m, plane, Y, piece)
        send(half, half, m, plane, DX, (across_x, mp))
        send(piece, piece, m, plane, SY, (across_core, mp))

    def to_core(m, i):
        plane = others[i]
        half = wholes[m].at[plane, rows_of(m, diag, 0)]
        arrived(m, plane, DY, half)
        send(half, half, m, plane, SDY, (across_core, mp))
        half = wholes[m].at[plane, rows_of(m, diag, 1)]
        arrived(m, plane, DX, half)
        send(half, half, m, plane, SDX, (across_core, mp))

    def whole(m, i):
        plane = others[i]
        arrived(m, plane, S, wholes[m].at[plane, rows_of(m, across_core)])
        arrived(m, plane, SX, wholes[m].at[plane, rows_of(m, across_x + shift)])
        arrived(m, plane, SY, wholes[m].at[plane, rows_of(m, across_y + shift)])
        arrived(m, plane, SDY, wholes[m].at[plane, rows_of(m, diag + shift, 0)])
        arrived(m, plane, SDX, wholes[m].at[plane, rows_of(m, diag + shift, 1)])

    for i in range(planes - 1):
        send(small, smalls.at[mp], count, mp, A, (dp, others[i]), others[i])
    own_small = pltpu.make_async_copy(small, smalls.at[mp], local_sem.at[count])
    own_small.start()
    held = []
    for m in range(count):
        copy = pltpu.make_async_copy(shards[m], holds[m], local_sem.at[m])
        copy.start()
        held.append(copy)
    units = [(m, i) for m in range(count) for i in range(planes - 1)]
    lag, ahead = 2, 6
    stages = (
        (0, along_z),
        (ahead, to_plane),
        (ahead + lag, to_corner),
        (ahead + 2 * lag, to_core),
        (ahead + 3 * lag, whole),
    )
    for tick in range(len(units) + ahead + 3 * lag):
        if tick == ahead:
            for m in range(count):
                held[m].wait()
                held[m] = pltpu.make_async_copy(holds[m], wholes[m].at[mp], local_sem.at[m])
                held[m].start()
        for late, stage in stages:
            if 0 <= tick - late < len(units):
                stage(*units[tick - late])
    for i in range(planes - 1):
        arrived(count, others[i], A, smalls.at[others[i]])
    for copy in held + [own_small]:
        copy.wait()
    for copy in sends:
        copy.wait_send()


def gather_weights(shards, small, planes):
    count = len(shards)
    kinds = 10
    everything = list(shards) + [small]
    return pl.pallas_call(
        partial(gather_kernel, count, planes),
        out_shape=[jax.ShapeDtypeStruct((planes,) + s.shape, s.dtype) for s in everything],
        in_specs=[pl.BlockSpec(memory_space=pl.ANY)] * (count + 1),
        out_specs=[pl.BlockSpec(memory_space=pl.ANY)] * (count + 1),
        scratch_shapes=[pltpu.VMEM(s.shape, s.dtype) for s in shards]
        + [
            pltpu.SemaphoreType.DMA((count + 1,)),
            pltpu.SemaphoreType.DMA((count + 1, planes, kinds)),
            pltpu.SemaphoreType.DMA((count + 1, planes, kinds)),
        ],
        compiler_params=pltpu.CompilerParams(
            collective_id=0, has_side_effects=True, vmem_limit_bytes=VMEM_BYTES
        ),
        name="gather_weights",
    )(*everything)


class Reducer:
    def __init__(self, shapes, planes, refs):
        self.planes, self.count = planes, len(shapes)
        refs = list(refs)
        take = lambda: [refs.pop(0) for _ in range(self.count)]
        self.mine, self.from_core, self.from_x, self.from_y = take(), take(), take(), take()
        self.then_y, self.then_x, self.from_z = take(), take(), take()
        self.local_sem, self.send_sem, self.recv_sem = refs
        self.dp, self.mp, self.core_id, self.x, self.y, *across = neighbours()
        self.across_core, self.across_x, self.across_y = across
        self.halves = [rows // 2 for rows, columns in shapes]
        self.parts = [None] * self.count

    @staticmethod
    def scratch(shapes, planes, resident=()):
        count = len(shapes)

        def buffers(*lead, halves=False, skip=()):
            return [
                pltpu.VMEM((1, 16, 128), BF16)
                if m in skip
                else pltpu.VMEM(lead + (r // 2 if halves else r, c), BF16)
                for m, (r, c) in enumerate(shapes)
            ]

        return (
            buffers(planes, 2, 2, skip=resident)
            + buffers(planes, 2, 2)
            + buffers(planes, 2, halves=True)
            + buffers(planes, 2, halves=True)
            + buffers(planes, halves=True)
            + buffers(planes, halves=True)
            + buffers(planes)
            + [
                pltpu.SemaphoreType.DMA((count, planes)),
                pltpu.SemaphoreType.DMA((count, planes, 6)),
                pltpu.SemaphoreType.DMA((count, planes, 6)),
            ]
        )

    def remote(self, m, p, kind, src, dst, target, recv_plane=None):
        return pltpu.make_async_remote_copy(
            src_ref=src,
            dst_ref=dst,
            send_sem=self.send_sem.at[m, p, kind],
            recv_sem=self.recv_sem.at[m, p if recv_plane is None else recv_plane, kind],
            device_id=target,
            device_id_type=MESH,
        )

    def own(self, m, p, b, a):
        if self.resident(m):
            return self.parts[m].at[p, b, a, self.core_id]
        return self.mine[m].at[p, b, a]

    def owned(self, m, p, b, a, rows):
        if self.resident(m):
            return self.parts[m].at[p, b, a, self.core_id, rows]
        return self.mine[m].at[p, b, a, rows]

    def resident(self, m):
        return self.mine[m].shape[0] == 1

    def begin(self, m, p):
        if not self.resident(m):
            pltpu.make_async_copy(
                self.parts[m].at[p, :, :, self.core_id], self.mine[m].at[p], self.local_sem.at[m, p]
            ).start()
        self.to_core(m, p).start()

    def to_core(self, m, p):
        return self.remote(
            m,
            p,
            0,
            self.parts[m].at[p, :, :, 1 - self.core_id],
            self.from_core[m].at[p],
            (self.across_core, self.mp),
        )

    def to_x(self, m, p):
        src = self.owned(m, p, slice(None), 1 - self.x, pl.ds(0, self.halves[m]))
        return self.remote(m, p, 1, src, self.from_x[m].at[p], (self.across_x, self.mp))

    def to_y(self, m, p):
        half = self.halves[m]
        src = self.owned(m, p, 1 - self.y, slice(None), pl.ds(half, half))
        return self.remote(m, p, 2, src, self.from_y[m].at[p], (self.across_y, self.mp))

    def x_to_y(self, m, p):
        src = self.owned(m, p, 1 - self.y, self.x, pl.ds(0, self.halves[m]))
        return self.remote(m, p, 3, src, self.then_y[m].at[p], (self.across_y, self.mp))

    def y_to_x(self, m, p):
        half = self.halves[m]
        src = self.owned(m, p, self.y, 1 - self.x, pl.ds(half, half))
        return self.remote(m, p, 4, src, self.then_x[m].at[p], (self.across_x, self.mp))

    def to_z(self, m, p):
        src = self.own(m, p, self.y, self.x)
        return self.remote(m, p, 5, src, self.from_z[m].at[self.mp], (self.dp, p), self.mp)

    def core(self, m, p):
        if not self.resident(m):
            pltpu.make_async_copy(
                self.parts[m].at[p, :, :, self.core_id], self.mine[m].at[p], self.local_sem.at[m, p]
            ).wait()
        self.to_core(m, p).wait_recv()
        for b in range(2):
            for a in range(2):
                ref = self.own(m, p, b, a)
                ref[...] = ref[...] + self.from_core[m][p, b, a]
        self.to_x(m, p).start()
        self.to_y(m, p).start()

    def plane(self, m, p):
        half = self.halves[m]
        self.to_x(m, p).wait_recv()
        for b in range(2):
            ref = self.owned(m, p, b, self.x, pl.ds(0, half))
            ref[...] = ref[...] + self.from_x[m][p, b]
        self.x_to_y(m, p).start()
        self.to_y(m, p).wait_recv()
        for a in range(2):
            ref = self.owned(m, p, self.y, a, pl.ds(half, half))
            ref[...] = ref[...] + self.from_y[m][p, a]
        self.y_to_x(m, p).start()

    def corner(self, m, p):
        half = self.halves[m]
        self.x_to_y(m, p).wait_recv()
        self.y_to_x(m, p).wait_recv()
        ref = self.owned(m, p, self.y, self.x, pl.ds(0, half))
        ref[...] = ref[...] + self.then_y[m][p]
        ref = self.owned(m, p, self.y, self.x, pl.ds(half, half))
        ref[...] = ref[...] + self.then_x[m][p]

        @pl.when(p != self.mp)
        def _():
            self.to_z(m, p).start()

    def finish(self, m, out):
        total = self.own(m, self.mp, self.y, self.x)[...].astype(F32)
        for step in range(1, self.planes):
            plane = (self.mp + step) % self.planes
            src = self.from_z[m].at[plane]
            self.remote(m, plane, 5, src, src, (self.dp, plane)).wait_recv()
            total = total + src[...].astype(F32)
        out[...] = total

    def drain(self):
        @pl.loop(0, self.planes)
        def _(p):
            for m in range(self.count):
                for copy in (self.to_core, self.to_x, self.to_y, self.x_to_y, self.y_to_x):
                    copy(m, p).wait_send()

                @pl.when(p != self.mp)
                def _():
                    self.to_z(m, p).wait_send()


def spread(shards, small, sizes):
    planes = sizes["mp"]
    if sizes["dp"] == 8:
        lines = -(-small.shape[0] // 1024) * 8
        small = jnp.pad(small, (0, lines * 128 - small.shape[0])).reshape(lines, 128)
        return gather_weights(shards, small, planes)
    return [lax.all_gather(s, "mp", axis=0) for s in shards + (small,)]


def collect(part, sizes):
    part = lax.psum_scatter(part, "mp", scatter_dimension=0, tiled=False)
    return lax.psum_scatter(part.astype(F32), "dp", scatter_dimension=0, tiled=False)


LOG2E = 1.4426950408889634
ROW_BLOCK = 32
NT = (((1,), (1,)), ((), ()))


def dot(left, right, dims=(((1,), (0,)), ((), ()))):
    return lax.dot_general(left, right, dims, preferred_element_type=F32)


def standardize(x):
    centered = x - jnp.mean(x, -1, keepdims=True)
    scale = lax.rsqrt(jnp.mean(centered * centered, -1, keepdims=True) + EPSILON)
    return centered * scale, scale


def gelu_and_slope(b):
    cdf = 0.5 * (1.0 + lax.erf(b * 0.7071067811865476))
    density = jnp.exp(-0.5 * b * b) * 0.3989422804014327
    return b * cdf, cdf + b * density


def fold_rows(x):
    return jnp.sum(x.reshape(x.shape[0] // 8, 8, x.shape[1]), 0)


def row_blocks(rows):
    return pl.loop(0, rows // ROW_BLOCK)


def block_at(i):
    return pl.ds(pl.multiple_of(i * ROW_BLOCK, ROW_BLOCK), ROW_BLOCK)


def strip_forward(head_dim, length, p, triple, attended, logsum):
    rows, width = triple.shape[1], triple.shape[2] // 3
    visible = lax.broadcasted_iota(jnp.int32, (rows, 1), 0) < length
    factor = head_dim**-0.5 * LOG2E
    outs = []
    for head in range(width // head_dim):
        low = head * head_dim
        query = triple[p, :, low : low + head_dim]
        key = triple[p, :, width + low : width + low + head_dim]
        value = triple[p, :, 2 * width + low : 2 * width + low + head_dim]
        scores = jnp.where(visible, dot(key, query, NT) * factor, -1e30)
        ceiling = jnp.max(scores, 0, keepdims=True)
        exponent = jnp.exp2(scores - ceiling)
        denominator = jnp.sum(exponent, 0, keepdims=True)
        outs.append(dot(value.T, exponent.astype(BF16)) * (1.0 / denominator))
        logsum[p, head : head + 1, :] = ceiling + jnp.log2(denominator)
    attended[p] = jnp.concatenate(outs, 0).T.astype(BF16)


def strip_backward(head_dim, length, p, triple, attended, mixed, logsum, out):
    rows, width = triple.shape[1], triple.shape[2] // 3
    visible = lax.broadcasted_iota(jnp.int32, (rows, 1), 0) < length
    factor = head_dim**-0.5
    products = (mixed.astype(F32) * attended[p].astype(F32)).T
    query_grads = []
    for head in range(width // head_dim):
        low = head * head_dim
        query = triple[p, :, low : low + head_dim]
        key = triple[p, :, width + low : width + low + head_dim]
        value = triple[p, :, 2 * width + low : 2 * width + low + head_dim]
        mixed_head = mixed[:, low : low + head_dim]
        row_sums = jnp.sum(products[low : low + head_dim], 0, keepdims=True)
        scores = dot(key, query, NT) * (factor * LOG2E) - logsum[p, head : head + 1, :]
        chances = jnp.exp2(jnp.where(visible, scores, -1e30))
        chance_grad = dot(value, mixed_head, NT)
        score_grad = (chances * (chance_grad - row_sums)).astype(BF16)
        key_grad = dot(score_grad, query) * factor
        value_grad = dot(chances.astype(BF16), mixed_head)
        query_grads.append(dot(key.T, score_grad) * factor)
        out[:, width + low : width + low + head_dim] = key_grad.astype(BF16)
        out[:, 2 * width + low : 2 * width + low + head_dim] = value_grad.astype(BF16)
    out[:, :width] = jnp.concatenate(query_grads, 0).T.astype(BF16)


def attn_forward(head_dim, length, stream, weight, gain, shift, bias, out_bias, outs):
    normed, triple, attended, logsum, middle = outs
    planes, rows = triple.shape[:2]
    width = attended.shape[2]

    @row_blocks(rows)
    def _(i):
        x = stream[block_at(i), :].astype(F32)
        normed[block_at(i), :] = (standardize(x)[0] * gain[...] + shift[...]).astype(BF16)
        middle[block_at(i), :] = x + out_bias[...]

    @pl.loop(0, planes)
    def _(p):
        triple[p] = (dot(normed[...], weight[p, :, : 3 * width]) + bias[p]).astype(BF16)
        strip_forward(head_dim, length, p, triple, attended, logsum)
        middle[...] += dot(attended[p], weight[p, :, 3 * width :], NT)


def feed_forward(middle, up, down, up_bias, gain, shift, down_bias, outs, total):
    feed_input, hidden, slope = outs
    planes, rows, width = hidden.shape

    @row_blocks(rows)
    def _(i):
        x = middle[block_at(i), :]
        feed_input[block_at(i), :] = (standardize(x)[0] * gain[...] + shift[...]).astype(BF16)
        total[block_at(i), :] = x + down_bias[...]

    @pl.loop(0, planes)
    def _(p):
        for low in range(0, width, 256):
            part = slice(low, low + 256)
            before = dot(feed_input[...], up[p, :, part]) + up_bias[p, :, part]
            activated, rise = gelu_and_slope(before)
            hidden[p, :, part] = activated.astype(BF16)
            slope[p, :, part] = rise.astype(BF16)
        total[...] += dot(hidden[p], down[p])


def layer_backward(stream, gain, upstream, spare, gain_sums, shift_sums):
    gain_sums[...] = jnp.zeros_like(gain_sums)
    shift_sums[...] = jnp.zeros_like(shift_sums)

    @row_blocks(stream.shape[0])
    def _(i):
        hat, scale = standardize(stream[block_at(i), :].astype(F32))
        grad = spare[block_at(i), :]
        gain_sums[...] += fold_rows(grad * hat)
        shift_sums[...] += fold_rows(grad)
        grad = grad * gain[...]
        part = grad - jnp.mean(grad, -1, keepdims=True)
        part = part - hat * jnp.mean(grad * hat, -1, keepdims=True)
        spare[block_at(i), :] = upstream[block_at(i), :].astype(F32) + part * scale


def put_transposed(values, turned):
    columns = values.shape[1]
    turned[:columns, :] = values.T
    turned[columns:, :] = jnp.ones((16, values.shape[0]), BF16)


def feed_backward(upstream, saved, weights, gain, outs, scratch, hook):
    hidden, slope, feed_input, middle = saved
    up, down = weights
    down_grad, up_grad, up_sums, middle_grad, branch_sums, gain_sums, shift_sums = outs
    branch, branch_turned, feed_turned = scratch
    planes, rows, width = hidden.ref.shape
    wide = branch.shape[1]
    branch_sums[...] = jnp.zeros_like(branch_sums)
    upstream = upstream.use()
    total = middle_grad.ref

    @row_blocks(rows)
    def _(i):
        rounded = upstream[block_at(i), :].astype(BF16)
        branch[block_at(i), :] = rounded
        branch_sums[...] += fold_rows(rounded.astype(F32))
        total[block_at(i), :] = jnp.zeros((ROW_BLOCK, wide), F32)

    branch_turned[...] = branch[...].T
    put_transposed(feed_input.use()[...], feed_turned)
    hidden, slope, up, down = hidden.use(), slope.use(), up.use(), down.use()

    @pl.loop(0, planes)
    def _(p):
        down_grad.ref[p] = dot(branch_turned[...], hidden[p]).astype(BF16)
        down_grad.flush(p)
        hidden_grad = dot(branch[...], down[p], NT)
        before_grad = (hidden_grad * slope[p].astype(F32)).astype(BF16)
        both = dot(feed_turned[...], before_grad)
        up_grad.ref[p] = both[:wide].astype(BF16)
        up_grad.flush(p)
        up_sums[p] = both[wide : wide + 8]
        total[...] += dot(before_grad, up[p], NT)
        hook(p)

    layer_backward(middle.use(), gain, upstream, total, gain_sums, shift_sums)
    middle_grad.flush()


def attn_backward(head_dim, length, middle_grad, saved, weight, gain, put, outs, scratch, hook):
    attended, triple, logsum, normed, stream = saved
    head_sums, input_grad, branch_sums, gain_sums, shift_sums = outs
    branch, branch_turned, normed_turned, triple_grad, total = scratch
    planes, rows, width = attended.ref.shape
    wide = branch.shape[1]
    branch_sums[...] = jnp.zeros_like(branch_sums)
    middle_grad = middle_grad.use()

    @row_blocks(rows)
    def _(i):
        rounded = middle_grad[block_at(i), :].astype(BF16)
        branch[block_at(i), :] = rounded
        branch_sums[...] += fold_rows(rounded.astype(F32))
        total[block_at(i), :] = jnp.zeros((ROW_BLOCK, wide), F32)

    branch_turned[...] = branch[...].T
    put_transposed(normed.use()[...], normed_turned)
    attended, triple, logsum, weight = attended.use(), triple.use(), logsum.use(), weight.use()

    @pl.loop(0, planes)
    def _(p):
        mixed = dot(branch[...], weight[p, :, 3 * width :]).astype(BF16)
        strip_backward(head_dim, length, p, triple, attended, mixed, logsum, triple_grad)
        both = dot(normed_turned[...], triple_grad[...])
        out_grad = dot(branch_turned[...], attended[p])
        put(p, jnp.concatenate([both[:wide].astype(BF16), out_grad.astype(BF16)], -1))
        head_sums[p] = both[wide : wide + 8]
        total[...] += dot(triple_grad[...], weight[p, :, : 3 * width], NT)
        hook(p)

    layer_backward(stream.use(), gain, middle_grad, total, gain_sums, shift_sums)

    @row_blocks(rows)
    def _(i):
        input_grad.ref[block_at(i), :] = total[block_at(i), :].astype(BF16)

    input_grad.flush()


IN_VMEM = pl.BlockSpec(memory_space=pltpu.VMEM)
IN_SMEM = pl.BlockSpec(memory_space=pltpu.SMEM)


def whole_call(kernel, name, ins, outs, scratch=()):
    return pl.pallas_call(
        kernel,
        out_shape=[jax.ShapeDtypeStruct(shape, dtype) for shape, dtype in outs],
        in_specs=[IN_SMEM if v.dtype == jnp.int32 else IN_VMEM for v in ins],
        out_specs=[IN_VMEM] * len(outs),
        scratch_shapes=list(scratch),
        compiler_params=pltpu.CompilerParams(vmem_limit_bytes=VMEM_BYTES),
        name=name,
    )(*ins)


class Load:
    def __init__(self, source, ref, sem):
        self.ref, self.copy, self.waits = ref, pltpu.make_async_copy(source, ref, sem), True
        self.copy.start()

    def use(self):
        if self.waits:
            self.copy.wait()
            self.waits = False
        return self.ref


class Store:
    def __init__(self, ref, target, sems):
        self.ref, self.target, self.sems, self.by_plane = ref, target, sems, False

    def flush(self, p=None):
        if p is None:
            pltpu.make_async_copy(self.ref, self.target, self.sems.at[0]).start()
        else:
            self.by_plane = True
            pltpu.make_async_copy(self.ref.at[p], self.target.at[p], self.sems.at[p]).start()

    def finish(self):
        if not self.by_plane:
            pltpu.make_async_copy(self.ref, self.target, self.sems.at[0]).wait()
            return
        for p in range(self.ref.shape[0]):
            pltpu.make_async_copy(self.ref.at[p], self.target.at[p], self.sems.at[p]).wait()


def staged_call(name, body, ins, outs, scratch=(), collective_id=None):
    any_spec = pl.BlockSpec(memory_space=pl.ANY)
    near = lambda v: IN_SMEM if v.dtype == jnp.int32 else IN_VMEM
    loads = [v for mode, v in ins if mode == "load"]
    stores = [(shape, dtype) for mode, shape, dtype in outs if mode == "store"]
    scratch = list(scratch)

    def kernel(*refs):
        refs = list(refs)
        take = lambda n: [refs.pop(0) for _ in range(n)]
        in_refs, out_refs = take(len(ins)), take(len(outs))
        load_refs, store_refs, rest = take(len(loads)), take(len(stores)), take(len(scratch))
        load_sem, store_sem = refs
        given, load_at = [], 0
        for (mode, _), ref in zip(ins, in_refs):
            if mode == "load":
                given.append(Load(ref, load_refs[load_at], load_sem.at[load_at]))
                load_at += 1
            else:
                given.append(ref)
        results, store_at = [], 0
        for (mode, _, _), ref in zip(outs, out_refs):
            if mode == "store":
                results.append(Store(store_refs[store_at], ref, store_sem.at[store_at]))
                store_at += 1
            else:
                results.append(ref)
        body(given, results, rest)
        for item in given:
            if isinstance(item, Load):
                item.use()
        for item in results:
            if isinstance(item, Store):
                item.finish()

    params = {"vmem_limit_bytes": VMEM_BYTES}
    if collective_id is not None:
        params.update(collective_id=collective_id, has_side_effects=True)
    return pl.pallas_call(
        kernel,
        out_shape=[jax.ShapeDtypeStruct(shape, dtype) for _, shape, dtype in outs],
        in_specs=[near(v) if mode == "near" else any_spec for mode, v in ins],
        out_specs=[any_spec if mode == "store" else IN_VMEM for mode, _, _ in outs],
        scratch_shapes=[pltpu.VMEM(v.shape, v.dtype) for v in loads]
        + [pltpu.VMEM(shape, dtype) for shape, dtype in stores]
        + scratch
        + [pltpu.SemaphoreType.DMA((max(len(loads), 1),))]
        + [pltpu.SemaphoreType.DMA((max(len(stores), 1), 4))],
        compiler_params=pltpu.CompilerParams(**params),
        name=name,
    )(*[v for _, v in ins])


def run_attn_forward(stream, weight, params, length, head_dim):
    gain, shift, bias, out_bias = params
    planes, wide, width = weight.shape
    width //= 4
    rows = stream.shape[0]

    def kernel(length, stream, weight, gain, shift, bias, out_bias, *outs):
        attn_forward(head_dim, length[0], stream, weight, gain, shift, bias, out_bias, outs)

    return whole_call(
        kernel,
        "attn_forward",
        (length, stream, weight, gain, shift, bias, out_bias),
        (
            ((rows, wide), BF16),
            ((planes, rows, 3 * width), BF16),
            ((planes, rows, width), BF16),
            ((planes, width // head_dim, rows), F32),
            ((rows, wide), F32),
        ),
    )


def run_feed_forward(middle, up, down, params, bridge=None):
    up_bias, gain, shift, down_bias = params
    planes, wide, width = up.shape
    rows = middle.shape[0]
    saved = (
        ((rows, wide), BF16),
        ((planes, rows, width), BF16),
        ((planes, rows, width), BF16),
        ((rows, wide), BF16),
    )
    ins = (middle, up, down, up_bias, gain, shift, down_bias)
    scratch = [pltpu.VMEM((rows, wide), F32)]
    if bridge is None:

        def kernel(*refs):
            outs, result, total = refs[7:10], refs[10], refs[11]
            feed_forward(*refs[:7], outs, total)
            result[...] = total[...].astype(BF16)

        return whole_call(kernel, "feed_forward", ins, saved, scratch)

    def kernel_bridge(*refs):
        weight, bias = refs[7:9]
        outs, result, bridged, total = refs[9:12], refs[12], refs[13], refs[14]
        feed_forward(*refs[:7], outs, total)
        result[...] = total[...].astype(BF16)
        bridged[...] = dot(result[...], weight[...]) + bias[...]

    outs = saved + (((rows, bridge[0].shape[1]), F32),)
    return whole_call(kernel_bridge, "feed_forward", ins + tuple(bridge), outs, scratch)


def nothing(p):
    pass


def at_planes(schedule):
    def hook(p):
        for k, work in enumerate(schedule):

            @pl.when(p == k)
            def _():
                for step in work:
                    step()

    return hook


def six_deep(grad):
    planes, rows, columns = grad.shape
    return grad.reshape(planes, 2, 2, 2, rows // 8, columns)


def even_schedule(reducer, matrices):
    every = lambda step, ps: [partial(step, m, p) for p in ps for m in matrices]
    return [
        every(reducer.core, (0, 1)),
        every(reducer.core, (2, 3)) + every(reducer.plane, (0, 1)),
        every(reducer.plane, (2, 3)) + every(reducer.corner, (0, 1)),
        every(reducer.corner, (2, 3)),
    ]


def feed_scratch(rows, wide):
    return [
        pltpu.VMEM((rows, wide), BF16),
        pltpu.VMEM((wide, rows), BF16),
        pltpu.VMEM((wide + 16, rows), BF16),
    ]


def feed_outs(planes, rows, wide, width):
    return [
        ("store", (planes, wide, width), BF16),
        ("store", (planes, wide, width), BF16),
        ("near", (planes, 8, width), F32),
        ("store", (rows, wide), F32),
        ("near", (8, wide), F32),
        ("near", (8, wide), F32),
        ("near", (8, wide), F32),
    ]


def run_feed_backward(upstream, saved, weights, gain):
    hidden, slope, feed_input, middle = saved
    planes, rows, width = hidden.shape
    wide = feed_input.shape[1]

    def body(ins, outs, scratch):
        feed_backward(ins[0], ins[1:5], ins[5:7], ins[7], outs, scratch, nothing)

    return staged_call(
        "feed_backward",
        body,
        [("load", v) for v in (upstream,) + saved + weights] + [("near", gain)],
        feed_outs(planes, rows, wide, width),
        feed_scratch(rows, wide),
    )


def run_bridge_feed_backward(bridge, saved, weights, gain, partial_grad):
    hidden, slope, feed_input, middle = saved
    planes, rows, width = hidden.shape
    wide = feed_input.shape[1]
    grad_rows, bridge_input, bridge_weight = bridge
    narrow = grad_rows.shape[1]
    ins = [("load", v) for v in bridge + saved + weights] + [("near", gain)]
    scratch = feed_scratch(rows, wide) + [pltpu.VMEM((rows, wide), F32)]
    outs = feed_outs(planes, rows, wide, width) + [("near", (8, narrow), F32)]
    deep = wide // 8 // planes
    tall = -(-deep // 32) * 32

    def prologue(ins, scratch, sums):
        turned = scratch[2]
        put_transposed(ins[1].use()[...], turned)
        both = dot(turned[...], ins[0].use()[...])
        sums[...] = both[wide : wide + 8]
        scratch[3][...] = dot(ins[0].use()[...], ins[2].use()[...], NT)
        return both[:wide]

    class Ready:
        def __init__(self, ref):
            self.ref = ref

        def use(self):
            return self.ref

    if partial_grad is None:
        outs += [("near", (wide, narrow), F32)]

        def body(ins, outs, scratch):
            outs[8][...] = prologue(ins, scratch, outs[7])
            upstream = Ready(scratch[3])
            feed_backward(upstream, ins[3:7], ins[7:9], ins[9], outs[:7], scratch[:3], nothing)

        return staged_call("feed_backward", body, ins, outs, scratch)

    parts = six_deep(partial_grad)
    shapes = (parts.shape[4:], (tall, narrow))
    outs += [("near", shape, F32) for shape in shapes]
    scratch = scratch + [pltpu.VMEM((planes, 2, 2, 2, tall, narrow), BF16)]
    own = len(scratch)
    scratch = scratch + Reducer.scratch(shapes, planes, resident=(1,))

    def body(ins, outs, scratch):
        reducer = Reducer(shapes, planes, scratch[own:])
        entry_barrier((reducer.mp, reducer.across_core, reducer.across_x, reducer.across_y))
        reducer.parts = [ins[10], scratch[4]]
        for p in range(planes):
            reducer.begin(0, p)
        grad = prologue(ins, scratch, outs[7])
        for g in range(8):
            for p in range(planes):
                low = (g * planes + p) * deep
                block = jnp.concatenate(
                    [grad[low : low + deep], jnp.zeros((tall - deep, narrow), F32)], 0
                )
                scratch[4][p, g // 4, g // 2 % 2, g % 2] = block.astype(BF16)
        for p in range(planes):
            reducer.begin(1, p)
        upstream = Ready(scratch[3])
        hook = at_planes(even_schedule(reducer, (0, 1)))
        feed_backward(upstream, ins[3:7], ins[7:9], ins[9], outs[:7], scratch[:3], hook)
        reducer.finish(0, outs[8])
        reducer.finish(1, outs[9])
        reducer.drain()

    return staged_call("feed_backward_sums", body, ins + [("raw", parts)], outs, scratch, 2)


def attn_parts(planes, rows, wide, width):
    outs = [
        ("near", (planes, 8, 3 * width), F32),
        ("store", (rows, wide), BF16),
        ("near", (8, wide), F32),
        ("near", (8, wide), F32),
        ("near", (8, wide), F32),
    ]
    scratch = feed_scratch(rows, wide) + [
        pltpu.VMEM((rows, 3 * width), BF16),
        pltpu.VMEM((rows, wide), F32),
    ]
    return outs, scratch


def run_attn_backward(middle_grad, saved, weight, gain, length, head_dim, partial_grads=None):
    planes, rows, width = saved[0].shape
    wide = weight.shape[1]
    outs, scratch = attn_parts(planes, rows, wide, width)
    outs = outs + [("store", (planes, wide, 4 * width), BF16)]
    ins = [("near", length)] + [("load", v) for v in (middle_grad,) + saved + (weight,)]
    ins = ins + [("near", gain)]

    def compute(ins, outs, scratch, hook):
        def put(p, value):
            outs[5].ref[p] = value
            outs[5].flush(p)

        attn_backward(
            head_dim,
            ins[0][0],
            ins[1],
            ins[2:7],
            ins[7],
            ins[8],
            put,
            outs[:5],
            scratch[:5],
            hook,
        )

    if partial_grads is None:

        def body(ins, outs, scratch):
            compute(ins, outs, scratch, nothing)

        return staged_call("attn_backward", body, ins, outs, scratch)

    parts = [six_deep(g) for g in partial_grads]
    shapes = tuple(part.shape[4:] for part in parts)
    outs += [("near", shape, F32) for shape in shapes]
    scratch = scratch + Reducer.scratch(shapes, planes)

    def body(ins, outs, scratch):
        reducer = Reducer(shapes, planes, scratch[5:])
        entry_barrier((reducer.mp, reducer.across_core, reducer.across_x, reducer.across_y))
        reducer.parts = ins[9:11]
        for p in range(planes):
            for m in range(2):
                reducer.begin(m, p)
        compute(ins, outs, scratch, at_planes(even_schedule(reducer, (0, 1))))
        reducer.finish(0, outs[6])
        reducer.finish(1, outs[7])
        reducer.drain()

    ins = ins + [("raw", part) for part in parts]
    return staged_call("attn_backward_sums", body, ins, outs, scratch, 1)


class VectorSum:
    def __init__(self, refs):
        self.levels, self.came, self.from_z, self.send_sem, self.recv_sem = refs
        self.dp, self.mp, core, x, y, *across = neighbours()
        self.across = across

    @staticmethod
    def scratch(rows, columns, planes):
        return [
            pltpu.VMEM((4, rows, columns), F32),
            pltpu.VMEM((3, rows, columns), F32),
            pltpu.VMEM((planes, rows, columns), F32),
            pltpu.SemaphoreType.DMA((3 + planes,)),
            pltpu.SemaphoreType.DMA((3 + planes,)),
        ]

    def hop(self, level):
        return pltpu.make_async_remote_copy(
            src_ref=self.levels.at[level],
            dst_ref=self.came.at[level],
            send_sem=self.send_sem.at[level],
            recv_sem=self.recv_sem.at[level],
            device_id=(self.across[level], self.mp),
            device_id_type=MESH,
        )

    def along(self, plane, receiving=False):
        slot = plane if receiving else self.mp
        return pltpu.make_async_remote_copy(
            src_ref=self.levels.at[3],
            dst_ref=self.from_z.at[slot],
            send_sem=self.send_sem.at[3 + plane],
            recv_sem=self.recv_sem.at[3 + slot],
            device_id=(self.dp, plane),
            device_id_type=MESH,
        )

    def begin(self):
        self.hop(0).start()

    def others(self):
        planes = self.from_z.shape[0]
        return [(self.mp + step) % planes for step in range(1, planes)]

    def advance(self, level):
        self.hop(level).wait_recv()
        self.levels[level + 1] = self.levels[level] + self.came[level]
        if level < 2:
            self.hop(level + 1).start()
        else:
            for plane in self.others():
                self.along(plane).start()

    def finish(self, out):
        total = self.levels[3]
        for plane in self.others():
            self.along(plane, receiving=True).wait_recv()
            total = total + self.from_z[plane]
        out[...] = total
        for level in range(3):
            self.hop(level).wait_send()
        for plane in self.others():
            self.along(plane).wait_send()


def stack_rows(rows, columns):
    wide = [
        row
        if row.shape[1] == columns
        else jnp.concatenate([row, jnp.zeros((1, columns - row.shape[1]), F32)], -1)
        for row in rows
    ]
    spare = -len(wide) % 8
    if spare:
        wide.append(jnp.zeros((spare, columns), F32))
    return jnp.concatenate(wide, 0)


def folded(sums):
    return jnp.sum(sums[...], 0, keepdims=True)


def first_rows(sums):
    return [sums[p, 0:1] for p in range(sums.shape[0])]


def early_rows(feed_sums, dec_sums, bridge_sums):
    f_gain, f_shift, down_bias, up_bias = feed_sums
    rows = [folded(f_gain), folded(f_shift), folded(down_bias)] + first_rows(up_bias)
    gain, shift, out_bias, head, f_gain, f_shift, down_bias, up_bias = dec_sums
    rows += [folded(v) for v in (gain, shift, out_bias, f_gain, f_shift, down_bias)]
    return rows + first_rows(up_bias) + first_rows(head) + [bridge_sums[0:1]]


def late_rows(gain, shift, out_bias, head):
    return [folded(gain), folded(shift), folded(out_bias)] + first_rows(head)


def run_last_backward(
    middle_grad, saved, weight, gain, length, head_dim, partial_grads, feed_sums, dec_sums, bridge_sums
):
    planes, rows, width = saved[0].shape
    wide = weight.shape[1]
    outs, scratch = attn_parts(planes, rows, wide, width)
    outs = outs[1:2]
    parts = [six_deep(g) for g in partial_grads]
    shapes = tuple(part.shape[4:] for part in parts) + ((wide // 8, 4 * width),)
    early = -(-(3 + 6 + 3 * planes + 1) // 8) * 8
    late = -(-(3 + planes) // 8) * 8
    outs += [("near", shape, F32) for shape in shapes]
    outs += [("near", (early, wide), F32), ("near", (late, wide), F32)]
    sums_scratch = [
        pltpu.VMEM((planes, 8, 3 * width), F32),
        pltpu.VMEM((8, wide), F32),
        pltpu.VMEM((8, wide), F32),
        pltpu.VMEM((8, wide), F32),
    ]
    sizes = [5, 4, 1, 5, 5]
    groups = [
        scratch,
        sums_scratch,
        [pltpu.VMEM((planes, 2, 2, 2, wide // 8, 4 * width), BF16)],
        VectorSum.scratch(early, wide, planes),
        VectorSum.scratch(late, wide, planes),
        Reducer.scratch(shapes, planes, resident=(2,)),
    ]
    loads = (middle_grad,) + saved + (weight,)
    small = tuple(feed_sums) + tuple(dec_sums) + (bridge_sums,)
    ins = [("near", length)] + [("load", v) for v in loads] + [("near", gain)]
    ins += [("raw", part) for part in parts] + [("near", v) for v in small]

    def body(ins, outs, scratch):
        cuts, at = [], 0
        for size in sizes:
            cuts.append(scratch[at : at + size])
            at += size
        compute_scratch, sums, (grads,), early_refs, late_refs = cuts
        reducer = Reducer(shapes, planes, scratch[at:])
        early_sum, late_sum = VectorSum(early_refs), VectorSum(late_refs)
        entry_barrier((reducer.mp, reducer.across_core, reducer.across_x, reducer.across_y))
        reducer.parts = ins[9:11] + [grads]
        for p in range(planes):
            for m in range(2):
                reducer.begin(m, p)
        small = ins[11:]
        early_sum.levels[0] = stack_rows(early_rows(small[:4], small[4:12], small[12]), wide)
        early_sum.begin()

        def put(p, value):
            grads[p] = value.reshape(grads.shape[1:])
            reducer.begin(2, p)

        every = lambda step, ps: [partial(step, m, p) for p in ps for m in range(2)]
        schedule = [
            every(reducer.core, range(planes)) + [partial(early_sum.advance, 0)],
            every(reducer.plane, (0, 1)) + [partial(early_sum.advance, 1)],
            every(reducer.plane, (2, 3)) + every(reducer.corner, (0,)),
            every(reducer.corner, (1, 2)) + [partial(early_sum.advance, 2)],
        ]
        head_sums, branch_sums, gain_sums, shift_sums = sums
        attn_backward(
            head_dim,
            ins[0][0],
            ins[1],
            ins[2:7],
            ins[7],
            ins[8],
            put,
            (head_sums, outs[0], branch_sums, gain_sums, shift_sums),
            compute_scratch,
            at_planes(schedule),
        )
        for p in range(planes):
            reducer.core(2, p)
        late_sum.levels[0] = stack_rows(
            late_rows(gain_sums, shift_sums, branch_sums, head_sums), wide
        )
        late_sum.begin()
        for step in every(reducer.corner, (3,)):
            step()
        late_sum.advance(0)
        for p in range(planes):
            reducer.plane(2, p)
        late_sum.advance(1)
        for p in range(planes):
            reducer.corner(2, p)
        late_sum.advance(2)
        early_sum.finish(outs[4])
        for m in range(3):
            reducer.finish(m, outs[1 + m])
        late_sum.finish(outs[5])
        reducer.drain()

    return staged_call("attn_backward_last", body, ins, outs, sum(groups, []), 3)


def block_forward(stream, params, weights, length, head_dim, bridge=None):
    (gain, shift, head_bias, output_bias, feed_gain, feed_shift, up_bias, down_bias) = params
    attn, up, down = weights
    zeros = jnp.zeros_like(head_bias[0])
    bias = jnp.concatenate([head_bias[0], zeros, head_bias[1]], -1)[:, None]
    normed, triple, attended, logsum, middle = run_attn_forward(
        stream, attn, (gain[None], shift[None], bias, output_bias[None]), length, head_dim
    )
    feed_input, hidden, slope, *results = run_feed_forward(
        middle, up, down, (up_bias[:, None], feed_gain[None], feed_shift[None], down_bias[None]), bridge
    )
    return results, (
        (hidden, slope, feed_input, middle),
        (attended, triple, logsum, normed, stream),
    )


def shards(sizes, *inputs):
    patches, lengths = inputs[:2]
    cotangent = inputs[28]
    planes, groups = sizes["mp"], sizes["dp"]
    mp = lax.axis_index("mp")
    length = lax.dynamic_slice_in_dim(lengths, mp, 1)

    def block_of(at):
        (gain, shift, proj, head_bias, out, out_bias, f_gain, f_shift, up, up_bias, down, d_bias) = (
            inputs[at : at + 12]
        )
        packed = jnp.concatenate([proj[0], proj[1], proj[2], out.T], -1)
        vectors = (gain, shift, out_bias, f_gain, f_shift, d_bias)
        return (packed, up, down), vectors, (head_bias, up_bias)

    enc_shards, enc_vectors, enc_split = block_of(2)
    bridge_weight, bridge_bias = inputs[14:16]
    dec_shards, dec_vectors, dec_split = block_of(16)
    small = jnp.concatenate([v.reshape(-1) for v in enc_split + dec_split])
    *wholes, small = spread(enc_shards + dec_shards, small, sizes)
    small = small.reshape(planes, -1)

    def params_of(vectors, split, at):
        gain, shift, out_bias, f_gain, f_shift, d_bias = vectors
        width, hidden = split[0].shape[1], split[1].shape[0]
        head_bias = small[:, at : at + 2 * width].reshape(planes, 2, width).transpose(1, 0, 2)
        up_bias = small[:, at + 2 * width : at + 2 * width + hidden]
        return (gain, shift, head_bias, out_bias, f_gain, f_shift, up_bias, d_bias)

    encoder = params_of(enc_vectors, enc_split, 0)
    decoder = params_of(dec_vectors, dec_split, 2 * enc_split[0].shape[1] + enc_split[1].shape[0])

    rows = patches.shape[0]
    padded = -(-rows // 32) * 32
    stream = jnp.pad(patches, ((0, padded - rows), (0, 0)))
    upstream = jnp.pad(cotangent, ((0, padded - rows), (0, 0)))

    (bridge_input, bridged), enc_stored = block_forward(
        stream, encoder, wholes[:3], length, HEAD, (bridge_weight, bridge_bias[None])
    )
    (decoded,), dec_stored = block_forward(bridged, decoder, wholes[3:], length, DHEAD)
    fast = groups == 8 and planes == 4
    dec_attn, dec_up, dec_down = wholes[3:]
    enc_attn, enc_up, enc_down = wholes[:3]
    down_part, up_part, up_sums, middle_grad, down_sums, f_gain_sums, f_shift_sums = (
        run_feed_backward(upstream, dec_stored[0], (dec_up, dec_down), decoder[4][None])
    )
    head_sums, bridge_rows, out_sums, gain_sums, shift_sums, attn_part, *dec_sums = run_attn_backward(
        middle_grad,
        dec_stored[1],
        dec_attn,
        decoder[0][None],
        length,
        DHEAD,
        (down_part, up_part) if fast else None,
    )
    dec_vectors = (
        gain_sums,
        shift_sums,
        out_sums,
        head_sums,
        f_gain_sums,
        f_shift_sums,
        down_sums,
        up_sums,
    )
    dec_parts = (attn_part, up_part, down_part)
    down_part, up_part, up_sums, middle_grad, down_sums, f_gain_sums, f_shift_sums, *more = (
        run_bridge_feed_backward(
            (bridge_rows, bridge_input, bridge_weight),
            enc_stored[0],
            (enc_up, enc_down),
            encoder[4][None],
            attn_part if fast else None,
        )
    )
    bridge_sums, *more = more
    feed_vectors = (f_gain_sums, f_shift_sums, down_sums, up_sums)
    deep = bridge_weight.shape[0] // planes // groups
    if fast:
        dec_attn_sum, bridge_sum = more
        dec_grads = (dec_attn_sum, dec_sums[1], dec_sums[0])
        bridge_out = bridge_sum[:deep]
        patches_grad, down_sum, up_sum, attn_sum, early, late = run_last_backward(
            middle_grad,
            enc_stored[1],
            enc_attn,
            encoder[0][None],
            length,
            HEAD,
            (down_part, up_part),
            feed_vectors,
            dec_vectors,
            bridge_sums,
        )
        enc_grads = (attn_sum, up_sum, down_sum)
    else:
        head_sums, patches_grad, out_sums, gain_sums, shift_sums, attn_part = run_attn_backward(
            middle_grad, enc_stored[1], enc_attn, encoder[0][None], length, HEAD
        )
        wide = patches.shape[1]
        early = stack_rows(early_rows(feed_vectors, dec_vectors, bridge_sums), wide)
        late = stack_rows(late_rows(gain_sums, shift_sums, out_sums, head_sums), wide)
        early, late = lax.psum(early, ("dp", "mp")), lax.psum(late, ("dp", "mp"))

        def in_groups(grad):
            return collect(grad.reshape(planes, groups, -1, grad.shape[-1]), sizes)

        dec_grads = tuple(in_groups(g) for g in dec_parts)
        enc_grads = tuple(in_groups(g) for g in (attn_part, up_part, down_part))
        bridge_part = more[0].reshape(groups, planes, deep, -1).transpose(1, 0, 2, 3)
        bridge_out = collect(bridge_part, sizes)

    dp = lax.axis_index("dp")

    def shared(row):
        row = row[: patches.shape[1]]
        size = row.shape[0] // groups // planes
        return lax.dynamic_slice_in_dim(row, (dp * planes + mp) * size, size)

    def split(rows):
        size = rows.shape[1] // groups
        return lax.dynamic_slice(rows, (mp, dp * size), (1, size))[0]

    def block_out(mats, shared_rows, head, up_bias, wide):
        attn, up, down = mats
        width = attn.shape[1] // 4
        proj = attn[:, : 3 * width].reshape(-1, 3, width).transpose(1, 0, 2)
        gain, shift, out_bias, f_gain, f_shift, d_bias = (shared(v[:wide]) for v in shared_rows)
        head_bias = jnp.stack([split(head[:, :width]), split(head[:, 2 * width : 3 * width])])
        up_out = split(up_bias[:, : up.shape[1]])
        out = attn[:, 3 * width :].T
        return (gain, shift, proj, head_bias, out, out_bias, f_gain, f_shift, up, up_out, down.T, d_bias)

    at = 3 + planes
    wide, narrow = patches.shape[1], cotangent.shape[1]
    enc_out = block_out(
        enc_grads,
        (late[0], late[1], late[2], early[0], early[1], early[2]),
        late[3 : 3 + planes],
        early[3:at],
        wide,
    )
    dec_out = block_out(
        dec_grads,
        [early[at + k] for k in range(6)],
        early[at + 6 + planes : at + 6 + 2 * planes],
        early[at + 6 : at + 6 + planes],
        narrow,
    )
    bridge_bias_out = shared(early[at + 6 + 2 * planes, :narrow])
    return (
        (decoded[:rows], patches_grad[:rows])
        + enc_out
        + (bridge_out, bridge_bias_out)
        + dec_out
    )


def solution(mesh):
    block_in = (
        P(),
        P(),
        P(None, None, "mp"),
        P(None, "mp"),
        P("mp", None),
        P(),
        P(),
        P(),
        P(None, "mp"),
        P("mp"),
        P("mp", None),
        P(),
    )
    both = P(("dp", "mp"))
    block_out = (
        both,
        both,
        P(None, "dp", "mp"),
        P(None, ("mp", "dp")),
        P("mp", "dp"),
        both,
        both,
        both,
        P("dp", "mp"),
        P(("mp", "dp")),
        P("mp", "dp"),
        both,
    )
    rows = P(("dp", "mp"), None)
    return jax.shard_map(
        partial(shards, dict(mesh.shape)),
        mesh=mesh,
        in_specs=(rows, P("dp")) + block_in + (P(), P()) + block_in + (rows,),
        out_specs=(rows, rows) + block_out + (rows, both) + block_out,
        check_vma=False,
    )
```

time: 552 us -> 410 us (0.74)
  matrix products: 118 us -> 0 us
  other arithmetic: 26.8 us -> 4.14 us
  Pallas kernels: 346 us -> 365 us
  blocking collectives: 13.2 us -> 0 us
    dot_general x27 -> x0, matrix products: 118 us -> none  [mm(): return jnp.einsum(spec, left, right, preferred_element_type=F32)]
    pallas_call x5 -> x8, Pallas kernels: 183 us -> 274 us  [the longest x4 203 us: staged_call(): pl.pallas_call(kernel, out_shape=[jax.ShapeDtypeStruct(shape, dtype) for...]
    pallas_call x1, Pallas kernels: 162 us -> 91.8 us  [gather_weights(): pl.pallas_call(partial(gather_kernel, count, planes), out_shape=[jax.Shap...]
    transpose x19 -> x2, local copies, waits for them, and re-layouts: 14.9 us -> 1.59 us  [block_out(): out = attn[:, 3 * width:].T]
    all_gather x1 -> x0, blocking collectives: 13.2 us -> none  [shards(): small = lax.all_gather(small, 'mp', axis=0)]
    concatenate x6 -> x2, other arithmetic: 10.5 us -> 0.02 us  [block_forward(): bias = jnp.concatenate([head_bias[0], zeros, head_bias[1]], -1)[:, None]]
    reduce_sum x14 -> x0, other arithmetic: 10.4 us -> none  [the longest x5 4.92 us: column_sums(): return jnp.sum(values.astype(F32), -2)]
    dynamic_slice x0 -> x14, local copies, waits for them, and re-layouts: none -> 6.13 us  [the longest x10 5.83 us: shared(): return lax.dynamic_slice_in_dim(row, (dp * planes + mp) * size, size)]
where the time goes in v2:
time: 410 us; the launch traced here: 406 us
  Pallas kernels  365 us (89%)
  local copies, waits for them, and re-layouts  34.6 us (8%)
  other arithmetic  4.14 us (1%)
    pallas_call x4, Pallas kernels, staged_call(): pl.pallas_call(kernel, out_shape=[jax.ShapeDtypeStruct(shape, dtype) for...  203 us
    pallas_call x1, Pallas kernels, gather_weights(): pl.pallas_call(partial(gather_kernel, count, planes), out_shape=[jax.Shap...  91.8 us
    pallas_call x4, Pallas kernels, whole_call(): pl.pallas_call(kernel, out_shape=[jax.ShapeDtypeStruct(shape, dtype) for...  70.8 us

profile of v2, /device:TPU:28, one launch (start us, length us, event | category | flops | bytes accessed | tf_op | source)
XLA Modules:
  0.0 405.6 jit_solution(18431551040619455516)
XLA Ops:
  0.7 1.3 dynamic_slice.86.length.refs_0_
  2.0 2.1 pad.12.stream.refs_6_
  4.1 1.1 copy.71
  5.9 1.5 pad_maximum_fusion.refs_0_
  7.6 0.9 pad_maximum_fusion.1.refs_3_
  8.6 0.6 fusion.refs_6_
  9.2 91.8 %gather_weights.1 = (bf16[4,768,768]{2,1,0:T(8,128)(2,1)}, bf16[4,768,768]{2,1,0:T(8,128)(2,1)}, bf16[4,768,768]{2,1,0:T(8,128)(2,1)}, bf16[4,512,512]{2,1,0:T(8...) custom-call(bf16[768,768]{1,0:T(8,128)(2,1)} %pad_maximum_fusion.refs_0_, ...), custom_call_target="tpu_custom_call" | custom-call | tf_op jit(solution)/shard_map/gather_weights/pallas_call | solution.py:172
  101.0 0.6 broadcast_in_dim.61.gain.refs_8_
  102.2 0.8 copy.86
  103.2 0.6 broadcast_in_dim.64.bias
  104.4 20.1 %attn_forward.2 = (bf16[544,768]{1,0:T(8,128)(2,1)}, bf16[4,544,576]{2,1,0:T(8,128)(2,1)}, bf16[4,544,192]{2,1,0:T(8,128)(2,1)}, f32[4,3,544]{2,1,0:T(4,128)}, f32[544,768]{1,0:T(8,128)}) custom-call(s32[1]{0:T(128)} %dynamic_slice.86.length.refs_0_, bf16[544,768]{1,0:T(8,128)(2,1)} %pad.12.stream.refs_6_, ...), custom_call_target="tpu_custom_call" | custom-call | tf_op jit(solution)/shard_map/attn_forward/pallas_call | solution.py:588
  124.4 0.6 copy.74.refs_3_
  126.8 19.0 %feed_forward.2 = (bf16[544,768]{1,0:T(8,128)(2,1)}, bf16[4,544,768]{2,1,0:T(8,128)(2,1)}, bf16[4,544,768]{2,1,0:T(8,128)(2,1)}, bf16[544,768]{1,0:T(8,128)(2,1)}, f32[544,512]{1,0:T(8,128)}) custom-call(f32[544,768]{1,0:T(8,128)} %get-tuple-element.87.refs_0_.refs_6_, bf16[4,768,768]{2,1,0:T(8,128)(2,1)} %get-tuple-element.88.refs_1_.refs_7_, ...), custom_call_target="tpu_custom_call" | custom-call | tf_op jit(solution)/shard_map/feed_forward/pallas_call | solution.py:588
  145.8 0.6 broadcast_in_dim.74.bias
  146.4 19.5 %attn_forward.3 = (bf16[544,512]{1,0:T(8,128)(2,1)}, bf16[4,544,384]{2,1,0:T(8,128)(2,1)}, bf16[4,544,128]{2,1,0:T(8,128)(2,1)}, f32[4,4,544]{2,1,0:T(4,128)}, f32[544,512]{1,0:T(8,128)}) custom-call(s32[1]{0:T(128)} %dynamic_slice.86.length.refs_0_, f32[544,512]{1,0:T(8,128)} %get-tuple-element.90.stream.refs_6_, ...), custom_call_target="tpu_custom_call" | custom-call | tf_op jit(solution)/shard_map/attn_forward/pallas_call | solution.py:588
  165.9 0.6 broadcast_in_dim.76.refs_3_
  166.5 12.3 %feed_forward.3 = (bf16[544,512]{1,0:T(8,128)(2,1)}, bf16[4,544,512]{2,1,0:T(8,128)(2,1)}, bf16[4,544,512]{2,1,0:T(8,128)(2,1)}, bf16[544,512]{1,0:T(8,128)(2,1)}) custom-call(f32[544,512]{1,0:T(8,128)} %get-tuple-element.92.refs_0_.refs_4_, bf16[4,512,512]{2,1,0:T(8,128)(2,1)} %get-tuple-element.93.refs_1_.refs_5_, ...), custom_call_target="tpu_custom_call" | custom-call | tf_op jit(solution)/shard_map/feed_forward/pallas_call | solution.py:588
  178.8 1.9 slice.160
  180.7 0.9 pad.14.refs_0_
  181.6 17.7 %feed_backward.1 = (bf16[4,512,512]{2,1,0:T(8,128)(2,1)}, bf16[4,512,512]{2,1,0:T(8,128)(2,1)}, f32[4,8,512]{2,1,0:T(8,128)}, f32[544,512]{1,0:T(8,128)}, f32[8,...) custom-call(bf16[544,512]{1,0:T(8,128)(2,1)} %pad.14.refs_0_, bf16[4,544,512]{2,1,0:T(8,128)(2,1)} %get-tuple-element.96.refs_1_, ...), custom_call_target="tpu_custom_call" | custom-call | tf_op jit(solution)/shard_map/feed_backward/pallas_call | solution.py:668
  199.3 46.6 %attn_backward_sums.1 = (f32[4,8,384]{2,1,0:T(8,128)}, bf16[544,512]{1,0:T(8,128)(2,1)}, f32[8,512]{1,0:T(8,128)}, f32[8,512]{1,0:T(8,128)}, f32[8,512]{1,0:T(8,...) custom-call(s32[1]{0:T(128)} %dynamic_slice.86.length.refs_0_, ...), custom_call_target="tpu_custom_call" | custom-call | tf_op jit(solution)/shard_map/attn_backward_sums/pallas_call | solution.py:668
  245.9 35.4 %feed_backward_sums.1 = (bf16[4,768,768]{2,1,0:T(8,128)(2,1)}, bf16[4,768,768]{2,1,0:T(8,128)(2,1)}, f32[4,8,768]{2,1,0:T(8,128)}, f32[544,768]{1,0:T(8,128)}, f...) custom-call(bf16[544,512]{1,0:T(8,128)(2,1)} %get-tuple-element.106., ...), custom_call_target="tpu_custom_call" | custom-call | tf_op jit(solution)/shard_map/feed_backward_sums/pallas_call | solution.py:668
  281.3 102.9 %attn_backward_last.1 = (bf16[544,768]{1,0:T(8,128)(2,1)}, f32[96,768]{1,0:T(8,128)}, f32[96,768]{1,0:T(8,128)}, f32[96,768]{1,0:T(8,128)}, f32[24,768]{1,0:T(8,128)}, /*index=5*/f32[8,768]{1,0:T(8,128)}) custom-call(s32[1]{0:T(128)} %dynamic_slice.86.length.refs_0_, f32[544,768]{1,0:T(8,128)} %get-tuple-element.112.refs_1_, ...), custom_call_target="tpu_custom_call" | custom-call | tf_op jit(solution)/shard_map/attn_backward_last/pallas_call | solution.py:668
  384.3 2.1 slice.161
  386.5 0.9 fusion.17
  387.5 0.6 fusion.1
  388.0 0.6 fusion.2
  388.6 1.0 slice.164
  389.8 0.9 copy.77
  390.7 0.7 fusion.19
  392.1 1.0 slice_bitcast_fusion.3
  393.1 0.7 copy.78
  393.8 0.6 fusion.3
  394.4 0.6 fusion.4
  395.0 0.6 fusion.5
  395.6 0.6 dynamic-slice_bitcast_fusion.1
  396.2 0.6 fusion.6
  396.8 0.6 slice.173
  397.4 0.6 fusion.7
  398.0 0.6 fusion.9
  398.6 0.6 copy.79
  400.0 0.6 slice_bitcast_fusion.4
  400.6 0.6 fusion.11
  401.2 0.6 dynamic-slice_bitcast_fusion
  402.4 0.7 copy.92
  403.1 0.7 copy.93
  403.8 0.7 copy.94
  404.5 0.7 copy.95
  (82 shorter events, 6.3 us)
Async XLA Ops:
  0.7 4.6 %copy-start = (bf16[3,768,192]{1,2,0:T(8,128)(2,1)S(1)}, bf16[3,768,192]{1,2,0:T(8,128)(2,1)}, u32[]{:S(2)}) copy-start(bf16[3,768,192]{1,2,0:T(8,128)(2,1)} %param.33) | copy-start | bytes 2654212
  5.5 1.9 copy-start.6
  5.5 2.1 copy-start.2
  5.9 2.6 copy-start.19
  5.9 2.7 copy-start.11
  5.9 2.7 copy-start.18
  5.9 2.6 copy-start.20
  9.2 91.8 %copy-start.12 = (f32[768]{0:T(1024)S(1)}, f32[768]{0:T(1024)}, u32[]{:S(2)}) copy-start(f32[768]{0:T(1024)} %param.31) | copy-start | bytes 9220
  9.2 92.4 %copy-start.13 = (f32[768]{0:T(1024)S(1)}, f32[768]{0:T(1024)}, u32[]{:S(2)}) copy-start(f32[768]{0:T(1024)} %param.32) | copy-start | bytes 9220
  9.2 94.6 %copy-start.14 = (f32[768]{0:T(1024)S(1)}, f32[768]{0:T(1024)}, u32[]{:S(2)}) copy-start(f32[768]{0:T(1024)} %param.36) | copy-start | bytes 9220
  104.4 20.7 %copy-start.15 = (f32[768]{0:T(1024)S(1)}, f32[768]{0:T(1024)}, u32[]{:S(2)}) copy-start(f32[768]{0:T(1024)} %param.37) | copy-start | bytes 9220
  104.4 21.3 %copy-start.16 = (f32[768]{0:T(1024)S(1)}, f32[768]{0:T(1024)}, u32[]{:S(2)}) copy-start(f32[768]{0:T(1024)} %param.38) | copy-start | bytes 9220
  104.4 21.9 %copy-start.17 = (f32[768]{0:T(1024)S(1)}, f32[768]{0:T(1024)}, u32[]{:S(2)}) copy-start(f32[768]{0:T(1024)} %param.42) | copy-start | bytes 9220
  166.5 14.2 %copy-start.1 = (bf16[529,512]{1,0:T(8,128)(2,1)S(1)}, bf16[529,512]{1,0:T(8,128)(2,1)}, u32[]{:S(2)}) copy-start(bf16[529,512]{1,0:T(8,128)(2,1)} %param.57) | copy-start | bytes 1625092
  384.3 11.3 %copy-start.10 = (f32[24,768]{1,0:T(8,128)S(1)}, f32[24,768]{1,0:T(8,128)}, u32[]{:S(2)}) copy-start(f32[24,768]{1,0:T(8,128)} %get-tuple-element.135) | copy-start | bytes 221188
  384.3 12.4 %copy-start.9 = (f32[32,512]{1,0:T(8,128)S(1)}, f32[32,512]{1,0:T(8,128)}, u32[]{:S(2)}) copy-start(f32[32,512]{1,0:T(8,128)} %get-tuple-element.138) | copy-start | bytes 196612
  384.3 14.3 %copy-start.5 = (f32[64,512]{1,0:T(8,128)S(1)}, f32[64,512]{1,0:T(8,128)}, u32[]{:S(2)}) copy-start(f32[64,512]{1,0:T(8,128)} %get-tuple-element.139) | copy-start | bytes 393220
  384.3 18.1 %copy-start.4 = (f32[96,768]{1,0:T(8,128)S(1)}, f32[96,768]{1,0:T(8,128)}, u32[]{:S(2)}) copy-start(f32[96,768]{1,0:T(8,128)} %get-tuple-element.272) | copy-start | bytes 884740
  386.5 16.6 %copy-start.3 = (f32[96,768]{1,0:T(8,128)S(1)}, f32[96,768]{1,0:T(8,128)}, u32[]{:S(2)}) copy-start(f32[96,768]{1,0:T(8,128)} %get-tuple-element.137) | copy-start | bytes 884740
  388.6 15.2 %copy-start.8 = (f32[64,512]{1,0:T(8,128)S(1)}, f32[64,512]{1,0:T(8,128)}, u32[]{:S(2)}) copy-start(f32[64,512]{1,0:T(8,128)} %get-tuple-element.286) | copy-start | bytes 393220
  389.6 14.9 %copy-start.7 = (f32[64,512]{1,0:T(8,128)S(1)}, f32[64,512]{1,0:T(8,128)}, u32[]{:S(2)}) copy-start(f32[64,512]{1,0:T(8,128)} %get-tuple-element.141) | copy-start | bytes 393220

commit v3 on v2

v3 whole, which is shorter than its diff:
```python
from functools import partial

import jax
import jax.numpy as jnp
from jax import lax
from jax.experimental import pallas as pl
from jax.experimental.pallas import tpu as pltpu
from jax.sharding import PartitionSpec as P

HEAD = 64
DHEAD = 32
EPSILON = 1e-06
MESH = pl.DeviceIdType.MESH
F32 = jnp.float32
BF16 = jnp.bfloat16
VMEM_BYTES = 60 * 1024 * 1024


def neighbours():
    dp, mp = lax.axis_index("dp"), lax.axis_index("mp")
    core, x, y = dp % 2, (dp // 2) % 2, dp // 4
    across_core = dp + 1 - 2 * core
    across_x = dp + 2 - 4 * x
    across_y = dp + 4 - 8 * y
    return dp, mp, core, x, y, across_core, across_x, across_y


def entry_barrier(parts):
    mp, across_core, across_x, across_y = parts
    dp = lax.axis_index("dp")
    barrier = pltpu.get_barrier_semaphore()
    planes = lax.axis_size("mp")
    for other in (across_core, across_x, across_y):
        pl.semaphore_signal(barrier, inc=1, device_id=(other, mp), device_id_type=MESH)
    for step in range(1, planes):
        pl.semaphore_signal(
            barrier, inc=1, device_id=(dp, (mp + step) % planes), device_id_type=MESH
        )
    pl.semaphore_wait(barrier, 3 + planes - 1)


def plane_order(mp, planes):
    if planes != 4:
        return [(mp + step) % planes for step in range(1, planes)]
    upper = mp // 2
    place = mp + upper * (3 - 2 * mp)
    return [o + upper * (3 - 2 * o) for o in (place + 1, 2 - 2 * place, 3)]


def order_of(k, mp):
    upper = mp // 2
    place = mp + upper * (3 - 2 * mp)
    plane = (k + place) % 3 * (1 - k // 3) + 3 * (k // 3)
    return plane + upper * (3 - 2 * plane)


class Gatherer:
    A, X, Y, S, DY, DX, SX, SY, SDY, SDX = range(10)
    kinds = 10

    def __init__(self, planes, shards, placed, wholes, targets, smalls, sems):
        self.planes, self.count, self.placed = planes, len(shards), placed
        self.shards, self.wholes, self.targets = shards, wholes, targets
        self.small, self.smalls = smalls.at[lax.axis_index("mp")], smalls
        self.local_sem, self.flush_sem, self.send_sem, self.recv_sem = sems
        self.dp, self.mp, core, x, y, *across = neighbours()
        self.across_core, self.across_x, self.across_y = across
        self.others = plane_order(self.mp, planes)
        corner = self.across_x + self.across_y - self.dp
        shift = self.across_core - self.dp
        self.arrivals = {
            self.A: (self.dp, None),
            self.X: (self.across_x, None),
            self.Y: (self.across_y, None),
            self.S: (self.across_core, None),
            self.DY: (corner, 0),
            self.DX: (corner, 1),
            self.SX: (self.across_x + shift, None),
            self.SY: (self.across_y + shift, None),
            self.SDY: (corner + shift, 0),
            self.SDX: (corner + shift, 1),
        }
        self.onward = {
            self.X: (self.dp, None, self.across_x),
            self.Y: (self.dp, None, self.across_y),
            self.S: (self.dp, None, self.across_core),
            self.DY: (self.across_x, 0, self.across_y),
            self.DX: (self.across_y, 1, self.across_x),
            self.SX: (self.across_x, None, self.across_core),
            self.SY: (self.across_y, None, self.across_core),
            self.SDY: (corner, 0, self.across_core),
            self.SDX: (corner, 1, self.across_core),
        }

    @staticmethod
    def sems(count, planes):
        return [
            pltpu.SemaphoreType.DMA((count,)),
            pltpu.SemaphoreType.DMA((count, planes)),
            pltpu.SemaphoreType.DMA((count + 1, planes, Gatherer.kinds)),
            pltpu.SemaphoreType.DMA((count + 1, planes, Gatherer.kinds)),
        ]

    def rows_of(self, m, owner, half):
        piece = self.shards[m].shape[0] // 8
        if half is None:
            return pl.ds(owner * piece, piece)
        return pl.ds(owner * piece + half * (piece // 2), piece // 2)

    def remote(self, m, kind, src, dst, send_plane, recv_plane, target):
        return pltpu.make_async_remote_copy(
            src_ref=src,
            dst_ref=dst,
            send_sem=self.send_sem.at[m, send_plane, kind],
            recv_sem=self.recv_sem.at[m, recv_plane, kind],
            device_id=target,
            device_id_type=MESH,
        )

    def send(self, m, i, kind):
        plane = self.others[i]
        if kind == self.A:
            own = self.rows_of(m, self.dp, None)
            src, dst = self.shards[m].at[own], self.wholes[m].at[self.mp, own]
            return self.remote(m, kind, src, dst, plane, self.mp, (self.dp, plane))
        owner, half, target = self.onward[kind]
        part = self.wholes[m].at[plane, self.rows_of(m, owner, half)]
        return self.remote(m, kind, part, part, plane, plane, (target, self.mp))

    def send_small(self, i):
        plane = self.others[i]
        return self.remote(
            self.count,
            self.A,
            self.small,
            self.smalls.at[self.mp],
            plane,
            self.mp,
            (self.dp, plane),
        )

    def arrived(self, m, i, kind):
        plane = self.others[i]
        owner, half = self.arrivals[kind]
        part = self.wholes[m].at[plane, self.rows_of(m, owner, half)]
        self.remote(m, kind, part, part, plane, plane, (self.across_core, self.mp)).wait_recv()

    def along_z(self, m, i):
        self.send(m, i, self.A).start()

    def to_plane(self, m, i):
        self.arrived(m, i, self.A)
        for kind in (self.X, self.Y, self.S):
            self.send(m, i, kind).start()

    def to_corner(self, m, i):
        self.arrived(m, i, self.X)
        self.send(m, i, self.DY).start()
        self.send(m, i, self.SX).start()
        self.arrived(m, i, self.Y)
        self.send(m, i, self.DX).start()
        self.send(m, i, self.SY).start()

    def to_core(self, m, i):
        self.arrived(m, i, self.DY)
        self.send(m, i, self.SDY).start()
        self.arrived(m, i, self.DX)
        self.send(m, i, self.SDX).start()

    def flush(self, m, plane):
        return pltpu.make_async_copy(
            self.wholes[m].at[plane], self.targets[m].at[plane], self.flush_sem.at[m, plane]
        )

    def whole(self, m, i):
        for kind in (self.S, self.SX, self.SY, self.SDY, self.SDX):
            self.arrived(m, i, kind)
        self.flush(m, self.others[i]).start()

    def own(self, m):
        return pltpu.make_async_copy(
            self.shards[m], self.wholes[m].at[self.mp], self.local_sem.at[m]
        )

    def begin(self):
        for m in range(self.count):
            if m not in self.placed:
                self.own(m).start()

    def begin_small(self):
        for i in range(self.planes - 1):
            self.send_small(i).start()

    def have_own(self, m):
        if m not in self.placed:
            self.own(m).wait()
        self.flush(m, self.mp).start()

    def have_small(self):
        for i in range(self.planes - 1):
            part = self.smalls.at[self.others[i]]
            self.remote(
                self.count,
                self.A,
                part,
                part,
                self.others[i],
                self.others[i],
                (self.across_core, self.mp),
            ).wait_recv()

    def drain(self):
        for m in range(self.count):
            for i in range(self.planes - 1):
                for kind in range(self.kinds):
                    self.send(m, i, kind).wait_send()
            for p in range(self.planes):
                self.flush(m, p).wait()
        for i in range(self.planes - 1):
            self.send_small(i).wait_send()


class Reducer:
    def __init__(self, shapes, planes, refs):
        self.planes, self.count = planes, len(shapes)
        refs = list(refs)
        take = lambda: [refs.pop(0) for _ in range(self.count)]
        self.mine, self.from_core, self.from_x, self.from_y = take(), take(), take(), take()
        self.then_y, self.then_x, self.from_z = take(), take(), take()
        self.local_sem, self.send_sem, self.recv_sem = refs
        self.dp, self.mp, self.core_id, self.x, self.y, *across = neighbours()
        self.across_core, self.across_x, self.across_y = across
        self.halves = [rows // 2 for rows, columns in shapes]
        self.parts = [None] * self.count

    @staticmethod
    def scratch(shapes, planes, resident=()):
        count = len(shapes)

        def buffers(*lead, halves=False, skip=()):
            return [
                pltpu.VMEM((1, 16, 128), BF16)
                if m in skip
                else pltpu.VMEM(lead + (r // 2 if halves else r, c), BF16)
                for m, (r, c) in enumerate(shapes)
            ]

        return (
            buffers(planes, 2, 2, skip=resident)
            + buffers(planes, 2, 2)
            + buffers(planes, 2, halves=True)
            + buffers(planes, 2, halves=True)
            + buffers(planes, halves=True)
            + buffers(planes, halves=True)
            + buffers(planes)
            + [
                pltpu.SemaphoreType.DMA((count, planes)),
                pltpu.SemaphoreType.DMA((count, planes, 6)),
                pltpu.SemaphoreType.DMA((count, planes, 6)),
            ]
        )

    def remote(self, m, p, kind, src, dst, target, recv_plane=None):
        return pltpu.make_async_remote_copy(
            src_ref=src,
            dst_ref=dst,
            send_sem=self.send_sem.at[m, p, kind],
            recv_sem=self.recv_sem.at[m, p if recv_plane is None else recv_plane, kind],
            device_id=target,
            device_id_type=MESH,
        )

    def own(self, m, p, b, a):
        if self.resident(m):
            return self.parts[m].at[p, b, a, self.core_id]
        return self.mine[m].at[p, b, a]

    def owned(self, m, p, b, a, rows):
        if self.resident(m):
            return self.parts[m].at[p, b, a, self.core_id, rows]
        return self.mine[m].at[p, b, a, rows]

    def resident(self, m):
        return self.mine[m].shape[0] == 1

    def begin(self, m, p):
        if not self.resident(m):
            pltpu.make_async_copy(
                self.parts[m].at[p, :, :, self.core_id], self.mine[m].at[p], self.local_sem.at[m, p]
            ).start()
        self.to_core(m, p).start()

    def to_core(self, m, p):
        return self.remote(
            m,
            p,
            0,
            self.parts[m].at[p, :, :, 1 - self.core_id],
            self.from_core[m].at[p],
            (self.across_core, self.mp),
        )

    def to_x(self, m, p):
        src = self.owned(m, p, slice(None), 1 - self.x, pl.ds(0, self.halves[m]))
        return self.remote(m, p, 1, src, self.from_x[m].at[p], (self.across_x, self.mp))

    def to_y(self, m, p):
        half = self.halves[m]
        src = self.owned(m, p, 1 - self.y, slice(None), pl.ds(half, half))
        return self.remote(m, p, 2, src, self.from_y[m].at[p], (self.across_y, self.mp))

    def x_to_y(self, m, p):
        src = self.owned(m, p, 1 - self.y, self.x, pl.ds(0, self.halves[m]))
        return self.remote(m, p, 3, src, self.then_y[m].at[p], (self.across_y, self.mp))

    def y_to_x(self, m, p):
        half = self.halves[m]
        src = self.owned(m, p, self.y, 1 - self.x, pl.ds(half, half))
        return self.remote(m, p, 4, src, self.then_x[m].at[p], (self.across_x, self.mp))

    def to_z(self, m, p):
        src = self.own(m, p, self.y, self.x)
        return self.remote(m, p, 5, src, self.from_z[m].at[self.mp], (self.dp, p), self.mp)

    def core(self, m, p):
        if not self.resident(m):
            pltpu.make_async_copy(
                self.parts[m].at[p, :, :, self.core_id], self.mine[m].at[p], self.local_sem.at[m, p]
            ).wait()
        self.to_core(m, p).wait_recv()
        for b in range(2):
            for a in range(2):
                ref = self.own(m, p, b, a)
                ref[...] = ref[...] + self.from_core[m][p, b, a]
        self.to_x(m, p).start()
        self.to_y(m, p).start()

    def plane(self, m, p):
        half = self.halves[m]
        self.to_x(m, p).wait_recv()
        for b in range(2):
            ref = self.owned(m, p, b, self.x, pl.ds(0, half))
            ref[...] = ref[...] + self.from_x[m][p, b]
        self.x_to_y(m, p).start()
        self.to_y(m, p).wait_recv()
        for a in range(2):
            ref = self.owned(m, p, self.y, a, pl.ds(half, half))
            ref[...] = ref[...] + self.from_y[m][p, a]
        self.y_to_x(m, p).start()

    def corner(self, m, p):
        half = self.halves[m]
        self.x_to_y(m, p).wait_recv()
        self.y_to_x(m, p).wait_recv()
        ref = self.owned(m, p, self.y, self.x, pl.ds(0, half))
        ref[...] = ref[...] + self.then_y[m][p]
        ref = self.owned(m, p, self.y, self.x, pl.ds(half, half))
        ref[...] = ref[...] + self.then_x[m][p]

        @pl.when(p != self.mp)
        def _():
            self.to_z(m, p).start()

    def finish(self, m, out):
        total = self.own(m, self.mp, self.y, self.x)[...].astype(F32)
        for step in range(1, self.planes):
            plane = (self.mp + step) % self.planes
            src = self.from_z[m].at[plane]
            self.remote(m, plane, 5, src, src, (self.dp, plane)).wait_recv()
            total = total + src[...].astype(F32)
        out[...] = total

    def drain(self):
        @pl.loop(0, self.planes)
        def _(p):
            for m in range(self.count):
                for copy in (self.to_core, self.to_x, self.to_y, self.x_to_y, self.y_to_x):
                    copy(m, p).wait_send()

                @pl.when(p != self.mp)
                def _():
                    self.to_z(m, p).wait_send()


def collect(part, sizes):
    part = lax.psum_scatter(part, "mp", scatter_dimension=0, tiled=False)
    return lax.psum_scatter(part.astype(F32), "dp", scatter_dimension=0, tiled=False)


LOG2E = 1.4426950408889634
ROW_BLOCK = 32
NT = (((1,), (1,)), ((), ()))


def dot(left, right, dims=(((1,), (0,)), ((), ()))):
    return lax.dot_general(left, right, dims, preferred_element_type=F32)


def standardize(x):
    centered = x - jnp.mean(x, -1, keepdims=True)
    scale = lax.rsqrt(jnp.mean(centered * centered, -1, keepdims=True) + EPSILON)
    return centered * scale, scale


def gelu_and_slope(b):
    cdf = 0.5 * (1.0 + lax.erf(b * 0.7071067811865476))
    density = jnp.exp(-0.5 * b * b) * 0.3989422804014327
    return b * cdf, cdf + b * density


def fold_rows(x):
    return jnp.sum(x.reshape(x.shape[0] // 8, 8, x.shape[1]), 0)


def row_blocks(rows):
    return pl.loop(0, rows // ROW_BLOCK)


def block_at(i):
    return pl.ds(pl.multiple_of(i * ROW_BLOCK, ROW_BLOCK), ROW_BLOCK)


def whole_lanes(columns):
    return -(-columns // 128) * 128


def strip_forward(head_dim, width, length, p, triple, attended, logsum):
    rows = triple.shape[1]
    visible = lax.broadcasted_iota(jnp.int32, (rows, 1), 0) < length
    factor = head_dim**-0.5 * LOG2E
    outs = []
    for head in range(width // head_dim):
        low = head * head_dim
        query = triple[p, :, low : low + head_dim]
        key = triple[p, :, width + low : width + low + head_dim]
        value = triple[p, :, 2 * width + low : 2 * width + low + head_dim]
        scores = jnp.where(visible, dot(key, query, NT) * factor, -1e30)
        ceiling = jnp.max(scores, 0, keepdims=True)
        exponent = jnp.exp2(scores - ceiling)
        denominator = jnp.sum(exponent, 0, keepdims=True)
        outs.append(dot(value.T, exponent.astype(BF16)) * (1.0 / denominator))
        logsum[p, head : head + 1, :] = ceiling + jnp.log2(denominator)
    attended[p, :, :width] = jnp.concatenate(outs, 0).T.astype(BF16)


def strip_backward(head_dim, width, length, p, triple, attended, mixed, logsum, out):
    rows = triple.shape[1]
    visible = lax.broadcasted_iota(jnp.int32, (rows, 1), 0) < length
    factor = head_dim**-0.5
    products = (mixed.astype(F32) * attended[p, :, :width].astype(F32)).T
    query_grads = []
    for head in range(width // head_dim):
        low = head * head_dim
        query = triple[p, :, low : low + head_dim]
        key = triple[p, :, width + low : width + low + head_dim]
        value = triple[p, :, 2 * width + low : 2 * width + low + head_dim]
        mixed_head = mixed[:, low : low + head_dim]
        row_sums = jnp.sum(products[low : low + head_dim], 0, keepdims=True)
        scores = dot(key, query, NT) * (factor * LOG2E) - logsum[p, head : head + 1, :]
        chances = jnp.exp2(jnp.where(visible, scores, -1e30))
        chance_grad = dot(value, mixed_head, NT)
        score_grad = (chances * (chance_grad - row_sums)).astype(BF16)
        key_grad = dot(score_grad, query) * factor
        value_grad = dot(chances.astype(BF16), mixed_head)
        query_grads.append(dot(key.T, score_grad) * factor)
        out[:, width + low : width + low + head_dim] = key_grad.astype(BF16)
        out[:, 2 * width + low : 2 * width + low + head_dim] = value_grad.astype(BF16)
    out[:, :width] = jnp.concatenate(query_grads, 0).T.astype(BF16)


def attn_forward(head_dim, length, stream, weight, vectors, bias_of, outs, order, before):
    gain, shift, out_bias = [as_row(v) for v in vectors]
    normed, triple, attended, logsum, middle = outs
    planes, rows = triple.shape[:2]
    width = weight.shape[2] // 4

    @row_blocks(rows)
    def _(i):
        x = stream[block_at(i), :].astype(F32)
        normed[block_at(i), :] = (standardize(x)[0] * gain + shift).astype(BF16)
        middle[block_at(i), :] = x + out_bias

    @pl.loop(0, planes)
    def _(k):
        before(k)
        p = order(k)
        projected = dot(normed[...], weight[p, :, : 3 * width]) + bias_of(p)
        triple[p, :, : 3 * width] = projected.astype(BF16)
        strip_forward(head_dim, width, length, p, triple, attended, logsum)
        middle[...] += dot(attended[p, :, :width], weight[p, :, 3 * width :], NT)


def feed_forward(middle, up, down, vectors, bias_of, outs, total, order, before):
    gain, shift, down_bias = [as_row(v) for v in vectors]
    feed_input, hidden, slope = outs
    planes, rows, width = hidden.shape

    @row_blocks(rows)
    def _(i):
        x = middle[block_at(i), :]
        feed_input[block_at(i), :] = (standardize(x)[0] * gain + shift).astype(BF16)
        total[block_at(i), :] = x + down_bias

    @pl.loop(0, planes)
    def _(k):
        before(k)
        p = order(k)
        bias = bias_of(p)
        for low in range(0, width, 256):
            part = slice(low, low + 256)
            activated, rise = gelu_and_slope(dot(feed_input[...], up[p, :, part]) + bias[:, part])
            hidden[p, :, part] = activated.astype(BF16)
            slope[p, :, part] = rise.astype(BF16)
        total[...] += dot(hidden[p], down[p])


def as_row(vector):
    return vector[...].reshape(1, -1)


def layer_backward(stream, gain, upstream, spare, gain_sums, shift_sums):
    gain_sums[...] = jnp.zeros_like(gain_sums)
    shift_sums[...] = jnp.zeros_like(shift_sums)
    gain = as_row(gain)

    @row_blocks(stream.shape[0])
    def _(i):
        hat, scale = standardize(stream[block_at(i), :].astype(F32))
        grad = spare[block_at(i), :]
        gain_sums[...] += fold_rows(grad * hat)
        shift_sums[...] += fold_rows(grad)
        grad = grad * gain
        part = grad - jnp.mean(grad, -1, keepdims=True)
        part = part - hat * jnp.mean(grad * hat, -1, keepdims=True)
        spare[block_at(i), :] = upstream[block_at(i), :].astype(F32) + part * scale


def put_transposed(values, turned):
    columns = values.shape[1]
    turned[:columns, :] = values.T
    turned[columns:, :] = jnp.ones((16, values.shape[0]), BF16)


def start_branch(upstream, branch, turned, sums, total):
    rows, wide = branch.shape
    sums[...] = jnp.zeros_like(sums)

    @row_blocks(rows)
    def _(i):
        rounded = upstream[block_at(i), :].astype(BF16)
        branch[block_at(i), :] = rounded
        sums[...] += fold_rows(rounded.astype(F32))
        total[block_at(i), :] = jnp.zeros((ROW_BLOCK, wide), F32)

    turned[...] = branch[...].T


def matrix(ref, p):
    values = ref[p]
    return values.reshape(8 * values.shape[3], values.shape[4])


def put_matrix(ref, p, value):
    ref[p] = value.reshape(ref.shape[1:])


def feed_backward(upstream, saved, weights, scratch, sums, total, hook):
    hidden, slope, feed_input = saved
    up, down = weights
    branch, branch_turned, feed_turned = scratch
    branch_sums, up_sums = sums
    planes = hidden.shape[0]
    wide = branch.shape[1]
    start_branch(upstream, branch, branch_turned, branch_sums, total)
    put_transposed(feed_input[...], feed_turned)

    @pl.loop(0, planes)
    def _(p):
        down_grad = dot(branch_turned[...], hidden[p]).astype(BF16)
        hidden_grad = dot(branch[...], matrix(down, p), NT)
        put_matrix(down, p, down_grad)
        before_grad = (hidden_grad * slope[p].astype(F32)).astype(BF16)
        total[...] += dot(before_grad, matrix(up, p), NT)
        both = dot(feed_turned[...], before_grad)
        put_matrix(up, p, both[:wide].astype(BF16))
        up_sums[p] = both[wide : wide + 8]
        hook(p)


def attn_backward(head_dim, length, upstream, saved, weight, scratch, sums, total, hook):
    attended, triple, logsum, normed = saved
    branch, branch_turned, normed_turned, triple_grad = scratch
    branch_sums, head_sums = sums
    planes, width = attended.shape[0], weight.shape[5] // 4
    wide = branch.shape[1]
    start_branch(upstream, branch, branch_turned, branch_sums, total)
    put_transposed(normed[...], normed_turned)

    @pl.loop(0, planes)
    def _(p):
        own = matrix(weight, p)
        mixed = dot(branch[...], own[:, 3 * width :]).astype(BF16)
        strip_backward(head_dim, width, length, p, triple, attended, mixed, logsum, triple_grad)
        total[...] += dot(triple_grad[...], own[:, : 3 * width], NT)
        both = dot(normed_turned[...], triple_grad[...])
        out_grad = dot(branch_turned[...], attended[p, :, :width])
        grad = jnp.concatenate([both[:wide].astype(BF16), out_grad.astype(BF16)], -1)
        put_matrix(weight, p, grad)
        head_sums[p] = both[wide : wide + 8]
        hook(p)


IN_VMEM = pl.BlockSpec(memory_space=pltpu.VMEM)
IN_SMEM = pl.BlockSpec(memory_space=pltpu.SMEM)


class Load:
    def __init__(self, source, ref, sem):
        self.ref, self.copy, self.waits = ref, pltpu.make_async_copy(source, ref, sem), True
        self.copy.start()

    def use(self):
        if self.waits:
            self.copy.wait()
            self.waits = False
        return self.ref


class Store:
    def __init__(self, ref, target, sems):
        self.ref, self.target, self.sems, self.by_plane = ref, target, sems, False

    def flush(self, p=None):
        if p is None:
            pltpu.make_async_copy(self.ref, self.target, self.sems.at[0]).start()
        else:
            self.by_plane = True
            pltpu.make_async_copy(self.ref.at[p], self.target.at[p], self.sems.at[p]).start()

    def finish(self):
        if not self.by_plane:
            pltpu.make_async_copy(self.ref, self.target, self.sems.at[0]).wait()
            return
        for p in range(self.ref.shape[0]):
            pltpu.make_async_copy(self.ref.at[p], self.target.at[p], self.sems.at[p]).wait()


def staged_call(name, body, ins, outs, scratch=(), collective_id=None):
    any_spec = pl.BlockSpec(memory_space=pl.ANY)
    near = lambda v: IN_SMEM if v.dtype == jnp.int32 else IN_VMEM
    loads = [v for mode, v in ins if mode == "load"]
    stores = [(shape, dtype) for mode, shape, dtype in outs if mode == "store"]
    scratch = list(scratch)

    def kernel(*refs):
        refs = list(refs)
        take = lambda n: [refs.pop(0) for _ in range(n)]
        in_refs, out_refs = take(len(ins)), take(len(outs))
        load_refs, store_refs, rest = take(len(loads)), take(len(stores)), take(len(scratch))
        load_sem, store_sem = refs
        given, load_at = [], 0
        for (mode, _), ref in zip(ins, in_refs):
            if mode == "load":
                given.append(Load(ref, load_refs[load_at], load_sem.at[load_at]))
                load_at += 1
            else:
                given.append(ref)
        results, store_at = [], 0
        for (mode, _, _), ref in zip(outs, out_refs):
            if mode == "store":
                results.append(Store(store_refs[store_at], ref, store_sem.at[store_at]))
                store_at += 1
            else:
                results.append(ref)
        body(given, results, rest)
        for item in given:
            if isinstance(item, Load):
                item.use()
        for item in results:
            if isinstance(item, Store):
                item.finish()

    params = {"vmem_limit_bytes": VMEM_BYTES}
    if collective_id is not None:
        params.update(collective_id=collective_id, has_side_effects=True)
    return pl.pallas_call(
        kernel,
        out_shape=[jax.ShapeDtypeStruct(shape, dtype) for _, shape, dtype in outs],
        in_specs=[near(v) if mode == "near" else any_spec for mode, v in ins],
        out_specs=[IN_VMEM if mode == "near" else any_spec for mode, _, _ in outs],
        scratch_shapes=[pltpu.VMEM(v.shape, v.dtype) for v in loads]
        + [pltpu.VMEM(shape, dtype) for shape, dtype in stores]
        + scratch
        + [pltpu.SemaphoreType.DMA((max(len(loads), 1),))]
        + [pltpu.SemaphoreType.DMA((max(len(stores), 1), 4))],
        compiler_params=pltpu.CompilerParams(**params),
        name=name,
    )(*[v for _, v in ins])


def nothing(p):
    pass


def at_planes(schedule):
    def hook(p):
        for k, work in enumerate(schedule):

            @pl.when(p == k)
            def _():
                for step in work:
                    step()

    return hook


def six_deep(grad):
    planes, rows, columns = grad.shape
    return grad.reshape(planes, 2, 2, 2, rows // 8, columns)


class VectorSum:
    def __init__(self, refs):
        self.levels, self.came, self.from_z, self.send_sem, self.recv_sem = refs
        self.dp, self.mp, core, x, y, *across = neighbours()
        self.across = across

    @staticmethod
    def scratch(rows, columns, planes):
        return [
            pltpu.VMEM((4, rows, columns), F32),
            pltpu.VMEM((3, rows, columns), F32),
            pltpu.VMEM((planes, rows, columns), F32),
            pltpu.SemaphoreType.DMA((3 + planes,)),
            pltpu.SemaphoreType.DMA((3 + planes,)),
        ]

    def hop(self, level):
        return pltpu.make_async_remote_copy(
            src_ref=self.levels.at[level],
            dst_ref=self.came.at[level],
            send_sem=self.send_sem.at[level],
            recv_sem=self.recv_sem.at[level],
            device_id=(self.across[level], self.mp),
            device_id_type=MESH,
        )

    def along(self, plane, receiving=False):
        slot = plane if receiving else self.mp
        return pltpu.make_async_remote_copy(
            src_ref=self.levels.at[3],
            dst_ref=self.from_z.at[slot],
            send_sem=self.send_sem.at[3 + plane],
            recv_sem=self.recv_sem.at[3 + slot],
            device_id=(self.dp, plane),
            device_id_type=MESH,
        )

    def begin(self):
        self.hop(0).start()

    def others(self):
        planes = self.from_z.shape[0]
        return [(self.mp + step) % planes for step in range(1, planes)]

    def advance(self, level):
        self.hop(level).wait_recv()
        self.levels[level + 1] = self.levels[level] + self.came[level]
        if level < 2:
            self.hop(level + 1).start()
        else:
            for plane in self.others():
                self.along(plane).start()

    def finish(self, out):
        total = self.levels[3]
        for plane in self.others():
            self.along(plane, receiving=True).wait_recv()
            total = total + self.from_z[plane]
        out[...] = total
        for level in range(3):
            self.hop(level).wait_send()
        for plane in self.others():
            self.along(plane).wait_send()


def stack_rows(rows, columns):
    wide = [
        row
        if row.shape[1] == columns
        else jnp.concatenate([row, jnp.zeros((1, columns - row.shape[1]), F32)], -1)
        for row in rows
    ]
    spare = -len(wide) % 8
    if spare:
        wide.append(jnp.zeros((spare, columns), F32))
    return jnp.concatenate(wide, 0)


def folded(sums):
    return jnp.sum(sums[...], 0, keepdims=True)


def first_rows(sums):
    return [sums[p, 0:1] for p in range(sums.shape[0])]


EARLY_DEC = 8
EARLY_ROWS = 24


def early_rows(feed_sums, dec_sums, bridge_sums):
    f_gain, f_shift, down_bias, up_bias = feed_sums
    rows = [folded(f_gain), folded(f_shift), folded(down_bias)] + first_rows(up_bias)
    empty = [jnp.zeros_like(rows[0])]
    gain, shift, out_bias, head, f_gain, f_shift, down_bias, up_bias = dec_sums
    rows += empty + [folded(v) for v in (gain, shift, out_bias)] + first_rows(up_bias) + empty
    rows += [folded(v) for v in (f_gain, f_shift, down_bias)] + first_rows(head)
    return rows + [bridge_sums[0:1]]


def late_rows(gain, shift, out_bias, head):
    return [folded(gain), folded(shift), folded(out_bias)] + first_rows(head)


def named_call(name, body, ins, outs, scratch, collective_id=None):
    flat, counts = [], {}
    for key, item in scratch.items():
        items = item if isinstance(item, list) else [item]
        counts[key] = len(items)
        flat += items

    def inner(in_refs, out_refs, refs):
        buffers, at = {}, 0
        for key, count in counts.items():
            part = refs[at : at + count]
            buffers[key] = part if isinstance(scratch[key], list) else part[0]
            at += count
        body(dict(zip(ins, in_refs)), dict(zip(outs, out_refs)), buffers)

    results = staged_call(name, inner, list(ins.values()), list(outs.values()), flat, collective_id)
    return dict(zip(outs, results))


SUM_NAMES = ("gain", "shift", "out_bias", "head", "f_gain", "f_shift", "down_bias", "up_bias")


def run_backward(fast, top, saved, weights, gains, lengths, head_dim, carry=None, dec_sums=None):
    (hidden, slope, feed_input, middle), (attended, triple, logsum, normed, stream) = saved
    attn, up, down = weights
    planes, rows, hidden_width = hidden.shape
    wide, width = attn.shape[1], attn.shape[2] // 4
    encoder = len(top) == 3
    last = fast and encoder
    narrow = top[0].shape[1]
    strip = top[0].shape[0]
    deep = wide // 8 // planes
    tall = -(-deep // 32) * 32

    ins = {"lengths": ("near", lengths)}
    for key, value in zip(("rows", "input", "weight") if encoder else ("cotangent",), top):
        ins[key] = ("load" if encoder else "near", value)
    loads = {"feed_input": feed_input, "hidden": hidden, "slope": slope}
    loads.update(down=six_deep(down), up=six_deep(up), middle=middle)
    loads.update(attn=six_deep(attn), logsum=logsum, stream=stream)
    ins.update((key, ("load", value)) for key, value in loads.items())
    late_loads = {"triple": triple, "attended": attended, "normed": normed}
    ins.update((key, ("raw", value)) for key, value in late_loads.items())
    ins.update(attn_gain=("near", gains[0]), feed_gain=("near", gains[1]))

    sum_shapes = {key: (8, wide) for key in SUM_NAMES}
    sum_shapes.update(head=(planes, 8, 3 * width), up_bias=(planes, 8, hidden_width))
    if encoder:
        sum_shapes["bridge"] = (8, narrow)
    outs = {"input_grad": ("store", (rows, wide), BF16)}
    scratch = {
        "upstream": pltpu.VMEM((rows, wide), F32 if encoder else BF16),
        "middle_grad": pltpu.VMEM((rows, wide), F32),
        "branch": pltpu.VMEM((rows, wide), BF16),
        "branch_turned": pltpu.VMEM((wide, rows), BF16),
        "turned": pltpu.VMEM((wide + 16, rows), BF16),
        "triple_grad": pltpu.VMEM((rows, 3 * width), BF16),
        "late_sem": pltpu.SemaphoreType.DMA((3,)),
        "flush_sem": pltpu.SemaphoreType.DMA((3, planes)),
    }
    if encoder:
        scratch["total"] = pltpu.VMEM((rows, wide), F32)
    else:
        scratch["total"] = pltpu.VMEM((rows, wide), F32)
    if last:
        scratch.update((key, pltpu.VMEM(shape, F32)) for key, shape in sum_shapes.items())
    else:
        outs.update((key, ("near", shape, F32)) for key, shape in sum_shapes.items())
    feed_shape, attn_shape = (wide // 8, hidden_width), (wide // 8, 4 * width)
    flushed = () if last else ("attn",) if fast else ("attn", "up", "down")
    for key in flushed:
        outs[key + "_part"] = ("raw", loads[key].shape, BF16)
    shapes, names, resident = (), (), ()
    if fast:
        shapes, names, resident = (feed_shape, feed_shape), ("down", "up"), (0, 1)
    if last:
        shapes = (carry.shape[4:], (tall, narrow), feed_shape, feed_shape, attn_shape)
        names, resident = ("carry", "bridge_grad", "down", "up", "attn"), (1, 2, 3, 4)
        ins["carry"] = ("raw", carry)
        ins.update(("dec_" + key, ("near", dec_sums[key])) for key in SUM_NAMES)
        scratch["bridge_grad"] = pltpu.VMEM((planes, 2, 2, 2, tall, narrow), BF16)
        scratch["early"] = VectorSum.scratch(EARLY_ROWS, wide, planes)
        scratch["late"] = VectorSum.scratch(8, wide, planes)
        outs["early"] = ("near", (EARLY_ROWS, wide), F32)
        outs["late"] = ("near", (8, wide), F32)
    elif encoder:
        outs["bridge_grad"] = ("near", (wide, narrow), F32)
    if fast:
        scratch["reducer"] = Reducer.scratch(shapes, planes, resident)
        outs.update((key + "_sum", ("near", shape, F32)) for key, shape in zip(names, shapes))

    def body(ins, outs, buffers):
        length = ins["lengths"][lax.axis_index("mp")]
        sums = {key: (buffers if last else outs)[key] for key in sum_shapes}
        turned, total, middle_grad = buffers["turned"], buffers["total"], buffers["middle_grad"]
        upstream = buffers["upstream"]
        up, down, attn = (ins[key].ref for key in ("up", "down", "attn"))
        schedules = [[[] for _ in range(planes)] for _ in range(2)]
        if fast:
            reducer = Reducer(shapes, planes, buffers["reducer"])
            entry_barrier((reducer.mp, reducer.across_core, reducer.across_x, reducer.across_y))
            where = {"up": up, "down": down, "attn": attn}
            if last:
                where.update(carry=ins["carry"], bridge_grad=buffers["bridge_grad"])
            reducer.parts = [where[key] for key in names]
            at = {key: m for m, key in enumerate(names)}

            def todo(schedule, step, keys, ps):
                schedule += [partial(step, at[key], p) for p in ps for key in keys]

            feed, both = schedules[0], ("down", "up")
            core, plane, corner = reducer.core, reducer.plane, reducer.corner
            if last:
                for p in range(planes):
                    reducer.begin(at["carry"], p)
                others = ("carry", "bridge_grad")
                todo(feed[0], core, others, range(4))
                todo(feed[1], plane, others, range(4))
                todo(feed[1], core, both, (0,))
                todo(feed[2], corner, others, range(4))
                todo(feed[2], core, both, (1,))
                todo(feed[2], plane, both, (0,))
                todo(feed[3], core, both, (2,))
                todo(feed[3], plane, both, (1,))
                rest = schedules[1]
                todo(rest[0], plane, both, (2,))
                todo(rest[0], corner, both, (0,))
                todo(rest[1], plane, both, (3,))
                todo(rest[1], corner, both, (1,))
                todo(rest[1], core, ("attn",), (0,))
                todo(rest[2], corner, both, (2,))
                todo(rest[2], core, ("attn",), (1,))
                todo(rest[2], plane, ("attn",), (0,))
                todo(rest[3], corner, both, (3,))
                todo(rest[3], core, ("attn",), (2,))
                todo(rest[3], plane, ("attn",), (1,))
            else:
                todo(feed[1], core, both, (0,))
                todo(feed[2], core, both, (1,))
                todo(feed[2], plane, both, (0,))
                todo(feed[3], core, both, (2,))
                todo(feed[3], plane, both, (1,))
                todo(feed[3], corner, both, (0,))
                rest = schedules[1]
                todo(rest[0], plane, both, (2, 3))
                todo(rest[0], corner, both, (1,))
                todo(rest[1], corner, both, (2, 3))

        def flush(key, p):
            part = ins[key].ref.at[p]
            target = outs[key + "_part"].at[p]
            sem = buffers["flush_sem"].at[("attn", "up", "down").index(key), p]
            return pltpu.make_async_copy(part, target, sem)

        def leave(keys):
            def act(p):
                for key in keys:
                    if key in names:
                        reducer.begin(at[key], p)
                    if key in flushed:
                        flush(key, p).start()

            return act

        if encoder:
            put_transposed(ins["input"].use()[...], turned)
            both_grads = dot(turned[...], ins["rows"].use()[...])
            sums["bridge"][...] = both_grads[wide : wide + 8]
            if last:
                for g in range(8):
                    for p in range(planes):
                        low = (g * planes + p) * deep
                        part = both_grads[low : low + deep]
                        part = jnp.concatenate([part, jnp.zeros((tall - deep, narrow), F32)], 0)
                        grads = buffers["bridge_grad"]
                        grads[p, g // 4, g // 2 % 2, g % 2] = part.astype(BF16)
                for p in range(planes):
                    reducer.begin(at["bridge_grad"], p)
            else:
                outs["bridge_grad"][...] = both_grads[:wide]
            upstream[...] = dot(ins["rows"].use()[...], ins["weight"].use()[...], NT)
        else:
            upstream[rows - 32 :, :] = jnp.zeros((32, wide), BF16)
            upstream[:strip, :] = ins["cotangent"][...]

        def hook_of(schedule, keys):
            first, then = leave(keys), at_planes(schedule)

            def hook(p):
                first(p)
                then(p)

            return hook

        branches = [buffers[key] for key in ("branch", "branch_turned", "turned")]
        feed_saved = [ins[key].use() for key in ("hidden", "slope", "feed_input")]
        for key in ("down", "up"):
            ins[key].use()
        feed_backward(
            upstream,
            feed_saved,
            (up, down),
            branches,
            (sums["down_bias"], sums["up_bias"]),
            middle_grad,
            hook_of(schedules[0], ("down", "up")),
        )
        hidden, slope, feed_input = feed_saved
        spots = {
            "triple": hidden.at[:, :, : triple.shape[2]],
            "attended": slope.at[:, :, : attended.shape[2]],
            "normed": feed_input,
        }
        late = {
            key: Load(ins[key], spot, buffers["late_sem"].at[k])
            for k, (key, spot) in enumerate(spots.items())
        }
        layer_backward(
            ins["middle"].use(),
            ins["feed_gain"],
            upstream,
            middle_grad,
            sums["f_gain"],
            sums["f_shift"],
        )
        if fast:
            for key in ("down", "up"):
                reducer.core(at[key], 3)
        if last:
            early, late_sum = VectorSum(buffers["early"]), VectorSum(buffers["late"])
            feed_sums = [sums[key] for key in ("f_gain", "f_shift", "down_bias", "up_bias")]
            dec_sums = [ins["dec_" + key] for key in SUM_NAMES]
            early.levels[0] = stack_rows(early_rows(feed_sums, dec_sums, sums["bridge"]), wide)
            early.begin()
            for level in range(3):
                schedules[1][level].append(partial(early.advance, level))
        attn_saved = [late["attended"].use(), late["triple"].use(), ins["logsum"].use()]
        attn_saved.append(late["normed"].use())
        ins["attn"].use()
        attn_backward(
            head_dim,
            length,
            middle_grad,
            attn_saved,
            attn,
            branches + [buffers["triple_grad"]],
            (sums["out_bias"], sums["head"]),
            total,
            hook_of(schedules[1], ("attn",)),
        )
        if last:
            reducer.core(at["attn"], 3)
            reducer.plane(at["attn"], 2)
        layer_backward(
            ins["stream"].use(),
            ins["attn_gain"],
            middle_grad,
            total,
            sums["gain"],
            sums["shift"],
        )
        if last:
            late_sum.levels[0] = stack_rows(
                late_rows(*(sums[key] for key in ("gain", "shift", "out_bias", "head"))), wide
            )
            late_sum.begin()
        grad = outs["input_grad"]

        @row_blocks(rows)
        def _(i):
            grad.ref[block_at(i), :] = total[block_at(i), :].astype(BF16)

        grad.flush()
        if last:
            m = at["attn"]
            reducer.corner(m, 0)
            late_sum.advance(0)
            reducer.plane(m, 3)
            late_sum.advance(1)
            reducer.corner(m, 1)
            reducer.corner(m, 2)
            late_sum.advance(2)
            for key in ("carry", "bridge_grad", "down", "up"):
                reducer.finish(at[key], outs[key + "_sum"])
            reducer.corner(m, 3)
            early.finish(outs["early"])
            late_sum.finish(outs["late"])
            reducer.finish(m, outs["attn_sum"])
        elif fast:
            for key in names:
                reducer.finish(at[key], outs[key + "_sum"])
        if fast:
            reducer.drain()
        for key in flushed:
            for p in range(planes):
                flush(key, p).wait()

    name = "backward_encoder" if encoder else "backward_decoder"
    barrier = (2 if encoder else 1) if fast else None
    return named_call(name, body, ins, outs, scratch, barrier)


def pack_attention(proj, out, turned=False):
    if turned:
        return jnp.concatenate([proj[0], proj[1], proj[2], out], 0).T
    return jnp.concatenate([proj[0], proj[1], proj[2], out.T], -1)


def bias_rows(head_bias, up_bias):
    return [
        jnp.concatenate(
            [head_bias[0:1], jnp.zeros((1, head_bias.shape[1]), F32), head_bias[1:2]], -1
        ),
        up_bias.reshape(1, -1),
    ]


def run_forward(patches, lengths, enc, dec, vectors, bridge, fast):
    enc_vectors, dec_vectors = vectors
    bridge_weight, bridge_bias = bridge
    planes = lengths.shape[0]
    strip, wide = patches.shape
    narrow = bridge_weight.shape[1]
    rows = -(-strip // 32) * 32
    attns, heads, feeds = [], [], []
    for block in (enc, dec):
        _, _, proj, head_bias, out, _, _, _, up, up_bias, down, _ = block
        attns.append((proj, out))
        heads.append((head_bias, up_bias))
        feeds.append((up, down))
    small_shape = (8, feeds[0][0].shape[1])
    packed = [(proj.shape[1], 4 * proj.shape[2]) for proj, _ in attns]
    kinds = [packed[0][1], feeds[0][0].shape[1], None, packed[1][1], feeds[1][0].shape[1], None]
    mat_shapes = [packed[0], feeds[0][0].shape, feeds[0][1].shape]
    mat_shapes += [packed[1], feeds[1][0].shape, feeds[1][1].shape]
    count = len(mat_shapes)
    small_whole = wholes = None
    if not fast:
        mats = [m for attn, feed in zip(attns, feeds) for m in (pack_attention(*attn),) + feed]
        wholes = [lax.all_gather(m, "mp", axis=0) for m in mats]
        small = stack_rows([r for pair in heads for r in bias_rows(*pair)], small_shape[1])
        small_whole = lax.all_gather(small, "mp", axis=0)

    def block_outs(columns, width, hidden, head_dim):
        return [
            ("store", (rows, columns), BF16),
            ("store", (planes, rows, whole_lanes(3 * width)), BF16),
            ("store", (planes, rows, whole_lanes(width)), BF16),
            ("store", (planes, width // head_dim, rows), F32),
            ("store", (rows, columns), F32),
            ("store", (rows, columns), BF16),
            ("store", (planes, rows, hidden), BF16),
            ("store", (planes, rows, hidden), BF16),
        ]

    outs = block_outs(wide, kinds[0] // 4, kinds[1], HEAD)
    outs += block_outs(narrow, kinds[3] // 4, kinds[4], DHEAD)
    outs += [
        ("store", (rows, wide), BF16),
        ("store", (rows, wide), BF16),
        ("store", (rows, narrow), F32),
        ("near", (strip, narrow), BF16),
    ]
    ins = [("near", lengths), ("near", patches)]
    ins += [("near", v) for v in enc_vectors + dec_vectors + (bridge_bias,)]
    ins += [("load", bridge_weight)]
    first = len(ins)
    scratch = [pltpu.VMEM((rows, wide), F32), pltpu.VMEM((rows, narrow), F32)]
    if fast:
        turned = [stands(*proj.shape[1:]) for proj, _ in attns]
        for (proj, out), turn in zip(attns, turned):
            ins += [("near", jnp.swapaxes(proj, 1, 2) if turn else proj), ("near", out)]
        ins += [("near", v) for pair in heads for v in pair]
        ins += [("raw", v) for pair in feeds for v in pair]
        outs += [("raw", (planes,) + shape, BF16) for shape in mat_shapes]
        scratch += [pltpu.VMEM((planes,) + shape, BF16) for shape in mat_shapes]
        scratch += [pltpu.VMEM((planes,) + small_shape, F32)]
        scratch += Gatherer.sems(count, planes)
    else:
        ins += [("load", w) for w in wholes] + [("near", small_whole)]

    def body(ins, outs, scratch):
        mp = lax.axis_index("mp")
        lengths, patches = ins[:2]
        enc, dec, bridge_bias = ins[2:8], ins[8:14], ins[14]
        enc_outs, dec_outs = outs[:8], outs[8:16]
        stream, bridge_input, bridged, decoded = outs[16:20]
        totals = scratch[:2]
        length = lengths[mp]
        if fast:
            weights, smalls = scratch[2 : 2 + count], scratch[2 + count]
            attn_refs, head_refs = ins[first : first + 4], ins[first + 4 : first + 8]
            up_down = ins[first + 8 : first + 12]
            sources = [weights[0].at[mp], *up_down[:2], weights[3].at[mp], *up_down[2:]]
            gatherer = Gatherer(
                planes, sources, (0, 3), weights, outs[20:], smalls, scratch[3 + count :]
            )
            gatherer.begin()
            weights[0][mp] = pack_attention(attn_refs[0][...], attn_refs[1][...], turned[0])
            weights[3][mp] = pack_attention(attn_refs[2][...], attn_refs[3][...], turned[1])
            heads = [ref[...] for ref in head_refs]
            small_rows = bias_rows(*heads[:2]) + bias_rows(*heads[2:])
            smalls[mp] = stack_rows(small_rows, small_shape[1])
            entry_barrier(
                (mp, gatherer.across_core, gatherer.across_x, gatherer.across_y)
            )
            units = [(0, i) for i in range(3)] + [(m, i) for i in range(3) for m in (1, 2)]
            units += [(3, i) for i in range(3)] + [(m, i) for i in range(3) for m in (4, 5)]
            lag, ahead = 2, 6
            stages = (
                (0, gatherer.along_z),
                (ahead, gatherer.to_plane),
                (ahead + lag, gatherer.to_corner),
                (ahead + 2 * lag, gatherer.to_core),
                (ahead + 3 * lag, gatherer.whole),
            )

            def ticks(start, stop):
                for tick in range(start, stop):
                    for late, stage in stages:
                        if 0 <= tick - late < len(units):
                            stage(*units[tick - late])

            def before_steps(own, cuts):
                def before(k):
                    for step in range(planes):

                        @pl.when(k == step)
                        def _():
                            if step == 0:
                                for m in own:
                                    gatherer.have_own(m)
                            ticks(cuts[step], cuts[step + 1])

                return before

            depth = ahead + 3 * lag
            befores = (
                before_steps((0,), (ahead, ahead, depth + 1, depth + 2, depth + 3)),
                before_steps((1, 2), (depth + 3, depth + 3, depth + 5, depth + 7, depth + 9)),
                before_steps((3,), (depth + 9, depth + 9, depth + 10, depth + 11, depth + 12)),
                before_steps((4, 5), (depth + 12, depth + 12, depth + 14, depth + 16, depth + 18)),
            )
            order = lambda k: order_of(k, mp)
            gatherer.begin_small()
            ticks(0, ahead)
        else:
            weights, smalls = [w.use() for w in ins[first : first + count]], ins[first + count]
            order = lambda k: k
            befores = (nothing,) * 4

        tail = slice(rows - 32, rows)
        stream.ref[tail, :] = jnp.zeros((32, wide), BF16)
        stream.ref[:strip, :] = patches[...]
        stream.flush()
        if fast:
            gatherer.have_small()

        def bias(row, columns):
            return lambda p: smalls[p, row : row + 1, :columns]

        def block(source, vectors, weights, row, outs, head_dim, total, befores):
            gain, shift, out_bias, feed_gain, feed_shift, down_bias = vectors
            attn, up, down = weights
            refs = [out.ref for out in outs]
            attn_forward(
                head_dim,
                length,
                source,
                attn,
                (gain, shift, out_bias),
                bias(row, attn.shape[2] // 4 * 3),
                refs[:5],
                order,
                befores[0],
            )
            for out in outs[:5]:
                out.flush()
            feed_forward(
                refs[4],
                up,
                down,
                (feed_gain, feed_shift, down_bias),
                bias(row + 1, refs[6].shape[2]),
                refs[5:8],
                total,
                order,
                befores[1],
            )
            for out in outs[5:8]:
                out.flush()

        block(stream.ref, enc, weights[:3], 0, enc_outs, HEAD, totals[0], befores[:2])
        bridge_input.ref[...] = totals[0][...].astype(BF16)
        bridge_input.flush()
        bridged.ref[...] = dot(bridge_input.ref[...], ins[first - 1].use()[...]) + as_row(bridge_bias)
        bridged.flush()
        block(bridged.ref, dec, weights[3:], 2, dec_outs, DHEAD, totals[1], befores[2:])
        decoded[...] = totals[1][:strip, :].astype(BF16)
        if fast:
            gatherer.drain()

    results = staged_call("forward", body, ins, outs, scratch, 0 if fast else None)

    def stored(outs, source):
        normed, triple, attended, logsum, middle, feed_input, hidden, slope = outs
        return (
            (hidden, slope, feed_input, middle),
            (attended, triple, logsum, normed, source),
        )

    stream, bridge_input, bridged, decoded, *gathered = results[16:]
    return (
        stored(results[:8], stream),
        stored(results[8:16], bridged),
        bridge_input,
        decoded,
        gathered if fast else wholes,
    )


def stands(tall, flat):
    return tall % 128 == 0 and flat % 128 != 0


def run_outputs(rows, early, late, enc_sums, dec_sums, bridge_sum, sizes, bridge_shape):
    planes, groups = sizes["mp"], sizes["dp"]
    decoded, patches_grad = rows
    strip = decoded.shape[0]
    wide, narrow = bridge_shape
    deep = wide // groups // planes

    def block_shapes(columns, mats):
        width, hidden = mats[0].shape[1] // 4, mats[1].shape[1]
        each, piece = columns // groups // planes, columns // groups
        return [
            (each,),
            (each,),
            (3, piece, width),
            (2, width // groups),
            (piece, width) if stands(width, piece) else (width, piece),
            (each,),
            (each,),
            (each,),
            (piece, hidden),
            (hidden // groups,),
            (piece, hidden) if stands(hidden, piece) else (hidden, piece),
            (each,),
        ]

    shapes = block_shapes(wide, enc_sums) + [(deep, narrow), (narrow // groups // planes,)]
    shapes += block_shapes(narrow, dec_sums)
    ins = [decoded, patches_grad, early, late, *enc_sums, *dec_sums, bridge_sum]

    def kernel(*refs):
        decoded, patches_grad, early, late = refs[:4]
        enc, dec, bridge_sum = refs[4:7], refs[7:10], refs[10]
        decoded_out, patches_out, *outs = refs[11:]
        decoded_out[...] = decoded[...]
        patches_out[...] = patches_grad[:strip, :]
        dp, mp = lax.axis_index("dp"), lax.axis_index("mp")
        lanes = early.shape[1]

        def cut(values, low, size):
            values = pltpu.roll(values, lax.rem(lanes - low, lanes), 1)
            return values[:, :size]

        def put_rows(values, targets):
            for k, target in enumerate(targets):
                target[...] = values[k]

        def block(mats, outs, columns, first, row, second, up_row, head_row):
            attn, up, down = mats
            width, hidden = attn.shape[1] // 4, up.shape[1]
            gain, shift, proj, head, out, out_bias, f_gain, f_shift, up_out, up_bias, down_out, d_bias = outs
            for j in range(3):
                proj[j] = attn[:, j * width : (j + 1) * width]
            out_grad = attn[:, 3 * width :]
            out[...] = out_grad if out.shape == out_grad.shape else out_grad.T
            up_out[...] = up[...]
            down_out[...] = down[...] if down_out.shape == down.shape else down[...].T
            each = columns // groups // planes
            low = (dp * planes + mp) * each
            put_rows(cut(first[row : row + 8, :], low, each), (gain, shift, out_bias))
            lane, ref = second
            put_rows(cut(ref[lane : lane + 8, :], low, each), (f_gain, f_shift, d_bias))
            line = up_row[0][pl.ds(up_row[1] + mp, 1), :]
            put_rows(cut(line, dp * (hidden // groups), hidden // groups), (up_bias,))
            line = head_row[0][pl.ds(head_row[1] + mp, 1), :]
            piece = width // groups
            head[0:1, :] = cut(line, dp * piece, piece)
            head[1:2, :] = cut(line, 2 * width + dp * piece, piece)

        at = EARLY_DEC
        block(enc, outs[:12], wide, late, 0, (0, early), (early, 3), (late, 3))
        block(dec, outs[14:], narrow, early, at, (at + 8, early), (early, at + 3), (early, at + 11))
        outs[12][...] = bridge_sum[:deep, :]
        each = narrow // groups // planes
        line = cut(early[at + 15 : at + 16, :], (dp * planes + mp) * each, each)
        put_rows(line, (outs[13],))

    results = pl.pallas_call(
        kernel,
        out_shape=[
            jax.ShapeDtypeStruct(decoded.shape, BF16),
            jax.ShapeDtypeStruct((strip, wide), BF16),
        ]
        + [jax.ShapeDtypeStruct(shape, F32) for shape in shapes],
        in_specs=[IN_VMEM] * len(ins),
        out_specs=[IN_VMEM] * (2 + len(shapes)),
        compiler_params=pltpu.CompilerParams(vmem_limit_bytes=VMEM_BYTES),
        name="outputs",
    )(*ins)
    first, second = list(results[2:14]), list(results[16:28])
    for block, mats in ((first, enc_sums), (second, dec_sums)):
        for at, (tall, flat) in ((4, (mats[0].shape[1] // 4, mats[0].shape[0])), (10, mats[2].shape[::-1])):
            block[at] = block[at] if block[at].shape == (tall, flat) else block[at].T
    return (*results[:2], *first, *results[14:16], *second)


def shards(sizes, *inputs):
    patches, lengths = inputs[:2]
    cotangent = inputs[28]
    planes, groups = sizes["mp"], sizes["dp"]
    fast = groups == 8 and planes == 4
    strip, wide = patches.shape
    enc, (bridge_weight, bridge_bias), dec = inputs[2:14], inputs[14:16], inputs[16:28]

    def vectors_of(block):
        gain, shift, _, _, _, out_bias, f_gain, f_shift, _, _, _, d_bias = block
        return (gain, shift, out_bias, f_gain, f_shift, d_bias)

    enc_vectors, dec_vectors = vectors_of(enc), vectors_of(dec)
    enc_stored, dec_stored, bridge_input, decoded, wholes = run_forward(
        patches, lengths, enc, dec, (enc_vectors, dec_vectors), (bridge_weight, bridge_bias), fast
    )
    dec_gains, enc_gains = (dec[0], dec[6]), (enc[0], enc[6])
    down = run_backward(
        fast, (cotangent,), dec_stored, wholes[3:], dec_gains, lengths, DHEAD
    )
    dec_sums = {key: down[key] for key in SUM_NAMES}
    bridge = (down["input_grad"], bridge_input, bridge_weight)
    on = run_backward(
        fast,
        bridge,
        enc_stored,
        wholes[:3],
        enc_gains,
        lengths,
        HEAD,
        down["attn_part"] if fast else None,
        dec_sums,
    )
    if fast:
        enc_grads = (on["attn_sum"], on["up_sum"], on["down_sum"])
        dec_grads = (on["carry_sum"], down["up_sum"], down["down_sum"])
        early, late, bridge_sum = on["early"], on["late"], on["bridge_grad_sum"]
    else:
        feed_sums = [on[key] for key in ("f_gain", "f_shift", "down_bias", "up_bias")]
        rows = early_rows(feed_sums, [dec_sums[key] for key in SUM_NAMES], on["bridge"])
        early = stack_rows(rows, wide)
        late = stack_rows(late_rows(*(on[key] for key in SUM_NAMES[:4])), wide)
        early, late = lax.psum(early, ("dp", "mp")), lax.psum(late, ("dp", "mp"))

        def in_groups(grad):
            return collect(grad.reshape(planes, groups, -1, grad.shape[-1]), sizes)

        keys = ("attn_part", "up_part", "down_part")
        dec_grads = tuple(in_groups(down[key]) for key in keys)
        enc_grads = tuple(in_groups(on[key]) for key in keys)
        deep = wide // planes // groups
        bridge_part = on["bridge_grad"].reshape(groups, planes, deep, -1).transpose(1, 0, 2, 3)
        bridge_sum = collect(bridge_part, sizes)
    patches_grad = on["input_grad"]
    return run_outputs(
        (decoded, patches_grad),
        early,
        late,
        enc_grads,
        dec_grads,
        bridge_sum,
        sizes,
        bridge_weight.shape,
    )


def solution(mesh):
    block_in = (
        P(),
        P(),
        P(None, None, "mp"),
        P(None, "mp"),
        P("mp", None),
        P(),
        P(),
        P(),
        P(None, "mp"),
        P("mp"),
        P("mp", None),
        P(),
    )
    both = P(("dp", "mp"))
    block_out = (
        both,
        both,
        P(None, "dp", "mp"),
        P(None, ("mp", "dp")),
        P("mp", "dp"),
        both,
        both,
        both,
        P("dp", "mp"),
        P(("mp", "dp")),
        P("mp", "dp"),
        both,
    )
    rows = P(("dp", "mp"), None)
    return jax.shard_map(
        partial(shards, dict(mesh.shape)),
        mesh=mesh,
        in_specs=(rows, P("dp")) + block_in + (P(), P()) + block_in + (rows,),
        out_specs=(rows, rows) + block_out + (rows, both) + block_out,
        check_vma=False,
    )
```

time: 410 us -> 291 us (0.71)
  Pallas kernels: 365 us -> 289 us
  local copies, waits for them, and re-layouts: 34.6 us -> 0 us
  other arithmetic: 4.14 us -> 0 us
    pallas_call x5 -> x1, Pallas kernels: 163 us -> 3.6 us  [run_outputs(): pl.pallas_call(kernel, out_shape=[jax.ShapeDtypeStruct(decoded.shape, BF1...]
    pallas_call x4 -> x3, Pallas kernels: 203 us -> 285 us  [staged_call(): pl.pallas_call(kernel, out_shape=[jax.ShapeDtypeStruct(shape, dtype) for...]
    unnamed x55 -> x0, local copies, waits for them, and re-layouts: 7.63 us -> none
    slice x15 -> x0, local copies, waits for them, and re-layouts: 7.56 us -> none  [the longest x1 2.15 us: shards(): patches_grad[:rows]]
    dynamic_slice x15 -> x0, local copies, waits for them, and re-layouts: 7.45 us -> none  [the longest x10 5.83 us: shared(): return lax.dynamic_slice_in_dim(row, (dp * planes + mp) * size, size)]
    broadcast_in_dim x13 -> x0, local copies, waits for them, and re-layouts: 5.92 us -> none  [the longest x3 1.22 us: block_forward(): up_bias[:, None]]
where the time goes in v3:
time: 291 us; the launch traced here: 289 us
  Pallas kernels  289 us (99%)
    pallas_call x3, Pallas kernels, staged_call(): pl.pallas_call(kernel, out_shape=[jax.ShapeDtypeStruct(shape, dtype) for...  285 us

profile of v3, /device:TPU:28, one launch (start us, length us, event | category | flops | bytes accessed | tf_op | source)
XLA Modules:
  0.0 289.5 jit_solution(13866732123478539079)
XLA Ops:
  0.7 115.6 %forward.1 = (bf16[544,768]{1,0:T(8,128)(2,1)}, bf16[4,544,640]{2,1,0:T(8,128)(2,1)}, bf16[4,544,256]{2,1,0:T(8,128)(2,1)}, f32[4,3,544]{2,1,0:T(4,128)}, f32[54...) custom-call(s32[4]{0:T(128)} %refs_0_.5, ...), custom_call_target="tpu_custom_call" | custom-call | tf_op jit(solution)/shard_map/forward/pallas_call | solution.py:686
  116.3 51.8 %backward_decoder.1 = (bf16[544,512]{1,0:T(8,128)(2,1)}, f32[8,512]{1,0:T(8,128)}, f32[8,512]{1,0:T(8,128)}, f32[8,512]{1,0:T(8,128)}, f32[4,8,384]{2,1,0:T(8,12...) custom-call(s32[4]{0:T(128)} %refs_0_.5, ...), custom_call_target="tpu_custom_call" | custom-call | tf_op jit(solution)/shard_map/backward_decoder/pallas_call | solution.py:686
  168.1 117.6 %backward_encoder.1 = (bf16[544,768]{1,0:T(8,128)(2,1)}, f32[24,768]{1,0:T(8,128)}, f32[8,768]{1,0:T(8,128)}, f32[64,512]{1,0:T(8,128)}, f32[32,512]{1,0:T(8,128...) custom-call(s32[4]{0:T(128)} %refs_0_.5, bf16[544,512]{1,0:T(8,128)(2,1)} %get-tuple-element.115.refs_1_, ...), custom_call_target="tpu_custom_call" | custom-call | tf_op jit(solution)/shard_map/backward_encoder/pallas_call | solution.py:686
  285.7 3.6 %outputs.1 = (bf16[529,512]{1,0:T(8,128)(2,1)}, bf16[529,768]{1,0:T(8,128)(2,1)}, f32[24]{0:T(128)}, f32[24]{0:T(128)}, f32[3,96,192]{2,1,0:T(8,128)}, /*index=5...) custom-call(bf16[529,512]{1,0:T(8,128)(2,1)} %get-tuple-element.102., ...), custom_call_target="tpu_custom_call" | custom-call | tf_op jit(solution)/shard_map/outputs/pallas_call | solution.py:1427
